TPU v7x, 512 devices: a whole 4x8x8 slice. The times are simulated.
512 devices in a mesh: ctx: 64 (over x, y, z_lo), head: 8 (over z_hi, core).
Axes of the slice: x: 4, y: 8, z: 8 (z_hi: 4, z_lo: 2; z = z_hi * 2 + z_lo), core: 2. Of those that a mesh axis runs over, the one named last changes fastest.
Arguments:
- query_in: bfloat16 [16384, 64, 128], P(('ctx', 'head')), may hold values from -8 to 8
- key_in: bfloat16 [16384, 8, 128], P(('ctx', 'head')), may hold values from -8 to 8
- value_in: bfloat16 [16384, 8, 128], P(('ctx', 'head')), may hold values from -6 to 6
- grad_out: bfloat16 [16384, 64, 128], P(('ctx', 'head')), may hold values from -6 to 6
- doc_lengths: int32 [32], replicated, may hold values from 1 to 1024, 16384 in all
Outputs:
- attn_out: bfloat16 [16384, 64, 128], P(('ctx', 'head'))
- grad_query: bfloat16 [16384, 64, 128], P(('ctx', 'head'))
- grad_key: bfloat16 [16384, 8, 128], P(('ctx', 'head'))
- grad_value: bfloat16 [16384, 8, 128], P(('ctx', 'head'))
Inputs may be any that keep to these rules, and one draw needn't show every extreme that they name: `doc_lengths`: 32 documents whose lengths sum to 16384; the longest has exactly 1024 tokens.
All inputs are finite; a program needn't handle non-finite values.
Results may differ from a plain program's by a relative error of at most 0.022.
Values may be sent and summed in bfloat16 or wider, within the bound.
No kernel may reach another device: no remote copies, remote signals or barrier semaphores. Data moves between devices by JAX's collectives and lax.ppermute only.
A program may use at most 64 MiB of HBM per device.

v0:
```python
import jax
import jax.numpy as jnp
from jax import lax
from jax.sharding import PartitionSpec as P

REACH = 4


def passed_along(array, axis, by):
    count = lax.axis_size(axis)
    pairs = [(i, i + by) for i in range(count) if 0 <= i + by < count]
    return lax.ppermute(array, axis, pairs)


def segment_of(doc_ends, places):
    return jnp.sum((doc_ends[None, :] <= places[:, None]).astype(jnp.int32), axis=1)


def shards(query_in, key_in, value_in, grad_out, doc_lengths):
    query_h, key_h, value_h, grad_h = (
        lax.all_to_all(query_in, "head", split_axis=1, concat_axis=0, tiled=True),
        lax.all_to_all(key_in, "head", split_axis=1, concat_axis=0, tiled=True),
        lax.all_to_all(value_in, "head", split_axis=1, concat_axis=0, tiled=True),
        lax.all_to_all(grad_out, "head", split_axis=1, concat_axis=0, tiled=True),
    )
    tok_rows = query_h.shape[0]
    kv_local = key_h.shape[1]
    q_local = query_h.shape[1]
    group_size = q_local // kv_local
    head_width = query_h.shape[2]
    score_scale = head_width ** (-0.5)
    query_r = query_h.reshape(tok_rows, kv_local, group_size, head_width)
    grad_r = grad_h.reshape(tok_rows, kv_local, group_size, head_width)
    shard_index = lax.axis_index("ctx")
    doc_ends = jnp.cumsum(doc_lengths)
    offsets = jnp.arange(tok_rows, dtype=jnp.int32)
    q_place = shard_index * tok_rows + offsets
    q_segment = segment_of(doc_ends, q_place)
    key_pair = jnp.stack([key_h, value_h])
    tiles = [key_pair]
    current = key_pair
    for distance in range(1, REACH + 1):
        current = passed_along(current, "ctx", 1)
        tiles.append(current)
    masks = []
    alive = []
    for distance in range(REACH + 1):
        k_place = (shard_index - distance) * tok_rows + offsets
        k_segment = segment_of(doc_ends, k_place)
        visible = (
            (q_segment[:, None] == k_segment[None, :])
            & (k_place[None, :] <= q_place[:, None])
            & (k_place[None, :] >= 0)
        )
        masks.append(visible)
        alive.append(jnp.any(visible))

    def scores_of(tile, visible):
        scores = (
            jnp.einsum("tkgd,skd->kgts", query_r, tile[0], preferred_element_type=jnp.float32)
            * score_scale
        )
        return jnp.where(visible[None, None], scores, -1e30)

    def gather_stats(carried, tile, visible):
        row_top, row_total = carried
        masked = scores_of(tile, visible)
        new_top = jnp.maximum(row_top, jnp.max(masked, axis=-1))
        row_total = row_total * jnp.exp(row_top - new_top) + jnp.sum(
            jnp.exp(masked - new_top[..., None]), axis=-1
        )
        return (new_top, row_total)

    stats = (
        jnp.full((kv_local, group_size, tok_rows), -1e30, jnp.float32),
        jnp.zeros((kv_local, group_size, tok_rows), jnp.float32),
    )
    for distance in range(REACH + 1):
        stats = lax.cond(
            alive[distance],
            gather_stats,
            lambda carried, tile, visible: carried,
            stats,
            tiles[distance],
            masks[distance],
        )
    log_total = stats[0] + jnp.log(stats[1])

    def weights_of(tile, visible):
        return jnp.exp(scores_of(tile, visible) - log_total[..., None])

    def add_output(out_acc, tile, visible):
        weights_b = weights_of(tile, visible).astype(jnp.bfloat16)
        return out_acc + jnp.einsum(
            "kgts,skd->tkgd", weights_b, tile[1], preferred_element_type=jnp.float32
        )

    out_acc = jnp.zeros((tok_rows, kv_local, group_size, head_width), jnp.float32)
    for distance in range(REACH + 1):
        out_acc = lax.cond(
            alive[distance],
            add_output,
            lambda carried, tile, visible: carried,
            out_acc,
            tiles[distance],
            masks[distance],
        )
    out_round = out_acc.astype(jnp.bfloat16)
    drift = jnp.sum(grad_r.astype(jnp.float32) * out_round.astype(jnp.float32), axis=-1)
    drift_t = jnp.transpose(drift, (1, 2, 0))

    def backward(grad_q_acc, tile, visible):
        weights = weights_of(tile, visible)
        weights_b = weights.astype(jnp.bfloat16)
        dprob = jnp.einsum("tkgd,skd->kgts", grad_r, tile[1], preferred_element_type=jnp.float32)
        dscore = (weights * (dprob - drift_t[..., None])).astype(jnp.bfloat16)
        grad_q_acc = grad_q_acc + score_scale * jnp.einsum(
            "kgts,skd->tkgd", dscore, tile[0], preferred_element_type=jnp.float32
        )
        grad_k = score_scale * jnp.einsum(
            "kgts,tkgd->skd", dscore, query_r, preferred_element_type=jnp.float32
        )
        grad_v = jnp.einsum("kgts,tkgd->skd", weights_b, grad_r, preferred_element_type=jnp.float32)
        return (grad_q_acc, jnp.stack([grad_k, grad_v]))

    def skipped(grad_q_acc, tile, visible):
        return (grad_q_acc, jnp.zeros((2, tok_rows, kv_local, head_width), jnp.float32))

    grad_q_acc = jnp.zeros((tok_rows, kv_local, group_size, head_width), jnp.float32)
    grad_terms = []
    for distance in range(REACH + 1):
        grad_q_acc, term = lax.cond(
            alive[distance], backward, skipped, grad_q_acc, tiles[distance], masks[distance]
        )
        grad_terms.append(term)
    returned = jnp.zeros_like(grad_terms[0])
    for distance in range(1, REACH + 1):
        returned = returned + passed_along(
            grad_terms[distance].astype(jnp.bfloat16), "ctx", -distance
        ).astype(jnp.float32)
    grad_pair = (grad_terms[0] + returned).astype(jnp.bfloat16)
    out_heads = out_round.reshape(tok_rows, q_local, head_width)
    grad_q_heads = grad_q_acc.astype(jnp.bfloat16).reshape(tok_rows, q_local, head_width)
    attn_out, grad_query, grad_key, grad_value = (
        lax.all_to_all(out_heads, "head", split_axis=0, concat_axis=1, tiled=True),
        lax.all_to_all(grad_q_heads, "head", split_axis=0, concat_axis=1, tiled=True),
        lax.all_to_all(grad_pair[0], "head", split_axis=0, concat_axis=1, tiled=True),
        lax.all_to_all(grad_pair[1], "head", split_axis=0, concat_axis=1, tiled=True),
    )
    return (attn_out, grad_query, grad_key, grad_value)


def solution(mesh):
    return jax.shard_map(
        shards,
        mesh=mesh,
        in_specs=(
            P(("ctx", "head"), None, None),
            P(("ctx", "head"), None, None),
            P(("ctx", "head"), None, None),
            P(("ctx", "head"), None, None),
            P(),
        ),
        out_specs=(
            P(("ctx", "head"), None, None),
            P(("ctx", "head"), None, None),
            P(("ctx", "head"), None, None),
            P(("ctx", "head"), None, None),
        ),
        check_vma=False,
    )
```

profile of v0, /device:TPU:6, one launch (start us, length us, event | category | flops | bytes accessed | tf_op | source)
XLA Modules:
  0.0 218.8 jit_solution(18194798174847828288)
XLA Ops:
  0.6 1.5 copy.154
  2.2 10.3 %all-to-all-start = ((bf16[32,8,128]{2,0,1:T(8,128)(2,1)}), bf16[32,8,128]{2,0,1:T(8,128)(2,1)S(1)}, u32[]{:S(2)}, u32[]{:S(2)}) async-start(bf16[32,8,128]{2,0,1:T(8,128)(2,1)} %copy.154), calls=%async_computation | async-start | bytes 131072 | tf_op jit(solution)/shard_map/all_to_all | solution.py:22
  14.0 7.1 %all-to-all-done = bf16[32,8,128]{2,0,1:T(8,128)(2,1)S(1)} async-done(((bf16[32,8,128]{2,0,1:T(8,128)(2,1)}), bf16[32,8,128]{2,0,1:T(8,128)(2,1)S(1)}, u32[]{:S(2)}, u32[]{:S(2)}) %all-to-all-start) | async-done | bytes 65568 | tf_op jit(solution)/shard_map/all_to_all | solution.py:22
  21.1 3.4 %all-to-all-start.2 = ((bf16[32,8,128]{2,0,1:T(8,128)(2,1)}), bf16[32,8,128]{2,0,1:T(8,128)(2,1)S(1)}, u32[]{:S(2)}, u32[]{:S(2)}) async-start(bf16[32,8,128]{2,0,1:T(8,128)(2,1)} %copy.157), calls=%async_computation.2 | async-start | bytes 131072 | tf_op jit(solution)/shard_map/all_to_all | solution.py:23
  24.4 2.2 copy.155
  26.6 6.1 %all-to-all-done.2 = bf16[32,8,128]{2,0,1:T(8,128)(2,1)S(1)} async-done(((bf16[32,8,128]{2,0,1:T(8,128)(2,1)}), bf16[32,8,128]{2,0,1:T(8,128)(2,1)S(1)}, u32[]{:S(2)}, u32[]{:S(2)}) %all-to-all-start.2) | async-done | bytes 65568 | tf_op jit(solution)/shard_map/all_to_all | solution.py:23
  32.7 3.5 %all-to-all-start.1 = ((bf16[32,64,128]{2,0,1:T(8,128)(2,1)}), bf16[32,64,128]{2,0,1:T(8,128)(2,1)S(1)}, u32[]{:S(2)}, u32[]{:S(2)}) async-start(bf16[32,64,128]{2,0,1:T(8,128)(2,1)} %copy.155), calls=%async_computation.1 | async-start | bytes 1048576 | tf_op jit(solution)/shard_map/all_to_all | solution.py:21
  37.3 17.0 %all-to-all-done.1 = bf16[32,64,128]{2,0,1:T(8,128)(2,1)S(1)} async-done(((bf16[32,64,128]{2,0,1:T(8,128)(2,1)}), bf16[32,64,128]{2,0,1:T(8,128)(2,1)S(1)}, u32[]{:S(2)}, u32[]{:S(2)}) %all-to-all-start.1) | async-done | bytes 524320 | tf_op jit(solution)/shard_map/all_to_all | solution.py:21
  54.3 3.5 %all-to-all-start.4 = ((bf16[32,64,128]{2,0,1:T(8,128)(2,1)}), bf16[32,64,128]{2,0,1:T(8,128)(2,1)S(1)}, u32[]{:S(2)}, u32[]{:S(2)}) async-start(bf16[32,64,128]{2,0,1:T(8,128)(2,1)} %copy.160), calls=%async_computation.4 | async-start | bytes 1048576 | tf_op jit(solution)/shard_map/all_to_all | solution.py:24
  57.8 2.8 %collective-permute-start = (bf16[2,256,1,128]{3,1,2,0:T(8,128)(2,1)S(1)}, bf16[2,256,1,128]{3,1,2,0:T(8,128)(2,1)S(1)}, u32[]{:S(2)}, u32[]{:S(2)}) collective-permute-start(bf16[2,256,1,128]{3,1,2,0:T(8,128)(2,1)S(1)} %pad_maximum_fusion.5), channel_id=1, source_target_pairs={{0,8},{8,16},{16,24},{24,32},{32,40},{40,48},{48,56},{56,64},{64,7... | collective-permute-start | bytes 393224 | tf_op jit(solution)/shard_map/ppermute | solution.py:12
  60.6 11.6 %collective-permute-done = bf16[2,256,1,128]{3,1,2,0:T(8,128)(2,1)S(1)} collective-permute-done((bf16[2,256,1,128]{3,1,2,0:T(8,128)(2,1)S(1)}, bf16[2,256,1,128]{3,1,2,0:T(8,128)(2,1)S(1)}, u32[]{:S(2)}, u32[]{:S(2)}) %collective-permute-start) | collective-permute-done | bytes 131104 | tf_op jit(solution)/shard_map/ppermute | solution.py:12
  72.2 4.3 %collective-permute-start.1 = (bf16[2,256,1,128]{3,1,2,0:T(8,128)(2,1)S(1)}, bf16[2,256,1,128]{3,1,2,0:T(8,128)(2,1)S(1)}, u32[]{:S(2)}, u32[]{:S(2)}) collective-permute-start(bf16[2,256,1,128]{3,1,2,0:T(8,128)(2,1)S(1)} %collective-permute-done), channel_id=1, source_target_pairs={{0,8},{8,16},{16,24},{24,32},{32,40},{40,48},{48,56},{56,64},{64,7... | collective-permute-start | bytes 393224 | tf_op jit(solution)/shard_map/ppermute | solution.py:12
  76.6 6.7 %collective-permute-done.1 = bf16[2,256,1,128]{3,1,2,0:T(8,128)(2,1)S(1)} collective-permute-done((bf16[2,256,1,128]{3,1,2,0:T(8,128)(2,1)S(1)}, bf16[2,256,1,128]{3,1,2,0:T(8,128)(2,1)S(1)}, u32[]{:S(2)}, u32[]{:S(2)}) %collective-permute-start.1) | collective-permute-done | bytes 131104 | tf_op jit(solution)/shard_map/ppermute | solution.py:12
  83.3 1.9 collective-permute-start.2
  85.6 7.5 %collective-permute-done.2 = bf16[2,256,1,128]{3,1,2,0:T(8,128)(2,1)S(1)} collective-permute-done((bf16[2,256,1,128]{3,1,2,0:T(8,128)(2,1)S(1)}, bf16[2,256,1,128]{3,1,2,0:T(8,128)(2,1)S(1)}, u32[]{:S(2)}, u32[]{:S(2)}) %collective-permute-start.2) | collective-permute-done | bytes 131104 | tf_op jit(solution)/shard_map/ppermute | solution.py:12
  93.1 1.9 collective-permute-start.3
  106.1 3.4 %conditional.25 = (f32[256,1,8,128]{3,0,2,1:T(8,128)S(1)}, f32[2,256,1,128]{3,1,2,0:T(8,128)S(1)}) conditional(s32[]{:T(128)} %convert_element_type.142, () %tuple.132, (pred[256,256]{0,1:T(8,128)(4,1)S(1)}, bf16[256,1,128]{2,0,1:T(8,128)(2,1)S(1)}, bf16[256,1,8,128]{3,0,2,1:T(8,128)(2,1)S(1)}, f32[1,8,256]{2,1,0:T(8,128)S(1)}, ...), branch_computations={%region_42.43_spmd, %region_43.44_spmd} | conditional | flops 675119104 | bytes 13926444 | solution.py:132
  109.5 3.6 %conditional.26 = (f32[256,1,8,128]{3,0,2,1:T(8,128)S(1)}, bf16[2,256,1,128]{3,1,2,0:T(8,128)(2,1)S(1)}) conditional(s32[]{:T(128)} %convert_element_type.141, f32[256,1,8,128]{3,0,2,1:T(8,128)S(1)} %get-tuple-element.332, (pred[256,256]{0,1:T(8,128)(4,1)}, bf16[2,256,1,128]{3,1,2,0:T(8,128)(2,1)}, bf16[256,1,8,128]{3,0,2,1:T(8,128)(2,1)S(1)}, ...), branch_computations={%region_44.45_spmd, %region_45.46_spmd} | conditional | flops 675414016 | bytes 14843948 | solution.py:132
  109.6 1.5 fusion.134
  115.5 17.7 %collective-permute-start.7 = (bf16[2,256,1,128]{3,1,2,0:T(8,128)(2,1)S(1)}, bf16[2,256,1,128]{3,1,2,0:T(8,128)(2,1)S(1)}, u32[]{:S(2)}, u32[]{:S(2)}) collective-permute-start(bf16[2,256,1,128]{3,1,2,0:T(8,128)(2,1)S(1)} %get-tuple-element.341), channel_id=1, source_target_pairs={{32,0},{40,8},{48,16},{56,24},{64,32},{72,40},{80,48},{88,56},{96,... | collective-permute-start | bytes 393224 | tf_op jit(solution)/shard_map/ppermute | solution.py:12
  133.2 1.9 collective-permute-start.6
  135.1 1.9 collective-permute-start.5
  137.0 7.1 %collective-permute-start.4 = (bf16[2,256,1,128]{3,1,2,0:T(8,128)(2,1)}, bf16[2,256,1,128]{3,1,2,0:T(8,128)(2,1)S(1)}, u32[]{:S(2)}, u32[]{:S(2)}) collective-permute-start(bf16[2,256,1,128]{3,1,2,0:T(8,128)(2,1)} %copy-done.14), channel_id=1, source_target_pairs={{8,0},{16,8},{24,16},{32,24},{40,32},{48,40},{56,48},{64,56},{72,6... | collective-permute-start | bytes 393224 | tf_op jit(solution)/shard_map/ppermute | solution.py:12
  144.2 2.8 %collective-permute-done.4 = bf16[2,256,1,128]{3,1,2,0:T(8,128)(2,1)S(1)} collective-permute-done((bf16[2,256,1,128]{3,1,2,0:T(8,128)(2,1)}, bf16[2,256,1,128]{3,1,2,0:T(8,128)(2,1)S(1)}, u32[]{:S(2)}, u32[]{:S(2)}) %collective-permute-start.4) | collective-permute-done | bytes 131104 | tf_op jit(solution)/shard_map/ppermute | solution.py:12
  148.9 7.2 %all-to-all-start.7 = ((bf16[8,2,2048]{2,1,0:T(2,128)(2,1)}), bf16[8,2,2048]{2,1,0:T(2,128)(2,1)S(1)}, u32[]{:S(2)}, u32[]{:S(2)}) async-start(bf16[8,2,2048]{2,1,0:T(2,128)(2,1)} %reshape.636), calls=%async_computation.7 | async-start | bytes 131072 | tf_op jit(solution)/shard_map/all_to_all | solution.py:148
  157.5 6.9 %all-to-all-done.7 = bf16[8,2,2048]{2,1,0:T(2,128)(2,1)S(1)} async-done(((bf16[8,2,2048]{2,1,0:T(2,128)(2,1)}), bf16[8,2,2048]{2,1,0:T(2,128)(2,1)S(1)}, u32[]{:S(2)}, u32[]{:S(2)}) %all-to-all-start.7) | async-done | bytes 65568 | tf_op jit(solution)/shard_map/all_to_all | solution.py:148
  164.4 3.4 %all-to-all-start.6 = ((bf16[8,2,2048]{2,1,0:T(2,128)(2,1)}), bf16[8,2,2048]{2,1,0:T(2,128)(2,1)S(1)}, u32[]{:S(2)}, u32[]{:S(2)}) async-start(bf16[8,2,2048]{2,1,0:T(2,128)(2,1)} %reshape.634), calls=%async_computation.6 | async-start | bytes 131072 | tf_op jit(solution)/shard_map/all_to_all | solution.py:147
  169.1 6.7 %all-to-all-done.6 = bf16[8,2,2048]{2,1,0:T(2,128)(2,1)S(1)} async-done(((bf16[8,2,2048]{2,1,0:T(2,128)(2,1)}), bf16[8,2,2048]{2,1,0:T(2,128)(2,1)S(1)}, u32[]{:S(2)}, u32[]{:S(2)}) %all-to-all-start.6) | async-done | bytes 65568 | tf_op jit(solution)/shard_map/all_to_all | solution.py:147
  175.9 3.5 %all-to-all-start.3 = ((bf16[256,8,128]{2,1,0:T(8,128)(2,1)}), bf16[256,8,128]{2,1,0:T(8,128)(2,1)S(1)}, u32[]{:S(2)}, u32[]{:S(2)}) async-start(bf16[256,8,128]{2,1,0:T(8,128)(2,1)} %bitcast.789), calls=%async_computation.3 | async-start | bytes 1048576 | tf_op jit(solution)/shard_map/all_to_all | solution.py:145
  180.8 15.4 %all-to-all-done.3 = bf16[256,8,128]{2,1,0:T(8,128)(2,1)S(1)} async-done(((bf16[256,8,128]{2,1,0:T(8,128)(2,1)}), bf16[256,8,128]{2,1,0:T(8,128)(2,1)S(1)}, u32[]{:S(2)}, u32[]{:S(2)}) %all-to-all-start.3) | async-done | bytes 524320 | tf_op jit(solution)/shard_map/all_to_all | solution.py:145
  196.1 3.5 %all-to-all-start.5 = ((bf16[256,8,128]{2,1,0:T(8,128)(2,1)}), bf16[256,8,128]{2,1,0:T(8,128)(2,1)S(1)}, u32[]{:S(2)}, u32[]{:S(2)}) async-start(bf16[256,8,128]{2,1,0:T(8,128)(2,1)} %bitcast.786), calls=%async_computation.5 | async-start | bytes 1048576 | tf_op jit(solution)/shard_map/all_to_all | solution.py:146
  202.1 15.8 %all-to-all-done.5 = bf16[256,8,128]{2,1,0:T(8,128)(2,1)S(1)} async-done(((bf16[256,8,128]{2,1,0:T(8,128)(2,1)}), bf16[256,8,128]{2,1,0:T(8,128)(2,1)S(1)}, u32[]{:S(2)}, u32[]{:S(2)}) %all-to-all-start.5) | async-done | bytes 524320 | tf_op jit(solution)/shard_map/all_to_all | solution.py:146
  (110 shorter events, 31.8 us)
Async XLA Ops:
  0.6 35.6 %copy-start.5 = (bf16[32,64,128]{2,1,0:T(8,128)(2,1)S(1)}, bf16[32,64,128]{2,1,0:T(8,128)(2,1)}, u32[]{:S(2)}) copy-start(bf16[32,64,128]{2,1,0:T(8,128)(2,1)} %param.38) | copy-start | bytes 1572868
  2.2 18.9 %all-to-all-start = ((bf16[32,8,128]{2,0,1:T(8,128)(2,1)}), bf16[32,8,128]{2,0,1:T(8,128)(2,1)S(1)}, u32[]{:S(2)}, u32[]{:S(2)}) async-start(bf16[32,8,128]{2,0,1:T(8,128)(2,1)} %copy.154), calls=%async_computation | async-start | bytes 131072 | tf_op jit(solution)/shard_map/all_to_all | solution.py:22
  21.1 11.6 %all-to-all-start.2 = ((bf16[32,8,128]{2,0,1:T(8,128)(2,1)}), bf16[32,8,128]{2,0,1:T(8,128)(2,1)S(1)}, u32[]{:S(2)}, u32[]{:S(2)}) async-start(bf16[32,8,128]{2,0,1:T(8,128)(2,1)} %copy.157), calls=%async_computation.2 | async-start | bytes 131072 | tf_op jit(solution)/shard_map/all_to_all | solution.py:23
  24.4 60.8 %copy-start.17 = (s32[32]{0:T(128)S(1)}, s32[32]{0:T(128)}, u32[]{:S(2)}) copy-start(s32[32]{0:T(128)} %param.39) | copy-start | bytes 388
  32.7 21.6 %all-to-all-start.1 = ((bf16[32,64,128]{2,0,1:T(8,128)(2,1)}), bf16[32,64,128]{2,0,1:T(8,128)(2,1)S(1)}, u32[]{:S(2)}, u32[]{:S(2)}) async-start(bf16[32,64,128]{2,0,1:T(8,128)(2,1)} %copy.155), calls=%async_computation.1 | async-start | bytes 1048576 | tf_op jit(solution)/shard_map/all_to_all | solution.py:21
  54.3 45.5 %all-to-all-start.4 = ((bf16[32,64,128]{2,0,1:T(8,128)(2,1)}), bf16[32,64,128]{2,0,1:T(8,128)(2,1)S(1)}, u32[]{:S(2)}, u32[]{:S(2)}) async-start(bf16[32,64,128]{2,0,1:T(8,128)(2,1)} %copy.160), calls=%async_computation.4 | async-start | bytes 1048576 | tf_op jit(solution)/shard_map/all_to_all | solution.py:24
  57.8 14.4 %collective-permute-start = (bf16[2,256,1,128]{3,1,2,0:T(8,128)(2,1)S(1)}, bf16[2,256,1,128]{3,1,2,0:T(8,128)(2,1)S(1)}, u32[]{:S(2)}, u32[]{:S(2)}) collective-permute-start(bf16[2,256,1,128]{3,1,2,0:T(8,128)(2,1)S(1)} %pad_maximum_fusion.5), channel_id=1, source_target_pairs={{0,8},{8,16},{16,24},{24,32},{32,40},{40,48},{48,56},{56,64},{64,7... | collective-permute-start | bytes 393224 | tf_op jit(solution)/shard_map/ppermute | solution.py:12
  72.2 31.8 %copy-start.12 = (bf16[2,256,1,128]{3,1,2,0:T(8,128)(2,1)}, bf16[2,256,1,128]{3,1,2,0:T(8,128)(2,1)S(1)}, u32[]{:S(2)}) copy-start(bf16[2,256,1,128]{3,1,2,0:T(8,128)(2,1)S(1)} %collective-permute-done) | copy-start | bytes 393220
  72.2 11.0 %collective-permute-start.1 = (bf16[2,256,1,128]{3,1,2,0:T(8,128)(2,1)S(1)}, bf16[2,256,1,128]{3,1,2,0:T(8,128)(2,1)S(1)}, u32[]{:S(2)}, u32[]{:S(2)}) collective-permute-start(bf16[2,256,1,128]{3,1,2,0:T(8,128)(2,1)S(1)} %collective-permute-done), channel_id=1, source_target_pairs={{0,8},{8,16},{16,24},{24,32},{32,40},{40,48},{48,56},{56,64},{64,7... | collective-permute-start | bytes 393224 | tf_op jit(solution)/shard_map/ppermute | solution.py:12
  83.3 21.9 %copy-start.10 = (bf16[2,256,1,128]{3,1,2,0:T(8,128)(2,1)}, bf16[2,256,1,128]{3,1,2,0:T(8,128)(2,1)S(1)}, u32[]{:S(2)}) copy-start(bf16[2,256,1,128]{3,1,2,0:T(8,128)(2,1)S(1)} %collective-permute-done.1) | copy-start | bytes 393220
  83.3 9.9 %collective-permute-start.2 = (bf16[2,256,1,128]{3,1,2,0:T(8,128)(2,1)S(1)}, bf16[2,256,1,128]{3,1,2,0:T(8,128)(2,1)S(1)}, u32[]{:S(2)}, u32[]{:S(2)}) collective-permute-start(bf16[2,256,1,128]{3,1,2,0:T(8,128)(2,1)S(1)} %collective-permute-done.1), channel_id=1, source_target_pairs={{0,8},{8,16},{16,24},{24,32},{32,40},{40,48},{48,56},{56,64},{64,7... | collective-permute-start | bytes 393224 | tf_op jit(solution)/shard_map/ppermute | solution.py:12
  93.1 12.1 %copy-start.8 = (bf16[2,256,1,128]{3,1,2,0:T(8,128)(2,1)}, bf16[2,256,1,128]{3,1,2,0:T(8,128)(2,1)S(1)}, u32[]{:S(2)}) copy-start(bf16[2,256,1,128]{3,1,2,0:T(8,128)(2,1)S(1)} %collective-permute-done.2) | copy-start | bytes 393220
  93.1 9.9 %collective-permute-start.3 = (bf16[2,256,1,128]{3,1,2,0:T(8,128)(2,1)S(1)}, bf16[2,256,1,128]{3,1,2,0:T(8,128)(2,1)S(1)}, u32[]{:S(2)}, u32[]{:S(2)}) collective-permute-start(bf16[2,256,1,128]{3,1,2,0:T(8,128)(2,1)S(1)} %collective-permute-done.2), channel_id=1, source_target_pairs={{0,8},{8,16},{16,24},{24,32},{32,40},{40,48},{48,56},{56,64},{64,7... | collective-permute-start | bytes 393224 | tf_op jit(solution)/shard_map/ppermute | solution.py:12
  96.5 7.5 %copy-start.4 = (pred[256,256]{0,1:T(8,128)(4,1)}, pred[256,256]{0,1:T(8,128)(4,1)S(1)}, u32[]{:S(2)}) copy-start(pred[256,256]{0,1:T(8,128)(4,1)S(1)} %get-tuple-element.537) | copy-start | bytes 196612
  96.5 8.6 %copy-start.3 = (pred[256,256]{0,1:T(8,128)(4,1)}, pred[256,256]{0,1:T(8,128)(4,1)S(1)}, u32[]{:S(2)}) copy-start(pred[256,256]{0,1:T(8,128)(4,1)S(1)} %get-tuple-element.539) | copy-start | bytes 196612
  96.5 8.7 %copy-start.2 = (pred[256,256]{0,1:T(8,128)(4,1)}, pred[256,256]{0,1:T(8,128)(4,1)S(1)}, u32[]{:S(2)}) copy-start(pred[256,256]{0,1:T(8,128)(4,1)S(1)} %get-tuple-element.541) | copy-start | bytes 196612
  96.5 8.7 %copy-start.1 = (pred[256,256]{0,1:T(8,128)(4,1)}, pred[256,256]{0,1:T(8,128)(4,1)S(1)}, u32[]{:S(2)}) copy-start(pred[256,256]{0,1:T(8,128)(4,1)S(1)} %get-tuple-element.543) | copy-start | bytes 196612
  103.0 2.2 %copy-start.6 = (bf16[2,256,1,128]{3,1,2,0:T(8,128)(2,1)}, bf16[2,256,1,128]{3,1,2,0:T(8,128)(2,1)S(1)}, u32[]{:S(2)}) copy-start(bf16[2,256,1,128]{3,1,2,0:T(8,128)(2,1)S(1)} %collective-permute-done.3) | copy-start | bytes 393220
  106.2 1.1 copy-start
  109.6 2.0 copy-start.13
  113.2 0.7 copy-start.14
  113.8 0.7 copy-start.15
  114.6 0.7 copy-start.16
  115.5 28.7 %collective-permute-start.7 = (bf16[2,256,1,128]{3,1,2,0:T(8,128)(2,1)S(1)}, bf16[2,256,1,128]{3,1,2,0:T(8,128)(2,1)S(1)}, u32[]{:S(2)}, u32[]{:S(2)}) collective-permute-start(bf16[2,256,1,128]{3,1,2,0:T(8,128)(2,1)S(1)} %get-tuple-element.341), channel_id=1, source_target_pairs={{32,0},{40,8},{48,16},{56,24},{64,32},{72,40},{80,48},{88,56},{96,... | collective-permute-start | bytes 393224 | tf_op jit(solution)/shard_map/ppermute | solution.py:12
  133.2 11.0 %collective-permute-start.6 = (bf16[2,256,1,128]{3,1,2,0:T(8,128)(2,1)}, bf16[2,256,1,128]{3,1,2,0:T(8,128)(2,1)S(1)}, u32[]{:S(2)}, u32[]{:S(2)}) collective-permute-start(bf16[2,256,1,128]{3,1,2,0:T(8,128)(2,1)} %copy-done.16), channel_id=1, source_target_pairs={{24,0},{32,8},{40,16},{48,24},{56,32},{64,40},{72,48},{80,56},{88,... | collective-permute-start | bytes 393224 | tf_op jit(solution)/shard_map/ppermute | solution.py:12
  135.1 9.1 %collective-permute-start.5 = (bf16[2,256,1,128]{3,1,2,0:T(8,128)(2,1)}, bf16[2,256,1,128]{3,1,2,0:T(8,128)(2,1)S(1)}, u32[]{:S(2)}, u32[]{:S(2)}) collective-permute-start(bf16[2,256,1,128]{3,1,2,0:T(8,128)(2,1)} %copy-done.15), channel_id=1, source_target_pairs={{16,0},{24,8},{32,16},{40,24},{48,32},{56,40},{64,48},{72,56},{80,... | collective-permute-start | bytes 393224 | tf_op jit(solution)/shard_map/ppermute | solution.py:12
  137.0 10.0 %collective-permute-start.4 = (bf16[2,256,1,128]{3,1,2,0:T(8,128)(2,1)}, bf16[2,256,1,128]{3,1,2,0:T(8,128)(2,1)S(1)}, u32[]{:S(2)}, u32[]{:S(2)}) collective-permute-start(bf16[2,256,1,128]{3,1,2,0:T(8,128)(2,1)} %copy-done.14), channel_id=1, source_target_pairs={{8,0},{16,8},{24,16},{32,24},{40,32},{48,40},{56,48},{64,56},{72,6... | collective-permute-start | bytes 393224 | tf_op jit(solution)/shard_map/ppermute | solution.py:12
  148.9 15.4 %all-to-all-start.7 = ((bf16[8,2,2048]{2,1,0:T(2,128)(2,1)}), bf16[8,2,2048]{2,1,0:T(2,128)(2,1)S(1)}, u32[]{:S(2)}, u32[]{:S(2)}) async-start(bf16[8,2,2048]{2,1,0:T(2,128)(2,1)} %reshape.636), calls=%async_computation.7 | async-start | bytes 131072 | tf_op jit(solution)/shard_map/all_to_all | solution.py:148
  164.4 11.5 %all-to-all-start.6 = ((bf16[8,2,2048]{2,1,0:T(2,128)(2,1)}), bf16[8,2,2048]{2,1,0:T(2,128)(2,1)S(1)}, u32[]{:S(2)}, u32[]{:S(2)}) async-start(bf16[8,2,2048]{2,1,0:T(2,128)(2,1)} %reshape.634), calls=%async_computation.6 | async-start | bytes 131072 | tf_op jit(solution)/shard_map/all_to_all | solution.py:147
  175.9 20.3 %all-to-all-start.3 = ((bf16[256,8,128]{2,1,0:T(8,128)(2,1)}), bf16[256,8,128]{2,1,0:T(8,128)(2,1)S(1)}, u32[]{:S(2)}, u32[]{:S(2)}) async-start(bf16[256,8,128]{2,1,0:T(8,128)(2,1)} %bitcast.789), calls=%async_computation.3 | async-start | bytes 1048576 | tf_op jit(solution)/shard_map/all_to_all | solution.py:145
  196.1 21.7 %all-to-all-start.5 = ((bf16[256,8,128]{2,1,0:T(8,128)(2,1)}), bf16[256,8,128]{2,1,0:T(8,128)(2,1)S(1)}, u32[]{:S(2)}, u32[]{:S(2)}) async-start(bf16[256,8,128]{2,1,0:T(8,128)(2,1)} %bitcast.786), calls=%async_computation.5 | async-start | bytes 1048576 | tf_op jit(solution)/shard_map/all_to_all | solution.py:146
where the time goes:
time: 221 us; the launch traced here: 219 us
  waiting for transfers between devices  104 us (47%)
  starting transfers between devices  77.8 us (35%)
  local copies, waits for them, and re-layouts  16.8 us (8%)
  matrix products  9.71 us (4%)
  other arithmetic  4.88 us (2%)
  between operations  4.32 us (2%)
    ppermute x8, starting transfers between devices, passed_along(): return lax.ppermute(array, axis, pairs)  39.6 us
    ppermute x8, waiting for transfers between devices, passed_along(): return lax.ppermute(array, axis, pairs)  29.6 us
    all_to_all x1, waiting for transfers between devices, shards(): lax.all_to_all(query_in, 'head', split_axis=1, concat_axis=0, tiled=True)  17 us
    all_to_all x1, waiting for transfers between devices, shards(): lax.all_to_all(grad_q_heads, 'head', split_axis=0, concat_axis=1, tiled=T...  15.8 us
    all_to_all x1, waiting for transfers between devices, shards(): lax.all_to_all(out_heads, 'head', split_axis=0, concat_axis=1, tiled=True)  15.4 us
    unnamed x38, local copies, waits for them, and re-layouts  11.1 us
    all_to_all x1, starting transfers between devices, shards(): lax.all_to_all(key_in, 'head', split_axis=1, concat_axis=0, tiled=True)  10.3 us
    all_to_all x1, starting transfers between devices, shards(): lax.all_to_all(grad_pair[1], 'head', split_axis=0, concat_axis=1, tiled=T...  7.22 us
  transfers between devices with their start and end apart: 16, of which 12 were waited for; matrix products, arithmetic and copies ran while one was open for 7% of the time, Pallas kernels for 0%

commit v1 on v0

v1 whole, which is shorter than its diff:
```python
import functools
import math

import jax
import jax.numpy as jnp
from jax import lax
from jax.experimental import pallas as pl
from jax.experimental.pallas import tpu as pltpu
from jax.sharding import Mesh
from jax.sharding import PartitionSpec as P

AXES = ("x", "y", "l", "h", "c")
SIZES = (4, 8, 2, 4, 2)
RING = ("l", "h")
COLUMNS = ("x", "y")

HD = 128
KVH = 8
GROUP = 8
TOK = 32
COL = 512
REACH = 2
KEYS = (REACH + 1) * COL
PIECE = TOK * GROUP
TILE = 128
PAIR = 2
ROWS = PAIR * PIECE
BLOCKS = KVH // PAIR
SCALE = HD**-0.5
SCALE2 = SCALE * math.log2(math.e)
NEG = -1e30

F32 = jnp.float32
BF16 = jnp.bfloat16
VMEM = pl.BlockSpec(memory_space=pltpu.VMEM)
SMEM = pl.BlockSpec(memory_space=pltpu.SMEM)
NT = (((1,), (1,)), ((), ()))
TN = (((0,), (0,)), ((), ()))
NN = (((1,), (0,)), ((), ()))


def dot(a, b, dims):
    return lax.dot_general(a, b, dims, preferred_element_type=F32)


def call(kernel, outs, ins, scratch, name, flops=0, nbytes=1 << 20):
    return pl.pallas_call(
        kernel,
        out_shape=outs,
        in_specs=ins,
        out_specs=[VMEM] * len(outs),
        scratch_shapes=scratch,
        compiler_params=pltpu.CompilerParams(vmem_limit_bytes=48 << 20),
        cost_estimate=pl.CostEstimate(flops=flops, bytes_accessed=nbytes, transcendentals=0),
        name=name,
    )


def shape(*dims, dtype=BF16):
    return jax.ShapeDtypeStruct(dims, dtype)


def put_heads(x_ref, out_ref):
    for pair in range(KVH // 2):
        both = x_ref[:, pair * 2 * GROUP : (pair + 1) * 2 * GROUP, :].astype(F32)
        for part in range(2):
            half = both[:, part * GROUP : (part + 1) * GROUP, :]
            out_ref[2 * pair + part, 0:PIECE, :] = half.reshape(PIECE, HD).astype(BF16)


def take_heads(x_ref, out_ref):
    for pair in range(KVH // 2):
        halves = [
            x_ref[2 * pair + part, 0:PIECE, :].astype(F32).reshape(TOK, GROUP, HD) for part in range(2)
        ]
        out_ref[:, pair * 2 * GROUP : (pair + 1) * 2 * GROUP, :] = jnp.concatenate(halves, axis=1).astype(
            BF16
        )


def pack_qkv(q_ref, k_ref, v_ref, out_ref, wide):
    put_heads(q_ref, out_ref)
    for at, ref in ((0, k_ref), (1, v_ref)):
        wide[...] = ref[...].astype(F32).reshape(TOK * KVH, HD)
        for j in range(KVH):
            out_ref[j, PIECE + at * TOK : PIECE + (at + 1) * TOK, :] = wide[
                pl.ds(j, TOK, stride=KVH), :
            ].astype(BF16)


def pack_g(g_ref, out_ref):
    put_heads(g_ref, out_ref)


def unpack_o(x_ref, out_ref):
    take_heads(x_ref, out_ref)


def unpack_grads(x_ref, q_ref, k_ref, v_ref, wide):
    take_heads(x_ref, q_ref)
    for at, ref in ((0, k_ref), (1, v_ref)):
        for j in range(KVH):
            wide[pl.ds(j, TOK, stride=KVH), :] = x_ref[
                j, PIECE + at * TOK : PIECE + (at + 1) * TOK, :
            ].astype(F32)
        ref[...] = wide[...].reshape(TOK, KVH, HD).astype(BF16)


def visible(start, place, tile):
    index = tile * TILE + lax.broadcasted_iota(jnp.int32, (TILE, ROWS), 0)
    return (index >= start) & (index <= place)


def rows_of(ref, block):
    return ref[pl.ds(block * PAIR, PAIR), 0:PIECE, :].reshape(ROWS, HD)


def place_of(block, core):
    row = lax.broadcasted_iota(jnp.int32, (1, ROWS), 1)
    return REACH * COL + block * (PAIR * 2 * TOK) + (row // PIECE) * (2 * TOK) + core * TOK + (row % PIECE) // GROUP


def first_tile(low_ref, block):
    return low_ref[block] // TILE


def last_tile(block):
    return (REACH * COL + (block + 1) * (PAIR * 2 * TOK) - 1) // TILE


def forward(low_ref, core_ref, a_ref, start_ref, own_ref, other_ref, old_ref, other_old_ref,
            out_ref, stat_ref, keys, values, scores, total, top):
    core = core_ref[0]
    for column in range(REACH + 1):
        for piece in range(KVH):
            base = (REACH - column) * COL + piece * 2 * TOK
            for ref, old, which in ((own_ref, old_ref, core), (other_ref, other_old_ref, 1 - core)):
                at = pl.ds(pl.multiple_of(base + which * TOK, TOK), TOK)
                got = ref[piece] if column == 0 else old[column - 1, piece]
                keys[at, :] = got[0:TOK]
                values[at, :] = got[TOK : 2 * TOK]

    def one_block(block, _):
        rows = rows_of(a_ref, block)
        start = start_ref[block]
        place = place_of(block, core)
        first, last = first_tile(low_ref, block), last_tile(block)
        top[...] = jnp.full(top.shape, NEG, F32)

        def score(tile, _):
            at = pl.ds(pl.multiple_of(tile * TILE, TILE), TILE)
            s = dot(keys[at, :], rows, NT)
            s = jnp.where(visible(start, place, tile), s, NEG)
            scores[at, :] = s
            top[...] = jnp.maximum(top[...], jnp.max(s.reshape(TILE // 8, 8, ROWS), axis=0))
            return 0

        lax.fori_loop(first, last + 1, score, 0)
        row_top = jnp.max(top[...], axis=0, keepdims=True) * SCALE2
        top[...] = jnp.zeros(top.shape, F32)
        total[...] = jnp.zeros(total.shape, F32)

        def weigh(tile, _):
            at = pl.ds(pl.multiple_of(tile * TILE, TILE), TILE)
            p = jnp.exp2(scores[at, :] * SCALE2 - row_top)
            top[...] += jnp.sum(p.reshape(TILE // 8, 8, ROWS), axis=0)
            total[...] += dot(values[at, :], p.astype(BF16), TN)
            return 0

        lax.fori_loop(first, last + 1, weigh, 0)
        row_sum = jnp.sum(top[...], axis=0, keepdims=True)
        stat_ref[block] = row_top + jnp.log2(row_sum)
        out = jnp.transpose(total[...] / row_sum)
        out_ref[pl.ds(block * PAIR, PAIR)] = out.astype(BF16).reshape(PAIR, PIECE, HD)
        return 0

    lax.fori_loop(0, BLOCKS, one_block, 0)


def backward(low_ref, core_ref, a_ref, g_ref, o_ref, start_ref, stat_ref, own_ref, other_ref, old_ref, other_old_ref,
             dq_ref, mine_ref, theirs_ref, keys, values, dk, dv, total):
    core = core_ref[0]
    for column in range(REACH + 1):
        for piece in range(KVH):
            base = (REACH - column) * COL + piece * 2 * TOK
            for ref, old, which in ((own_ref, old_ref, core), (other_ref, other_old_ref, 1 - core)):
                at = pl.ds(pl.multiple_of(base + which * TOK, TOK), TOK)
                got = ref[piece] if column == 0 else old[column - 1, piece]
                keys[at, :] = got[0:TOK]
                values[at, :] = got[TOK : 2 * TOK]
    dk[...] = jnp.zeros(dk.shape, F32)
    dv[...] = jnp.zeros(dv.shape, F32)

    def one_block(block, _):
        rows = rows_of(a_ref, block)
        grads = rows_of(g_ref, block)
        outs = rows_of(o_ref, block)
        start = start_ref[block]
        stat = stat_ref[block]
        place = place_of(block, core)
        prod = grads.astype(F32) * outs.astype(F32)
        high = prod.astype(BF16)
        low = (prod - high.astype(F32)).astype(BF16)
        ones = jnp.ones((8, HD), BF16)
        drift = (dot(ones, high, NT) + dot(ones, low, NT))[0:1]
        total[...] = jnp.zeros(total.shape, F32)

        def step(tile, _):
            at = pl.ds(pl.multiple_of(tile * TILE, TILE), TILE)
            key, value = keys[at, :], values[at, :]
            s = dot(key, rows, NT)
            dp = dot(value, grads, NT)
            p = jnp.where(visible(start, place, tile), jnp.exp2(s * SCALE2 - stat), 0.0)
            ds = (p * (dp - drift)).astype(BF16)
            dv[at, :] += dot(p.astype(BF16), grads, NN)
            dk[at, :] += dot(ds, rows, NN)
            total[...] += dot(key, ds, TN)
            return 0

        lax.fori_loop(first_tile(low_ref, block), last_tile(block) + 1, step, 0)
        dq = jnp.transpose(total[...] * SCALE)
        dq_ref[pl.ds(block * PAIR, PAIR)] = dq.astype(BF16).reshape(PAIR, PIECE, HD)
        return 0

    lax.fori_loop(0, BLOCKS, one_block, 0)
    for column in range(REACH + 1):
        for piece in range(KVH):
            base = (REACH - column) * COL + piece * 2 * TOK
            for ref, which in ((mine_ref, core), (theirs_ref, 1 - core)):
                at = pl.ds(pl.multiple_of(base + which * TOK, TOK), TOK)
                ref[column, piece, 0:TOK] = (dk[at, :] * SCALE).astype(ref.dtype)
                ref[column, piece, TOK : 2 * TOK] = dv[at, :].astype(ref.dtype)


def old_terms(mine_ref, got_ref, one_ref, two_ref):
    one_ref[...] = (mine_ref[1] + got_ref[1].astype(F32)).astype(BF16)
    two_ref[...] = (mine_ref[2] + got_ref[2].astype(F32)).astype(BF16)


def pack_grads(dq_ref, mine_ref, got_ref, one_ref, two_ref, out_ref):
    out_ref[:, 0:PIECE, :] = dq_ref[...]
    out_ref[:, PIECE : PIECE + 2 * TOK, :] = (
        mine_ref[0] + got_ref[0].astype(F32) + one_ref[...].astype(F32) + two_ref[...].astype(F32)
    ).astype(BF16)


def exchange(x):
    return lax.all_to_all(x, RING, split_axis=0, concat_axis=0, tiled=True)


def shifted(x, by):
    count = SIZES[0] * SIZES[1]
    return lax.ppermute(x, COLUMNS, [(i, (i + by) % count) for i in range(count)])


def swapped(x):
    return lax.ppermute(x, "c", [(0, 1), (1, 0)])


def shards(query_in, key_in, value_in, grad_out, doc_lengths):
    wide = TOK * GROUP
    packed = call(
        pack_qkv, [shape(KVH, PIECE + 2 * TOK, HD)], [VMEM] * 3, [pltpu.VMEM((TOK * KVH, HD), F32)], "pack_qkv"
    )(query_in, key_in, value_in)[0]
    a = exchange(packed)
    packed_g = call(pack_g, [shape(KVH, PIECE, HD)], [VMEM], [], "pack_g")(grad_out)[0]
    kv = a[:, PIECE:, :]
    old_one, old_two = shifted(kv, 1), shifted(kv, 2)
    other = swapped(kv)
    g = exchange(packed_g)
    old = jnp.stack([old_one, old_two])
    other_old = swapped(old)

    column = lax.axis_index(COLUMNS)
    core = lax.axis_index("c")
    ends = jnp.cumsum(doc_lengths)
    row = jnp.arange(ROWS, dtype=jnp.int32)
    piece = jnp.arange(BLOCKS, dtype=jnp.int32)[:, None] * PAIR + (row // PIECE)[None, :]
    place = column * COL + piece * (2 * TOK) + core * TOK + ((row % PIECE) // GROUP)[None, :]
    start = jnp.max(
        jnp.where(ends[:, None, None] <= place[None], ends[:, None, None], 0), axis=0
    )
    start = jnp.maximum(start - (column - REACH) * COL, 0).astype(jnp.int32)
    low = start[:, 0]
    start = start[:, None, :]
    core_in = core.astype(jnp.int32)[None]

    flops = 2 * BLOCKS * ROWS * 1024 * HD
    out, stat = call(
        forward,
        [shape(KVH, PIECE, HD), shape(BLOCKS, 1, ROWS, dtype=F32)],
        [SMEM] * 2 + [VMEM] * 6,
        [
            pltpu.VMEM((KEYS, HD), BF16),
            pltpu.VMEM((KEYS, HD), BF16),
            pltpu.VMEM((KEYS, ROWS), F32),
            pltpu.VMEM((HD, ROWS), F32),
            pltpu.VMEM((8, ROWS), F32),
        ],
        "attend",
        2 * flops,
    )(low, core_in, a, start, kv, other, old, other_old)
    out_back = exchange(out)
    dq, mine, theirs = call(
        backward,
        [
            shape(KVH, PIECE, HD),
            shape(REACH + 1, KVH, 2 * TOK, HD, dtype=F32),
            shape(REACH + 1, KVH, 2 * TOK, HD),
        ],
        [SMEM] * 2 + [VMEM] * 9,
        [
            pltpu.VMEM((KEYS, HD), BF16),
            pltpu.VMEM((KEYS, HD), BF16),
            pltpu.VMEM((KEYS, HD), F32),
            pltpu.VMEM((KEYS, HD), F32),
            pltpu.VMEM((HD, ROWS), F32),
        ],
        "gradients",
        5 * flops,
    )(low, core_in, a, g, out, start, stat, kv, other, old, other_old)
    got = swapped(theirs)
    term = shape(KVH, 2 * TOK, HD)
    one, two = call(old_terms, [term, term], [VMEM] * 2, [], "old_terms")(mine, got)
    back_one, back_two = shifted(one, -1), shifted(two, -2)
    packed_grads = call(pack_grads, [shape(KVH, PIECE + 2 * TOK, HD)], [VMEM] * 5, [], "pack_grads")(
        dq, mine, got, back_one, back_two
    )[0]
    grads_back = exchange(packed_grads)
    attn_out = call(unpack_o, [shape(TOK, KVH * GROUP, HD)], [VMEM], [], "unpack_o")(out_back)[0]
    grad_query, grad_key, grad_value = call(
        unpack_grads,
        [shape(TOK, KVH * GROUP, HD), shape(TOK, KVH, HD), shape(TOK, KVH, HD)],
        [VMEM],
        [pltpu.VMEM((TOK * KVH, HD), F32)],
        "unpack_grads",
    )(grads_back)
    return (attn_out, grad_query, grad_key, grad_value)


def solution(mesh):
    fine = Mesh(mesh.devices.reshape(SIZES), AXES)
    tokens = P(AXES, None, None)
    return jax.shard_map(
        shards,
        mesh=fine,
        in_specs=(tokens, tokens, tokens, tokens, P()),
        out_specs=(tokens, tokens, tokens, tokens),
        check_vma=False,
    )
```

time: 221 us -> 135 us (0.61)
  the two profiles are of different devices: /device:TPU:6 before, /device:TPU:76 now
where the time goes in v1:
time: 135 us; the launch traced here: 134 us
  waiting for transfers between devices  60.2 us (45%)
  starting transfers between devices  48.3 us (36%)
  Pallas kernels  21.1 us (16%)
  local copies, waits for them, and re-layouts  3.59 us (3%)
    all_to_all x4, waiting for transfers between devices, exchange(): return lax.all_to_all(x, RING, split_axis=0, concat_axis=0, tiled=True)  35.4 us
    all_to_all x4, starting transfers between devices, exchange(): return lax.all_to_all(x, RING, split_axis=0, concat_axis=0, tiled=True)  27.8 us
    ppermute x4, waiting for transfers between devices, shifted(): lax.ppermute(x, COLUMNS, [(i, (i + by) % count) for i in range(count)])  21.8 us
    ppermute x4, starting transfers between devices, shifted(): lax.ppermute(x, COLUMNS, [(i, (i + by) % count) for i in range(count)])  14.7 us
    pallas_call x1, Pallas kernels, shards(): call(backward, [shape(KVH, PIECE, HD), shape(REACH + 1, KVH, 2 * TOK, HD,...  8.59 us
    pallas_call x1, Pallas kernels, shards(): call(forward, [shape(KVH, PIECE, HD), shape(BLOCKS, 1, ROWS, dtype=F32)],...  7.83 us
    ppermute x3, starting transfers between devices, swapped(): return lax.ppermute(x, 'c', [(0, 1), (1, 0)])  5.76 us
    unnamed x10, local copies, waits for them, and re-layouts  3.37 us
  transfers between devices with their start and end apart: 11, of which 8 were waited for; matrix products, arithmetic and copies ran while one was open for 0% of the time, Pallas kernels for 14%

profile of v1, /device:TPU:76, one launch (start us, length us, event | category | flops | bytes accessed | tf_op | source)
XLA Modules:
  0.0 134.5 jit_solution(9264129894106708993)
XLA Ops:
  0.6 1.0 copy-done
  1.7 0.8 copy-done.2
  2.5 0.8 copy-done.3
  3.4 1.0 pack_qkv.1
  4.4 10.1 %all-to-all-start = ((bf16[8,320,128]{2,1,0:T(8,128)(2,1)}), bf16[8,320,128]{2,1,0:T(8,128)(2,1)S(1)}, u32[]{:S(2)}, u32[]{:S(2)}) async-start(bf16[8,320,128]{2,1,0:T(8,128)(2,1)} %pack_qkv.1), calls=%async_computation | async-start | bytes 1310720 | tf_op jit(solution)/shard_map/all_to_all | solution.py:248
  14.5 0.9 pack_g.1
  15.4 17.9 %all-to-all-done.a_ref = bf16[8,320,128]{2,1,0:T(8,128)(2,1)S(1)} async-done(((bf16[8,320,128]{2,1,0:T(8,128)(2,1)}), bf16[8,320,128]{2,1,0:T(8,128)(2,1)S(1)}, u32[]{:S(2)}, u32[]{:S(2)}) %all-to-all-start) | async-done | bytes 655392 | tf_op jit(solution)/shard_map/all_to_all | solution.py:248
  33.3 3.4 %all-to-all-start.2 = ((bf16[8,256,128]{2,1,0:T(8,128)(2,1)}), bf16[8,256,128]{2,1,0:T(8,128)(2,1)S(1)}, u32[]{:S(2)}, u32[]{:S(2)}) async-start(bf16[8,256,128]{2,1,0:T(8,128)(2,1)} %pack_g.1), calls=%async_computation.2 | async-start | bytes 1048576 | tf_op jit(solution)/shard_map/all_to_all | solution.py:248
  36.8 4.5 %collective-permute-start.2 = (bf16[8,64,128]{2,1,0:T(8,128)(2,1)S(1)}, bf16[8,64,128]{2,1,0:T(8,128)(2,1)S(1)}, u32[]{:S(2)}, u32[]{:S(2)}) collective-permute-start(bf16[8,64,128]{2,1,0:T(8,128)(2,1)S(1)} %slice.9.own_ref), channel_id=1, source_target_pairs={{0,32},{16,48},{32,64},{48,80},{64,96},{80,112},{96,128},{112,144}... | collective-permute-start | bytes 393224 | tf_op jit(solution)/shard_map/ppermute | solution.py:253
  41.3 4.7 %collective-permute-start.1 = (bf16[8,64,128]{2,1,0:T(8,128)(2,1)S(1)}, bf16[8,64,128]{2,1,0:T(8,128)(2,1)S(1)}, u32[]{:S(2)}, u32[]{:S(2)}) collective-permute-start(bf16[8,64,128]{2,1,0:T(8,128)(2,1)S(1)} %slice.9.own_ref), channel_id=1, source_target_pairs={{0,16},{16,32},{32,48},{48,64},{64,80},{80,96},{96,112},{112,128},... | collective-permute-start | bytes 393224 | tf_op jit(solution)/shard_map/ppermute | solution.py:253
  46.1 0.7 copy-done.4
  46.9 0.1 reduce
  47.0 0.1 select_reduce_fusion
  47.1 1.9 %collective-permute-start = (bf16[8,64,128]{2,1,0:T(8,128)(2,1)S(1)}, bf16[8,64,128]{2,1,0:T(8,128)(2,1)S(1)}, u32[]{:S(2)}, u32[]{:S(2)}) collective-permute-start(bf16[8,64,128]{2,1,0:T(8,128)(2,1)S(1)} %slice.9.own_ref), channel_id=1, source_target_pairs={{0,1},{1,0},{2,3},{3,2},{4,5},{5,4},{6,7},{7,6},{8,9},{9,8},{10,11... | collective-permute-start | bytes 393224 | tf_op jit(solution)/shard_map/ppermute | solution.py:257
  49.1 0.4 collective-permute-done.2
  49.4 0.8 collective-permute-done.1
  50.3 1.9 %collective-permute-start.3 = (bf16[2,8,64,128]{3,2,1,0:T(8,128)(2,1)S(1)}, bf16[2,8,64,128]{3,2,1,0:T(8,128)(2,1)S(1)}, u32[]{:S(2)}, u32[]{:S(2)}) collective-permute-start(bf16[2,8,64,128]{3,2,1,0:T(8,128)(2,1)S(1)} %pad_maximum_fusion.old_ref), channel_id=1, source_target_pairs={{0,1},{1,0},{2,3},{3,2},{4,5},{5,4},{6,7},{7,6},{8,9},{9,8},{10,11... | collective-permute-start | bytes 786440 | tf_op jit(solution)/shard_map/ppermute | solution.py:257
  52.3 1.4 %collective-permute-done.3.other_old_ref = bf16[2,8,64,128]{3,2,1,0:T(8,128)(2,1)S(1)} collective-permute-done((bf16[2,8,64,128]{3,2,1,0:T(8,128)(2,1)S(1)}, bf16[2,8,64,128]{3,2,1,0:T(8,128)(2,1)S(1)}, u32[]{:S(2)}, u32[]{:S(2)}) %collective-permute-start.3) | collective-permute-done | bytes 262176 | tf_op jit(solution)/shard_map/ppermute | solution.py:257
  53.7 7.8 %attend.1 = (bf16[8,256,128]{2,1,0:T(8,128)(2,1)}, f32[4,1,512]{2,1,0:T(1,128)S(1)}) custom-call(s32[4]{0:T(128)S(1)} %slice_reduce_fusion.low_ref, s32[1]{0:T(128)} %bitcast.1.core_ref, bf16[8,320,128]{2,1,0:T(8,128)(2,1)S(1)} %all-to-all-done.a_ref, s32[4,1,512]{2,1,0:T(1,128)S(1)} %max.18.start_ref, bf16[8,64,128]{2,1,0:T(8,128)(2,1)S(1)} %slice.9.own_ref, ...), custom_call_target="tpu_custom_call" | custom-call | flops 1073741824 | bytes 1048576 | tf_op jit(solution)/shard_map/attend/pallas_call | solution.py:289
  61.5 7.1 %all-to-all-start.1 = ((bf16[8,256,128]{2,1,0:T(8,128)(2,1)}), bf16[8,256,128]{2,1,0:T(8,128)(2,1)S(1)}, u32[]{:S(2)}, u32[]{:S(2)}) async-start(bf16[8,256,128]{2,1,0:T(8,128)(2,1)} %get-tuple-element.14.o_ref), calls=%async_computation.1 | async-start | bytes 1048576 | tf_op jit(solution)/shard_map/all_to_all | solution.py:248
  68.6 8.6 %gradients.1 = (bf16[8,256,128]{2,1,0:T(8,128)(2,1)S(1)}, f32[3,8,64,128]{3,2,1,0:T(8,128)S(1)}, bf16[3,8,64,128]{3,2,1,0:T(8,128)(2,1)S(1)}) custom-call(s32[4]{0:T(128)S(1)} %slice_reduce_fusion.low_ref, s32[1]{0:T(128)} %bitcast.1.core_ref, bf16[8,320,128]{2,1,0:T(8,128)(2,1)S(1)} %all-to-all-done.a_ref, bf16[8,256,128]{2,1,0:T(8,128)(2,1)S(1)} %all-to-all-done.2.g_ref, ...), custom_call_target="tpu_custom_call" | custom-call | flops 2684354560 | bytes 1048576 | tf_op jit(solution)/shard_map/gradients/pallas_call | solution.py:304
  77.2 1.9 %collective-permute-start.4 = (bf16[3,8,64,128]{3,2,1,0:T(8,128)(2,1)S(1)}, bf16[3,8,64,128]{3,2,1,0:T(8,128)(2,1)S(1)}, u32[]{:S(2)}, u32[]{:S(2)}) collective-permute-start(bf16[3,8,64,128]{3,2,1,0:T(8,128)(2,1)S(1)} %get-tuple-element.18), channel_id=1, source_target_pairs={{0,1},{1,0},{2,3},{3,2},{4,5},{5,4},{6,7},{7,6},{8,9},{9,8},{10,11... | collective-permute-start | bytes 1179656 | tf_op jit(solution)/shard_map/ppermute | solution.py:257
  79.1 1.7 %collective-permute-done.4.got_ref = bf16[3,8,64,128]{3,2,1,0:T(8,128)(2,1)S(1)} collective-permute-done((bf16[3,8,64,128]{3,2,1,0:T(8,128)(2,1)S(1)}, bf16[3,8,64,128]{3,2,1,0:T(8,128)(2,1)S(1)}, u32[]{:S(2)}, u32[]{:S(2)}) %collective-permute-start.4) | collective-permute-done | bytes 393248 | tf_op jit(solution)/shard_map/ppermute | solution.py:257
  80.9 3.6 %collective-permute-start.5 = (bf16[8,64,128]{2,1,0:T(8,128)(2,1)S(1)}, bf16[8,64,128]{2,1,0:T(8,128)(2,1)S(1)}, u32[]{:S(2)}, u32[]{:S(2)}) collective-permute-start(bf16[8,64,128]{2,1,0:T(8,128)(2,1)S(1)} %get-tuple-element.19), channel_id=1, source_target_pairs={{0,496},{16,0},{32,16},{48,32},{64,48},{80,64},{96,80},{112,96},{1... | collective-permute-start | bytes 393224 | tf_op jit(solution)/shard_map/ppermute | solution.py:253
  84.5 1.9 %collective-permute-start.6 = (bf16[8,64,128]{2,1,0:T(8,128)(2,1)S(1)}, bf16[8,64,128]{2,1,0:T(8,128)(2,1)S(1)}, u32[]{:S(2)}, u32[]{:S(2)}) collective-permute-start(bf16[8,64,128]{2,1,0:T(8,128)(2,1)S(1)} %get-tuple-element.20), channel_id=1, source_target_pairs={{0,480},{16,496},{32,0},{48,16},{64,32},{80,48},{96,64},{112,80},{... | collective-permute-start | bytes 393224 | tf_op jit(solution)/shard_map/ppermute | solution.py:253
  86.4 15.0 %collective-permute-done.5.one_ref = bf16[8,64,128]{2,1,0:T(8,128)(2,1)S(1)} collective-permute-done((bf16[8,64,128]{2,1,0:T(8,128)(2,1)S(1)}, bf16[8,64,128]{2,1,0:T(8,128)(2,1)S(1)}, u32[]{:S(2)}, u32[]{:S(2)}) %collective-permute-start.5) | collective-permute-done | bytes 131104 | tf_op jit(solution)/shard_map/ppermute | solution.py:253
  101.4 5.6 %collective-permute-done.6.two_ref = bf16[8,64,128]{2,1,0:T(8,128)(2,1)S(1)} collective-permute-done((bf16[8,64,128]{2,1,0:T(8,128)(2,1)S(1)}, bf16[8,64,128]{2,1,0:T(8,128)(2,1)S(1)}, u32[]{:S(2)}, u32[]{:S(2)}) %collective-permute-start.6) | collective-permute-done | bytes 131104 | tf_op jit(solution)/shard_map/ppermute | solution.py:253
  107.0 0.9 pack_grads.1
  108.0 7.2 %all-to-all-start.3 = ((bf16[8,320,128]{2,1,0:T(8,128)(2,1)}), bf16[8,320,128]{2,1,0:T(8,128)(2,1)S(1)}, u32[]{:S(2)}, u32[]{:S(2)}) async-start(bf16[8,320,128]{2,1,0:T(8,128)(2,1)} %pack_grads.1), calls=%async_computation.3 | async-start | bytes 1310720 | tf_op jit(solution)/shard_map/all_to_all | solution.py:248
  115.2 0.9 unpack_o.1
  116.1 17.4 %all-to-all-done.3.x_ref = bf16[8,320,128]{2,1,0:T(8,128)(2,1)S(1)} async-done(((bf16[8,320,128]{2,1,0:T(8,128)(2,1)}), bf16[8,320,128]{2,1,0:T(8,128)(2,1)S(1)}, u32[]{:S(2)}, u32[]{:S(2)}) %all-to-all-start.3) | async-done | bytes 655392 | tf_op jit(solution)/shard_map/all_to_all | solution.py:248
  133.5 0.9 unpack_grads.1
  (20 shorter events, 0.5 us)
Async XLA Ops:
  0.6 1.0 copy-start
  1.7 0.8 copy-start.2
  2.5 0.8 copy-start.3
  4.4 10.1 %copy-start.1 = (bf16[32,64,128]{2,1,0:T(8,128)(2,1)S(1)}, bf16[32,64,128]{2,1,0:T(8,128)(2,1)}, u32[]{:S(2)}) copy-start(bf16[32,64,128]{2,1,0:T(8,128)(2,1)} %g_ref.1) | copy-start | bytes 1572868
  4.4 28.9 %all-to-all-start = ((bf16[8,320,128]{2,1,0:T(8,128)(2,1)}), bf16[8,320,128]{2,1,0:T(8,128)(2,1)S(1)}, u32[]{:S(2)}, u32[]{:S(2)}) async-start(bf16[8,320,128]{2,1,0:T(8,128)(2,1)} %pack_qkv.1), calls=%async_computation | async-start | bytes 1310720 | tf_op jit(solution)/shard_map/all_to_all | solution.py:248
  33.3 28.2 %all-to-all-start.2 = ((bf16[8,256,128]{2,1,0:T(8,128)(2,1)}), bf16[8,256,128]{2,1,0:T(8,128)(2,1)S(1)}, u32[]{:S(2)}, u32[]{:S(2)}) async-start(bf16[8,256,128]{2,1,0:T(8,128)(2,1)} %pack_g.1), calls=%async_computation.2 | async-start | bytes 1048576 | tf_op jit(solution)/shard_map/all_to_all | solution.py:248
  36.8 12.6 %collective-permute-start.2 = (bf16[8,64,128]{2,1,0:T(8,128)(2,1)S(1)}, bf16[8,64,128]{2,1,0:T(8,128)(2,1)S(1)}, u32[]{:S(2)}, u32[]{:S(2)}) collective-permute-start(bf16[8,64,128]{2,1,0:T(8,128)(2,1)S(1)} %slice.9.own_ref), channel_id=1, source_target_pairs={{0,32},{16,48},{32,64},{48,80},{64,96},{80,112},{96,128},{112,144}... | collective-permute-start | bytes 393224 | tf_op jit(solution)/shard_map/ppermute | solution.py:253
  41.3 8.9 %collective-permute-start.1 = (bf16[8,64,128]{2,1,0:T(8,128)(2,1)S(1)}, bf16[8,64,128]{2,1,0:T(8,128)(2,1)S(1)}, u32[]{:S(2)}, u32[]{:S(2)}) collective-permute-start(bf16[8,64,128]{2,1,0:T(8,128)(2,1)S(1)} %slice.9.own_ref), channel_id=1, source_target_pairs={{0,16},{16,32},{32,48},{48,64},{64,80},{80,96},{96,112},{112,128},... | collective-permute-start | bytes 393224 | tf_op jit(solution)/shard_map/ppermute | solution.py:253
  46.1 0.7 copy-start.4
  47.1 5.2 %collective-permute-start = (bf16[8,64,128]{2,1,0:T(8,128)(2,1)S(1)}, bf16[8,64,128]{2,1,0:T(8,128)(2,1)S(1)}, u32[]{:S(2)}, u32[]{:S(2)}) collective-permute-start(bf16[8,64,128]{2,1,0:T(8,128)(2,1)S(1)} %slice.9.own_ref), channel_id=1, source_target_pairs={{0,1},{1,0},{2,3},{3,2},{4,5},{5,4},{6,7},{7,6},{8,9},{9,8},{10,11... | collective-permute-start | bytes 393224 | tf_op jit(solution)/shard_map/ppermute | solution.py:257
  50.3 3.4 %collective-permute-start.3 = (bf16[2,8,64,128]{3,2,1,0:T(8,128)(2,1)S(1)}, bf16[2,8,64,128]{3,2,1,0:T(8,128)(2,1)S(1)}, u32[]{:S(2)}, u32[]{:S(2)}) collective-permute-start(bf16[2,8,64,128]{3,2,1,0:T(8,128)(2,1)S(1)} %pad_maximum_fusion.old_ref), channel_id=1, source_target_pairs={{0,1},{1,0},{2,3},{3,2},{4,5},{5,4},{6,7},{7,6},{8,9},{9,8},{10,11... | collective-permute-start | bytes 786440 | tf_op jit(solution)/shard_map/ppermute | solution.py:257
  61.5 46.5 %all-to-all-start.1 = ((bf16[8,256,128]{2,1,0:T(8,128)(2,1)}), bf16[8,256,128]{2,1,0:T(8,128)(2,1)S(1)}, u32[]{:S(2)}, u32[]{:S(2)}) async-start(bf16[8,256,128]{2,1,0:T(8,128)(2,1)} %get-tuple-element.14.o_ref), calls=%async_computation.1 | async-start | bytes 1048576 | tf_op jit(solution)/shard_map/all_to_all | solution.py:248
  77.2 3.6 %collective-permute-start.4 = (bf16[3,8,64,128]{3,2,1,0:T(8,128)(2,1)S(1)}, bf16[3,8,64,128]{3,2,1,0:T(8,128)(2,1)S(1)}, u32[]{:S(2)}, u32[]{:S(2)}) collective-permute-start(bf16[3,8,64,128]{3,2,1,0:T(8,128)(2,1)S(1)} %get-tuple-element.18), channel_id=1, source_target_pairs={{0,1},{1,0},{2,3},{3,2},{4,5},{5,4},{6,7},{7,6},{8,9},{9,8},{10,11... | collective-permute-start | bytes 1179656 | tf_op jit(solution)/shard_map/ppermute | solution.py:257
  80.9 20.6 %collective-permute-start.5 = (bf16[8,64,128]{2,1,0:T(8,128)(2,1)S(1)}, bf16[8,64,128]{2,1,0:T(8,128)(2,1)S(1)}, u32[]{:S(2)}, u32[]{:S(2)}) collective-permute-start(bf16[8,64,128]{2,1,0:T(8,128)(2,1)S(1)} %get-tuple-element.19), channel_id=1, source_target_pairs={{0,496},{16,0},{32,16},{48,32},{64,48},{80,64},{96,80},{112,96},{1... | collective-permute-start | bytes 393224 | tf_op jit(solution)/shard_map/ppermute | solution.py:253
  84.5 22.6 %collective-permute-start.6 = (bf16[8,64,128]{2,1,0:T(8,128)(2,1)S(1)}, bf16[8,64,128]{2,1,0:T(8,128)(2,1)S(1)}, u32[]{:S(2)}, u32[]{:S(2)}) collective-permute-start(bf16[8,64,128]{2,1,0:T(8,128)(2,1)S(1)} %get-tuple-element.20), channel_id=1, source_target_pairs={{0,480},{16,496},{32,0},{48,16},{64,32},{80,48},{96,64},{112,80},{... | collective-permute-start | bytes 393224 | tf_op jit(solution)/shard_map/ppermute | solution.py:253
  108.0 25.5 %all-to-all-start.3 = ((bf16[8,320,128]{2,1,0:T(8,128)(2,1)}), bf16[8,320,128]{2,1,0:T(8,128)(2,1)S(1)}, u32[]{:S(2)}, u32[]{:S(2)}) async-start(bf16[8,320,128]{2,1,0:T(8,128)(2,1)} %pack_grads.1), calls=%async_computation.3 | async-start | bytes 1310720 | tf_op jit(solution)/shard_map/all_to_all | solution.py:248

commit v2 on v1

v2 whole, which is shorter than its diff:
```python
import math

import jax
import jax.numpy as jnp
from jax import lax
from jax.experimental import pallas as pl
from jax.experimental.pallas import tpu as pltpu
from jax.sharding import Mesh
from jax.sharding import PartitionSpec as P

AXES = ("x", "y", "l", "h", "c")
SIZES = (4, 8, 2, 4, 2)
RING = ("l", "h")
COLUMNS = ("x", "y")

HD = 128
KVH = 8
GROUP = 8
TOK = 32
COL = 512
REACH = 2
KEYS = (REACH + 1) * COL
PIECE = TOK * GROUP
TILE = 128
PAIR = 2
ROWS = PAIR * PIECE
BLOCKS = KVH // PAIR
WIN = 9
SCALE = HD**-0.5
SCALE2 = SCALE * math.log2(math.e)
NEG = -1e30

F32 = jnp.float32
BF16 = jnp.bfloat16
VMEM = pl.BlockSpec(memory_space=pltpu.VMEM)
SMEM = pl.BlockSpec(memory_space=pltpu.SMEM)
NT = (((1,), (1,)), ((), ()))
NN = (((1,), (0,)), ((), ()))


def dot(a, b, dims):
    return lax.dot_general(a, b, dims, preferred_element_type=F32)


def call(kernel, outs, ins, scratch, name, flops=0, nbytes=1 << 20):
    return pl.pallas_call(
        kernel,
        out_shape=outs,
        in_specs=ins,
        out_specs=[VMEM] * len(outs),
        scratch_shapes=scratch,
        compiler_params=pltpu.CompilerParams(vmem_limit_bytes=48 << 20),
        cost_estimate=pl.CostEstimate(flops=flops, bytes_accessed=nbytes, transcendentals=0),
        name=name,
    )


def shape(*dims, dtype=BF16):
    return jax.ShapeDtypeStruct(dims, dtype)


def put_heads(x_ref, out_ref, at):
    for pair in range(KVH // 2):
        both = x_ref[:, pair * 2 * GROUP : (pair + 1) * 2 * GROUP, :].astype(F32)
        for part in range(2):
            half = both[:, part * GROUP : (part + 1) * GROUP, :]
            out_ref[2 * pair + part, at : at + PIECE, :] = half.reshape(PIECE, HD).astype(BF16)


def take_heads(x_ref, at, out_ref):
    for pair in range(KVH // 2):
        halves = [
            x_ref[2 * pair + part, at : at + PIECE, :].astype(F32).reshape(TOK, GROUP, HD)
            for part in range(2)
        ]
        both = jnp.concatenate(halves, axis=1).astype(BF16)
        out_ref[:, pair * 2 * GROUP : (pair + 1) * 2 * GROUP, :] = both


def pack_kv(k_ref, v_ref, out_ref, wide):
    for at, ref in ((0, k_ref), (TOK, v_ref)):
        wide[...] = ref[...].astype(F32).reshape(TOK * KVH, HD)
        for j in range(KVH):
            out_ref[j, at : at + TOK, :] = wide[pl.ds(j, TOK, stride=KVH), :].astype(BF16)


def pack_qg(q_ref, g_ref, out_ref):
    put_heads(q_ref, out_ref, 0)
    put_heads(g_ref, out_ref, PIECE)


def unpack_od(x_ref, out_ref, dq_ref):
    take_heads(x_ref, 0, out_ref)
    take_heads(x_ref, PIECE, dq_ref)


def unpack_kv(x_ref, k_ref, v_ref, wide):
    for at, ref in ((0, k_ref), (TOK, v_ref)):
        for j in range(KVH):
            wide[pl.ds(j, TOK, stride=KVH), :] = x_ref[j, at : at + TOK, :].astype(F32)
        ref[...] = wide[...].reshape(TOK, KVH, HD).astype(BF16)


def attend(core_ref, qg_ref, start_ref, own_ref, other_ref, old_ref, other_old_ref,
           od_ref, mine_ref, theirs_ref,
           keys, values, keys_t, values_t, scores, probs, dscores, dk, dv):
    core = core_ref[0]
    for column in range(REACH + 1):
        for piece in range(KVH):
            base = (REACH - column) * COL + piece * 2 * TOK
            for ref, old, which in ((own_ref, old_ref, core), (other_ref, other_old_ref, 1 - core)):
                at = pl.ds(pl.multiple_of(base + which * TOK, TOK), TOK)
                got = ref[piece] if column == 0 else old[column - 1, piece]
                keys[at, :] = got[0:TOK]
                values[at, :] = got[TOK : 2 * TOK]
    for t in range(KEYS // TILE):
        at = slice(t * TILE, (t + 1) * TILE)
        keys_t[:, at] = jnp.transpose(keys[at, :])
        values_t[:, at] = jnp.transpose(values[at, :])
    dk[...] = jnp.zeros(dk.shape, F32)
    dv[...] = jnp.zeros(dv.shape, F32)
    index = lax.broadcasted_iota(jnp.int32, (TILE, ROWS), 0)
    row = lax.broadcasted_iota(jnp.int32, (1, ROWS), 1)
    inside = (row // PIECE) * (2 * TOK) + core * TOK + (row % PIECE) // GROUP

    def one_block(block, _):
        base = pl.multiple_of(block * TILE, TILE)
        window = pl.ds(base, WIN * TILE)
        q = qg_ref[pl.ds(block * PAIR, PAIR), 0:PIECE, :].reshape(ROWS, HD)
        g = qg_ref[pl.ds(block * PAIR, PAIR), PIECE : 2 * PIECE, :].reshape(ROWS, HD)
        start = start_ref[block] - base
        top = jnp.full((8, ROWS), NEG, F32)
        for t in range(WIN):
            s = dot(keys[pl.ds(base + t * TILE, TILE), :], q, NT)
            seen = index >= start - t * TILE
            if t == WIN - 1:
                seen = seen & (index <= inside)
            s = jnp.where(seen, s, NEG)
            scores[t * TILE : (t + 1) * TILE, :] = s
            top = jnp.maximum(top, jnp.max(s.reshape(TILE // 8, 8, ROWS), axis=0))
        row_top = jnp.max(top, axis=0, keepdims=True) * SCALE2
        sums = jnp.zeros((8, ROWS), F32)
        for t in range(WIN):
            p = jnp.exp2(scores[t * TILE : (t + 1) * TILE, :] * SCALE2 - row_top)
            sums = sums + jnp.sum(p.reshape(TILE // 8, 8, ROWS), axis=0)
            probs[t * TILE : (t + 1) * TILE, :] = p.astype(BF16)
        inv = 1.0 / jnp.sum(sums, axis=0, keepdims=True)
        out = jnp.transpose(dot(values_t[:, window], probs[...], NN) * inv).astype(BF16)
        od_ref[pl.ds(block * PAIR, PAIR), 0:PIECE, :] = out.reshape(PAIR, PIECE, HD)
        scaled = g.astype(F32) * jnp.transpose(jnp.broadcast_to(inv, (8, ROWS)))[:, 0:1]
        prod = scaled * out.astype(F32)
        high = prod.astype(BF16)
        low = (prod - high.astype(F32)).astype(BF16)
        ones = jnp.ones((8, HD), BF16)
        drift = (dot(ones, high, NT) + dot(ones, low, NT))[0:1]
        scaled = scaled.astype(BF16)
        for t in range(WIN):
            at = slice(t * TILE, (t + 1) * TILE)
            dp = dot(values[pl.ds(base + t * TILE, TILE), :], scaled, NT)
            dscores[at, :] = (dp - drift).astype(BF16) * probs[at, :]
        dv[window, :] += dot(probs[...], scaled, NN)
        dk[window, :] += dot(dscores[...], q, NN)
        dq = jnp.transpose(dot(keys_t[:, window], dscores[...], NN) * SCALE).astype(BF16)
        od_ref[pl.ds(block * PAIR, PAIR), PIECE : 2 * PIECE, :] = dq.reshape(PAIR, PIECE, HD)
        return 0

    lax.fori_loop(0, BLOCKS, one_block, 0)
    for column in range(REACH + 1):
        for piece in range(KVH):
            base = (REACH - column) * COL + piece * 2 * TOK
            for ref, which in ((mine_ref, core), (theirs_ref, 1 - core)):
                at = pl.ds(pl.multiple_of(base + which * TOK, TOK), TOK)
                ref[column, piece, 0:TOK] = (dk[at, :] * SCALE).astype(ref.dtype)
                ref[column, piece, TOK : 2 * TOK] = dv[at, :].astype(ref.dtype)


def old_terms(mine_ref, got_ref, one_ref, two_ref):
    one_ref[...] = (mine_ref[1] + got_ref[1].astype(F32)).astype(BF16)
    two_ref[...] = (mine_ref[2] + got_ref[2].astype(F32)).astype(BF16)


def add_terms(mine_ref, got_ref, one_ref, two_ref, out_ref):
    out_ref[...] = (
        mine_ref[0] + got_ref[0].astype(F32) + one_ref[...].astype(F32) + two_ref[...].astype(F32)
    ).astype(BF16)


def exchange(x):
    return lax.all_to_all(x, RING, split_axis=0, concat_axis=0, tiled=True)


def shifted(x, by):
    count = SIZES[0] * SIZES[1]
    return lax.ppermute(x, COLUMNS, [(i, (i + by) % count) for i in range(count)])


def swapped(x):
    return lax.ppermute(x, "c", [(0, 1), (1, 0)])


def starts(doc_lengths, column, core):
    ends = jnp.cumsum(doc_lengths)
    row = jnp.arange(ROWS, dtype=jnp.int32)
    piece = jnp.arange(BLOCKS, dtype=jnp.int32)[:, None] * PAIR + (row // PIECE)[None, :]
    place = column * COL + piece * (2 * TOK) + core * TOK + ((row % PIECE) // GROUP)[None, :]
    start = jnp.max(jnp.where(ends[:, None, None] <= place[None], ends[:, None, None], 0), axis=0)
    return jnp.maximum(start - (column - REACH) * COL, 0).astype(jnp.int32)[:, None, :]


def shards(query_in, key_in, value_in, grad_out, doc_lengths):
    both_kv = shape(KVH, 2 * TOK, HD)
    both_wide = shape(KVH, 2 * PIECE, HD)
    heads_kv = shape(TOK, KVH, HD)
    heads_wide = shape(TOK, KVH * GROUP, HD)
    wide = [pltpu.VMEM((TOK * KVH, HD), F32)]

    kv = exchange(call(pack_kv, [both_kv], [VMEM] * 2, wide, "pack_kv")(key_in, value_in)[0])
    qg = exchange(call(pack_qg, [both_wide], [VMEM] * 2, [], "pack_qg")(query_in, grad_out)[0])
    other = swapped(kv)
    old = jnp.stack([shifted(kv, 1), shifted(kv, 2)])
    other_old = swapped(old)

    core = lax.axis_index("c").astype(jnp.int32)
    start = starts(doc_lengths, lax.axis_index(COLUMNS), core)
    od, mine, theirs = call(
        attend,
        [both_wide, shape(REACH + 1, KVH, 2 * TOK, HD, dtype=F32), shape(REACH + 1, KVH, 2 * TOK, HD)],
        [SMEM] + [VMEM] * 6,
        [pltpu.VMEM((KEYS, HD), BF16)] * 2
        + [pltpu.VMEM((HD, KEYS), BF16)] * 2
        + [pltpu.VMEM((WIN * TILE, ROWS), F32)]
        + [pltpu.VMEM((WIN * TILE, ROWS), BF16)] * 2
        + [pltpu.VMEM((KEYS, HD), F32)] * 2,
        "attend",
        12 * BLOCKS * ROWS * WIN * TILE * HD,
    )(core[None], qg, start, kv, other, old, other_old)

    od_back = exchange(od)
    got = swapped(theirs)
    one, two = call(old_terms, [both_kv] * 2, [VMEM] * 2, [], "old_terms")(mine, got)
    one, two = shifted(one, -1), shifted(two, -2)
    total = call(add_terms, [both_kv], [VMEM] * 4, [], "add_terms")(mine, got, one, two)[0]
    od_back, total = lax.optimization_barrier((od_back, total))
    grads_kv = exchange(total)
    attn_out, grad_query = call(unpack_od, [heads_wide] * 2, [VMEM], [], "unpack_od")(od_back)
    grad_key, grad_value = call(unpack_kv, [heads_kv] * 2, [VMEM], wide, "unpack_kv")(grads_kv)
    return (attn_out, grad_query, grad_key, grad_value)


def solution(mesh):
    fine = Mesh(mesh.devices.reshape(SIZES), AXES)
    tokens = P(AXES, None, None)
    return jax.shard_map(
        shards,
        mesh=fine,
        in_specs=(tokens, tokens, tokens, tokens, P()),
        out_specs=(tokens, tokens, tokens, tokens),
        check_vma=False,
    )
```

time: 135 us -> 107 us (0.79)
  the two profiles are of different devices: /device:TPU:76 before, /device:TPU:6 now
where the time goes in v2:
time: 107 us; the launch traced here: 106 us
  starting transfers between devices  46.8 us (44%)
  waiting for transfers between devices  35.9 us (34%)
  Pallas kernels  17.6 us (16%)
  local copies, waits for them, and re-layouts  4.5 us (4%)
    all_to_all x4, starting transfers between devices, exchange(): return lax.all_to_all(x, RING, split_axis=0, concat_axis=0, tiled=True)  22.9 us
    all_to_all x4, waiting for transfers between devices, exchange(): return lax.all_to_all(x, RING, split_axis=0, concat_axis=0, tiled=True)  21.3 us
    ppermute x4, starting transfers between devices, shifted(): lax.ppermute(x, COLUMNS, [(i, (i + by) % count) for i in range(count)])  17.7 us
    pallas_call x1, Pallas kernels, shards(): call(attend, [both_wide, shape(REACH + 1, KVH, 2 * TOK, HD, dtype=F32), s...  13.1 us
    ppermute x4, waiting for transfers between devices, shifted(): lax.ppermute(x, COLUMNS, [(i, (i + by) % count) for i in range(count)])  12 us
    ppermute x3, starting transfers between devices, swapped(): return lax.ppermute(x, 'c', [(0, 1), (1, 0)])  6.24 us
    unnamed x10, local copies, waits for them, and re-layouts  4.4 us
    ppermute x3, waiting for transfers between devices, swapped(): return lax.ppermute(x, 'c', [(0, 1), (1, 0)])  2.63 us
  transfers between devices with their start and end apart: 11, of which 9 were waited for; matrix products, arithmetic and copies ran while one was open for 0% of the time, Pallas kernels for 3%

profile of v2, /device:TPU:6, one launch (start us, length us, event | category | flops | bytes accessed | tf_op | source)
XLA Modules:
  0.0 106.0 jit_solution(9034625234747036387)
XLA Ops:
  0.6 0.8 copy-done.2
  1.5 0.8 copy-done.3
  2.3 0.7 pack_kv.1
  3.0 10.3 %all-to-all-start.1 = ((bf16[8,64,128]{2,1,0:T(8,128)(2,1)}), bf16[8,64,128]{2,1,0:T(8,128)(2,1)S(1)}, u32[]{:S(2)}, u32[]{:S(2)}) async-start(bf16[8,64,128]{2,1,0:T(8,128)(2,1)} %pack_kv.1), calls=%async_computation.1 | async-start | bytes 262144 | tf_op jit(solution)/shard_map/all_to_all | solution.py:189
  13.4 1.0 copy-done
  14.4 1.0 copy-done.1
  15.4 1.2 %pack_qg.1 = bf16[8,512,128]{2,1,0:T(8,128)(2,1)} custom-call(bf16[32,64,128]{2,1,0:T(8,128)(2,1)S(1)} %copy-done, bf16[32,64,128]{2,1,0:T(8,128)(2,1)S(1)} %copy-done.1), custom_call_target="tpu_custom_call" | custom-call | bytes 1048576 | tf_op jit(solution)/shard_map/pack_qg/pallas_call | solution.py:218
  16.6 4.6 %all-to-all-done.1.own_ref = bf16[8,64,128]{2,1,0:T(8,128)(2,1)S(1)} async-done(((bf16[8,64,128]{2,1,0:T(8,128)(2,1)}), bf16[8,64,128]{2,1,0:T(8,128)(2,1)S(1)}, u32[]{:S(2)}, u32[]{:S(2)}) %all-to-all-start.1) | async-done | bytes 131104 | tf_op jit(solution)/shard_map/all_to_all | solution.py:189
  21.2 3.6 %all-to-all-start = ((bf16[8,512,128]{2,1,0:T(8,128)(2,1)}), bf16[8,512,128]{2,1,0:T(8,128)(2,1)S(1)}, u32[]{:S(2)}, u32[]{:S(2)}) async-start(bf16[8,512,128]{2,1,0:T(8,128)(2,1)} %pack_qg.1), calls=%async_computation | async-start | bytes 2097152 | tf_op jit(solution)/shard_map/all_to_all | solution.py:189
  24.8 0.6 copy-done.4
  25.7 4.5 %collective-permute-start.2 = (bf16[8,64,128]{2,1,0:T(8,128)(2,1)S(1)}, bf16[8,64,128]{2,1,0:T(8,128)(2,1)S(1)}, u32[]{:S(2)}, u32[]{:S(2)}) collective-permute-start(bf16[8,64,128]{2,1,0:T(8,128)(2,1)S(1)} %all-to-all-done.1.own_ref), channel_id=1, source_target_pairs={{0,32},{16,48},{32,64},{48,80},{64,96},{80,112},{96,128},{112,144}... | collective-permute-start | bytes 393224 | tf_op jit(solution)/shard_map/ppermute | solution.py:194
  30.2 3.5 %collective-permute-start.1 = (bf16[8,64,128]{2,1,0:T(8,128)(2,1)S(1)}, bf16[8,64,128]{2,1,0:T(8,128)(2,1)S(1)}, u32[]{:S(2)}, u32[]{:S(2)}) collective-permute-start(bf16[8,64,128]{2,1,0:T(8,128)(2,1)S(1)} %all-to-all-done.1.own_ref), channel_id=1, source_target_pairs={{0,16},{16,32},{32,48},{48,64},{64,80},{80,96},{96,112},{112,128},... | collective-permute-start | bytes 393224 | tf_op jit(solution)/shard_map/ppermute | solution.py:194
  33.8 3.9 %collective-permute-done.2 = bf16[8,64,128]{2,1,0:T(8,128)(2,1)S(1)} collective-permute-done((bf16[8,64,128]{2,1,0:T(8,128)(2,1)S(1)}, bf16[8,64,128]{2,1,0:T(8,128)(2,1)S(1)}, u32[]{:S(2)}, u32[]{:S(2)}) %collective-permute-start.2) | collective-permute-done | bytes 131104 | tf_op jit(solution)/shard_map/ppermute | solution.py:194
  37.7 2.7 %collective-permute-done.1 = bf16[8,64,128]{2,1,0:T(8,128)(2,1)S(1)} collective-permute-done((bf16[8,64,128]{2,1,0:T(8,128)(2,1)S(1)}, bf16[8,64,128]{2,1,0:T(8,128)(2,1)S(1)}, u32[]{:S(2)}, u32[]{:S(2)}) %collective-permute-start.1) | collective-permute-done | bytes 131104 | tf_op jit(solution)/shard_map/ppermute | solution.py:194
  40.4 1.9 %collective-permute-start.3 = (bf16[2,8,64,128]{3,2,1,0:T(8,128)(2,1)S(1)}, bf16[2,8,64,128]{3,2,1,0:T(8,128)(2,1)S(1)}, u32[]{:S(2)}, u32[]{:S(2)}) collective-permute-start(bf16[2,8,64,128]{3,2,1,0:T(8,128)(2,1)S(1)} %pad_maximum_fusion.old_ref), channel_id=1, source_target_pairs={{0,1},{1,0},{2,3},{3,2},{4,5},{5,4},{6,7},{7,6},{8,9},{9,8},{10,11... | collective-permute-start | bytes 786440 | tf_op jit(solution)/shard_map/ppermute | solution.py:198
  42.3 0.1 select_reduce_fusion
  42.5 2.4 %collective-permute-start = (bf16[8,64,128]{2,1,0:T(8,128)(2,1)S(1)}, bf16[8,64,128]{2,1,0:T(8,128)(2,1)S(1)}, u32[]{:S(2)}, u32[]{:S(2)}) collective-permute-start(bf16[8,64,128]{2,1,0:T(8,128)(2,1)S(1)} %all-to-all-done.1.own_ref), channel_id=1, source_target_pairs={{0,1},{1,0},{2,3},{3,2},{4,5},{5,4},{6,7},{7,6},{8,9},{9,8},{10,11... | collective-permute-start | bytes 393224 | tf_op jit(solution)/shard_map/ppermute | solution.py:198
  44.9 0.9 collective-permute-done.other_ref
  45.9 4.1 %all-to-all-done.qg_ref = bf16[8,512,128]{2,1,0:T(8,128)(2,1)S(1)} async-done(((bf16[8,512,128]{2,1,0:T(8,128)(2,1)}), bf16[8,512,128]{2,1,0:T(8,128)(2,1)S(1)}, u32[]{:S(2)}, u32[]{:S(2)}) %all-to-all-start) | async-done | bytes 1048608 | tf_op jit(solution)/shard_map/all_to_all | solution.py:189
  49.9 13.1 %attend.1 = (bf16[8,512,128]{2,1,0:T(8,128)(2,1)}, f32[3,8,64,128]{3,2,1,0:T(8,128)S(1)}, bf16[3,8,64,128]{3,2,1,0:T(8,128)(2,1)S(1)}) custom-call(s32[1]{0:T(128)} %bitcast.core_ref, bf16[8,512,128]{2,1,0:T(8,128)(2,1)S(1)} %all-to-all-done.qg_ref, s32[4,1,512]{2,1,0:T(1,128)S(1)} %max.18.start_ref, bf16[8,64,128]{2,1,0:T(8,128)(2,1)S(1)} %all-to-all-done.1.own_ref, ...), custom_call_target="tpu_custom_call" | custom-call | flops 3623878656 | bytes 1048576 | tf_op jit(solution)/shard_map/attend/pallas_call | solution.py:225
  63.0 4.5 %all-to-all-start.2 = ((bf16[8,512,128]{2,1,0:T(8,128)(2,1)}), bf16[8,512,128]{2,1,0:T(8,128)(2,1)S(1)}, u32[]{:S(2)}, u32[]{:S(2)}) async-start(bf16[8,512,128]{2,1,0:T(8,128)(2,1)} %get-tuple-element.15), calls=%async_computation.2 | async-start | bytes 2097152 | tf_op jit(solution)/shard_map/all_to_all | solution.py:189
  67.5 1.9 %collective-permute-start.4 = (bf16[3,8,64,128]{3,2,1,0:T(8,128)(2,1)S(1)}, bf16[3,8,64,128]{3,2,1,0:T(8,128)(2,1)S(1)}, u32[]{:S(2)}, u32[]{:S(2)}) collective-permute-start(bf16[3,8,64,128]{3,2,1,0:T(8,128)(2,1)S(1)} %get-tuple-element.17), channel_id=1, source_target_pairs={{0,1},{1,0},{2,3},{3,2},{4,5},{5,4},{6,7},{7,6},{8,9},{9,8},{10,11... | collective-permute-start | bytes 1179656 | tf_op jit(solution)/shard_map/ppermute | solution.py:198
  69.4 1.7 %collective-permute-done.4.got_ref = bf16[3,8,64,128]{3,2,1,0:T(8,128)(2,1)S(1)} collective-permute-done((bf16[3,8,64,128]{3,2,1,0:T(8,128)(2,1)S(1)}, bf16[3,8,64,128]{3,2,1,0:T(8,128)(2,1)S(1)}, u32[]{:S(2)}, u32[]{:S(2)}) %collective-permute-start.4) | collective-permute-done | bytes 393248 | tf_op jit(solution)/shard_map/ppermute | solution.py:198
  71.2 5.6 %collective-permute-start.5 = (bf16[8,64,128]{2,1,0:T(8,128)(2,1)S(1)}, bf16[8,64,128]{2,1,0:T(8,128)(2,1)S(1)}, u32[]{:S(2)}, u32[]{:S(2)}) collective-permute-start(bf16[8,64,128]{2,1,0:T(8,128)(2,1)S(1)} %get-tuple-element.18), channel_id=1, source_target_pairs={{0,496},{16,0},{32,16},{48,32},{64,48},{80,64},{96,80},{112,96},{1... | collective-permute-start | bytes 393224 | tf_op jit(solution)/shard_map/ppermute | solution.py:194
  76.8 4.1 %collective-permute-start.6 = (bf16[8,64,128]{2,1,0:T(8,128)(2,1)S(1)}, bf16[8,64,128]{2,1,0:T(8,128)(2,1)S(1)}, u32[]{:S(2)}, u32[]{:S(2)}) collective-permute-start(bf16[8,64,128]{2,1,0:T(8,128)(2,1)S(1)} %get-tuple-element.19), channel_id=1, source_target_pairs={{0,480},{16,496},{32,0},{48,16},{64,32},{80,48},{96,64},{112,80},{... | collective-permute-start | bytes 393224 | tf_op jit(solution)/shard_map/ppermute | solution.py:194
  80.9 5.4 %collective-permute-done.6.two_ref = bf16[8,64,128]{2,1,0:T(8,128)(2,1)S(1)} collective-permute-done((bf16[8,64,128]{2,1,0:T(8,128)(2,1)S(1)}, bf16[8,64,128]{2,1,0:T(8,128)(2,1)S(1)}, u32[]{:S(2)}, u32[]{:S(2)}) %collective-permute-start.6) | collective-permute-done | bytes 131104 | tf_op jit(solution)/shard_map/ppermute | solution.py:194
  86.2 0.7 add_terms.1
  87.0 5.8 %all-to-all-done.2.x_ref = bf16[8,512,128]{2,1,0:T(8,128)(2,1)S(1)} async-done(((bf16[8,512,128]{2,1,0:T(8,128)(2,1)}), bf16[8,512,128]{2,1,0:T(8,128)(2,1)S(1)}, u32[]{:S(2)}, u32[]{:S(2)}) %all-to-all-start.2) | async-done | bytes 1048608 | tf_op jit(solution)/shard_map/all_to_all | solution.py:189
  92.8 4.5 %all-to-all-start.3 = ((bf16[8,64,128]{2,1,0:T(8,128)(2,1)}), bf16[8,64,128]{2,1,0:T(8,128)(2,1)S(1)}, u32[]{:S(2)}, u32[]{:S(2)}) async-start(bf16[8,64,128]{2,1,0:T(8,128)(2,1)} %add_terms.1), calls=%async_computation.3 | async-start | bytes 262144 | tf_op jit(solution)/shard_map/all_to_all | solution.py:189
  97.3 1.1 %unpack_od.1 = (bf16[32,64,128]{2,1,0:T(8,128)(2,1)}, bf16[32,64,128]{2,1,0:T(8,128)(2,1)}) custom-call(bf16[8,512,128]{2,1,0:T(8,128)(2,1)S(1)} %all-to-all-done.2.x_ref), custom_call_target="tpu_custom_call" | custom-call | bytes 1048576 | tf_op jit(solution)/shard_map/unpack_od/pallas_call | solution.py:245
  98.5 6.8 %all-to-all-done.3.x_ref = bf16[8,64,128]{2,1,0:T(8,128)(2,1)S(1)} async-done(((bf16[8,64,128]{2,1,0:T(8,128)(2,1)}), bf16[8,64,128]{2,1,0:T(8,128)(2,1)S(1)}, u32[]{:S(2)}, u32[]{:S(2)}) %all-to-all-start.3) | async-done | bytes 131104 | tf_op jit(solution)/shard_map/all_to_all | solution.py:189
  105.3 0.7 unpack_kv.1
  (17 shorter events, 0.5 us)
Async XLA Ops:
  0.6 0.8 copy-start.2
  1.5 0.8 copy-start.3
  3.0 18.2 %all-to-all-start.1 = ((bf16[8,64,128]{2,1,0:T(8,128)(2,1)}), bf16[8,64,128]{2,1,0:T(8,128)(2,1)S(1)}, u32[]{:S(2)}, u32[]{:S(2)}) async-start(bf16[8,64,128]{2,1,0:T(8,128)(2,1)} %pack_kv.1), calls=%async_computation.1 | async-start | bytes 262144 | tf_op jit(solution)/shard_map/all_to_all | solution.py:189
  13.3 1.0 copy-start
  14.4 1.0 copy-start.1
  21.2 28.7 %all-to-all-start = ((bf16[8,512,128]{2,1,0:T(8,128)(2,1)}), bf16[8,512,128]{2,1,0:T(8,128)(2,1)S(1)}, u32[]{:S(2)}, u32[]{:S(2)}) async-start(bf16[8,512,128]{2,1,0:T(8,128)(2,1)} %pack_qg.1), calls=%async_computation | async-start | bytes 2097152 | tf_op jit(solution)/shard_map/all_to_all | solution.py:189
  24.8 0.7 copy-start.4
  25.7 11.9 %collective-permute-start.2 = (bf16[8,64,128]{2,1,0:T(8,128)(2,1)S(1)}, bf16[8,64,128]{2,1,0:T(8,128)(2,1)S(1)}, u32[]{:S(2)}, u32[]{:S(2)}) collective-permute-start(bf16[8,64,128]{2,1,0:T(8,128)(2,1)S(1)} %all-to-all-done.1.own_ref), channel_id=1, source_target_pairs={{0,32},{16,48},{32,64},{48,80},{64,96},{80,112},{96,128},{112,144}... | collective-permute-start | bytes 393224 | tf_op jit(solution)/shard_map/ppermute | solution.py:194
  30.2 10.2 %collective-permute-start.1 = (bf16[8,64,128]{2,1,0:T(8,128)(2,1)S(1)}, bf16[8,64,128]{2,1,0:T(8,128)(2,1)S(1)}, u32[]{:S(2)}, u32[]{:S(2)}) collective-permute-start(bf16[8,64,128]{2,1,0:T(8,128)(2,1)S(1)} %all-to-all-done.1.own_ref), channel_id=1, source_target_pairs={{0,16},{16,32},{32,48},{48,64},{64,80},{80,96},{96,112},{112,128},... | collective-permute-start | bytes 393224 | tf_op jit(solution)/shard_map/ppermute | solution.py:194
  40.4 5.4 %collective-permute-start.3 = (bf16[2,8,64,128]{3,2,1,0:T(8,128)(2,1)S(1)}, bf16[2,8,64,128]{3,2,1,0:T(8,128)(2,1)S(1)}, u32[]{:S(2)}, u32[]{:S(2)}) collective-permute-start(bf16[2,8,64,128]{3,2,1,0:T(8,128)(2,1)S(1)} %pad_maximum_fusion.old_ref), channel_id=1, source_target_pairs={{0,1},{1,0},{2,3},{3,2},{4,5},{5,4},{6,7},{7,6},{8,9},{9,8},{10,11... | collective-permute-start | bytes 786440 | tf_op jit(solution)/shard_map/ppermute | solution.py:198
  42.5 3.4 %collective-permute-start = (bf16[8,64,128]{2,1,0:T(8,128)(2,1)S(1)}, bf16[8,64,128]{2,1,0:T(8,128)(2,1)S(1)}, u32[]{:S(2)}, u32[]{:S(2)}) collective-permute-start(bf16[8,64,128]{2,1,0:T(8,128)(2,1)S(1)} %all-to-all-done.1.own_ref), channel_id=1, source_target_pairs={{0,1},{1,0},{2,3},{3,2},{4,5},{5,4},{6,7},{7,6},{8,9},{9,8},{10,11... | collective-permute-start | bytes 393224 | tf_op jit(solution)/shard_map/ppermute | solution.py:198
  63.0 29.8 %all-to-all-start.2 = ((bf16[8,512,128]{2,1,0:T(8,128)(2,1)}), bf16[8,512,128]{2,1,0:T(8,128)(2,1)S(1)}, u32[]{:S(2)}, u32[]{:S(2)}) async-start(bf16[8,512,128]{2,1,0:T(8,128)(2,1)} %get-tuple-element.15), calls=%async_computation.2 | async-start | bytes 2097152 | tf_op jit(solution)/shard_map/all_to_all | solution.py:189
  67.5 3.6 %collective-permute-start.4 = (bf16[3,8,64,128]{3,2,1,0:T(8,128)(2,1)S(1)}, bf16[3,8,64,128]{3,2,1,0:T(8,128)(2,1)S(1)}, u32[]{:S(2)}, u32[]{:S(2)}) collective-permute-start(bf16[3,8,64,128]{3,2,1,0:T(8,128)(2,1)S(1)} %get-tuple-element.17), channel_id=1, source_target_pairs={{0,1},{1,0},{2,3},{3,2},{4,5},{5,4},{6,7},{7,6},{8,9},{9,8},{10,11... | collective-permute-start | bytes 1179656 | tf_op jit(solution)/shard_map/ppermute | solution.py:198
  71.2 9.7 %collective-permute-start.5 = (bf16[8,64,128]{2,1,0:T(8,128)(2,1)S(1)}, bf16[8,64,128]{2,1,0:T(8,128)(2,1)S(1)}, u32[]{:S(2)}, u32[]{:S(2)}) collective-permute-start(bf16[8,64,128]{2,1,0:T(8,128)(2,1)S(1)} %get-tuple-element.18), channel_id=1, source_target_pairs={{0,496},{16,0},{32,16},{48,32},{64,48},{80,64},{96,80},{112,96},{1... | collective-permute-start | bytes 393224 | tf_op jit(solution)/shard_map/ppermute | solution.py:194
  76.8 9.4 %collective-permute-start.6 = (bf16[8,64,128]{2,1,0:T(8,128)(2,1)S(1)}, bf16[8,64,128]{2,1,0:T(8,128)(2,1)S(1)}, u32[]{:S(2)}, u32[]{:S(2)}) collective-permute-start(bf16[8,64,128]{2,1,0:T(8,128)(2,1)S(1)} %get-tuple-element.19), channel_id=1, source_target_pairs={{0,480},{16,496},{32,0},{48,16},{64,32},{80,48},{96,64},{112,80},{... | collective-permute-start | bytes 393224 | tf_op jit(solution)/shard_map/ppermute | solution.py:194
  92.8 12.5 %all-to-all-start.3 = ((bf16[8,64,128]{2,1,0:T(8,128)(2,1)}), bf16[8,64,128]{2,1,0:T(8,128)(2,1)S(1)}, u32[]{:S(2)}, u32[]{:S(2)}) async-start(bf16[8,64,128]{2,1,0:T(8,128)(2,1)} %add_terms.1), calls=%async_computation.3 | async-start | bytes 262144 | tf_op jit(solution)/shard_map/all_to_all | solution.py:189

commit v3 on v2

--- a/solution.py
+++ b/solution.py
@@ -123,48 +123,84 @@
     row = lax.broadcasted_iota(jnp.int32, (1, ROWS), 1)
     inside = (row // PIECE) * (2 * TOK) + core * TOK + (row % PIECE) // GROUP
 
-    def one_block(block, _):
-        base = pl.multiple_of(block * TILE, TILE)
-        window = pl.ds(base, WIN * TILE)
-        q = qg_ref[pl.ds(block * PAIR, PAIR), 0:PIECE, :].reshape(ROWS, HD)
-        g = qg_ref[pl.ds(block * PAIR, PAIR), PIECE : 2 * PIECE, :].reshape(ROWS, HD)
-        start = start_ref[block] - base
-        top = jnp.full((8, ROWS), NEG, F32)
-        for t in range(WIN):
-            s = dot(keys[pl.ds(base + t * TILE, TILE), :], q, NT)
-            seen = index >= start - t * TILE
+    tiles = [slice(t * TILE, (t + 1) * TILE) for t in range(WIN)]
+
+    class Block:
+        def __init__(self, at):
+            self.slot = at % 2
+            self.base = at * TILE
+            self.window = slice(self.base, self.base + WIN * TILE)
+            self.pieces = slice(at * PAIR, (at + 1) * PAIR)
+            self.q = qg_ref[self.pieces, 0:PIECE, :].reshape(ROWS, HD)
+            self.g = qg_ref[self.pieces, PIECE : 2 * PIECE, :].reshape(ROWS, HD)
+            self.g_t = jnp.transpose(self.g.astype(F32))
+            self.start = start_ref[at] - self.base
+            self.top = jnp.full((8, ROWS), NEG, F32)
+            self.sums = jnp.zeros((8, ROWS), F32)
+
+        def keys_of(self, t):
+            return slice(self.base + t * TILE, self.base + (t + 1) * TILE)
+
+        def score(self, t):
+            s = dot(keys[self.keys_of(t), :], self.q, NT)
+            seen = index >= self.start - t * TILE
             if t == WIN - 1:
                 seen = seen & (index <= inside)
             s = jnp.where(seen, s, NEG)
-            scores[t * TILE : (t + 1) * TILE, :] = s
-            top = jnp.maximum(top, jnp.max(s.reshape(TILE // 8, 8, ROWS), axis=0))
-        row_top = jnp.max(top, axis=0, keepdims=True) * SCALE2
-        sums = jnp.zeros((8, ROWS), F32)
+            scores[tiles[t], :] = s
+            self.top = jnp.maximum(self.top, jnp.max(s.reshape(TILE // 8, 8, ROWS), axis=0))
+
+        def find_top(self):
+            self.row_top = jnp.max(self.top, axis=0, keepdims=True) * SCALE2
+
+        def weigh(self, t):
+            p = jnp.exp2(scores[tiles[t], :] * SCALE2 - self.row_top)
+            self.sums = self.sums + jnp.sum(p.reshape(TILE // 8, 8, ROWS), axis=0)
+            probs[self.slot, tiles[t], :] = p.astype(BF16)
+
+        def output(self):
+            self.inv = 1.0 / jnp.sum(self.sums, axis=0, keepdims=True)
+            out = dot(values_t[:, self.window], probs[self.slot], NN) * self.inv
+            self.drift = jnp.sum(out * self.g_t, axis=0, keepdims=True)
+            od_ref[self.pieces, 0:PIECE, :] = jnp.transpose(out).astype(BF16).reshape(PAIR, PIECE, HD)
+            inv = jnp.transpose(jnp.broadcast_to(self.inv, (8, ROWS)))[:, 0:1]
+            self.g_scaled = (self.g.astype(F32) * inv).astype(BF16)
+            self.q_scaled = (self.q.astype(F32) * inv).astype(BF16)
+
+        def dscore(self, t):
+            dp = dot(values[self.keys_of(t), :], self.g, NT)
+            dscores[self.slot, tiles[t], :] = (dp - self.drift).astype(BF16) * probs[self.slot, tiles[t], :]
+
+        def key_terms(self, t):
+            at = self.keys_of(t)
+            dv[at, :] += dot(probs[self.slot, tiles[t], :], self.g_scaled, NN)
+            dk[at, :] += dot(dscores[self.slot, tiles[t], :], self.q_scaled, NN)
+
+        def dquery(self):
+            dq = dot(keys_t[:, self.window], dscores[self.slot], NN) * (self.inv * SCALE)
+            od_ref[self.pieces, PIECE : 2 * PIECE, :] = jnp.transpose(dq).astype(BF16).reshape(PAIR, PIECE, HD)
+
+    last = None
+    for at in range(BLOCKS + 1):
+        block = Block(at) if at < BLOCKS else None
         for t in range(WIN):
-            p = jnp.exp2(scores[t * TILE : (t + 1) * TILE, :] * SCALE2 - row_top)
-            sums = sums + jnp.sum(p.reshape(TILE // 8, 8, ROWS), axis=0)
-            probs[t * TILE : (t + 1) * TILE, :] = p.astype(BF16)
-        inv = 1.0 / jnp.sum(sums, axis=0, keepdims=True)
-        out = jnp.transpose(dot(values_t[:, window], probs[...], NN) * inv).astype(BF16)
-        od_ref[pl.ds(block * PAIR, PAIR), 0:PIECE, :] = out.reshape(PAIR, PIECE, HD)
-        scaled = g.astype(F32) * jnp.transpose(jnp.broadcast_to(inv, (8, ROWS)))[:, 0:1]
-        prod = scaled * out.astype(F32)
-        high = prod.astype(BF16)
-        low = (prod - high.astype(F32)).astype(BF16)
-        ones = jnp.ones((8, HD), BF16)
-        drift = (dot(ones, high, NT) + dot(ones, low, NT))[0:1]
-        scaled = scaled.astype(BF16)
+            if block:
+                block.score(t)
+            if last:
+                last.dscore(t)
+        if block:
+            block.find_top()
         for t in range(WIN):
-            at = slice(t * TILE, (t + 1) * TILE)
-            dp = dot(values[pl.ds(base + t * TILE, TILE), :], scaled, NT)
-            dscores[at, :] = (dp - drift).astype(BF16) * probs[at, :]
-        dv[window, :] += dot(probs[...], scaled, NN)
-        dk[window, :] += dot(dscores[...], q, NN)
-        dq = jnp.transpose(dot(keys_t[:, window], dscores[...], NN) * SCALE).astype(BF16)
-        od_ref[pl.ds(block * PAIR, PAIR), PIECE : 2 * PIECE, :] = dq.reshape(PAIR, PIECE, HD)
-        return 0
-
-    lax.fori_loop(0, BLOCKS, one_block, 0)
+            if block:
+                block.weigh(t)
+            if last:
+                last.key_terms(t)
+        if last:
+            last.dquery()
+        if block:
+            block.output()
+        last = block
+
     for column in range(REACH + 1):
         for piece in range(KVH):
             base = (REACH - column) * COL + piece * 2 * TOK
@@ -229,7 +265,7 @@
         [pltpu.VMEM((KEYS, HD), BF16)] * 2
         + [pltpu.VMEM((HD, KEYS), BF16)] * 2
         + [pltpu.VMEM((WIN * TILE, ROWS), F32)]
-        + [pltpu.VMEM((WIN * TILE, ROWS), BF16)] * 2
+        + [pltpu.VMEM((2, WIN * TILE, ROWS), BF16)] * 2
         + [pltpu.VMEM((KEYS, HD), F32)] * 2,
         "attend",
         12 * BLOCKS * ROWS * WIN * TILE * HD,

time: 107 us -> 104 us (0.972)
  Pallas kernels: 17.6 us -> 14.1 us
    pallas_call x1, Pallas kernels: 13.1 us -> 9.6 us  [shards(): call(attend, [both_wide, shape(REACH + 1, KVH, 2 * TOK, HD, dtype=F32), s...]
  transfers between devices with their start and end apart: 11 -> 11, of which waited for: 9 -> 9; matrix products, arithmetic and copies ran while one was open for 0% -> 1% of each run, Pallas kernels for 3% -> 3%
where the time goes in v3:
time: 104 us; the launch traced here: 103 us
  starting transfers between devices  46.8 us (45%)
  waiting for transfers between devices  35.9 us (35%)
  Pallas kernels  14.1 us (14%)
  local copies, waits for them, and re-layouts  4.5 us (4%)
    all_to_all x4, starting transfers between devices, exchange(): return lax.all_to_all(x, RING, split_axis=0, concat_axis=0, tiled=True)  22.9 us
    all_to_all x4, waiting for transfers between devices, exchange(): return lax.all_to_all(x, RING, split_axis=0, concat_axis=0, tiled=True)  21.3 us
    ppermute x4, starting transfers between devices, shifted(): lax.ppermute(x, COLUMNS, [(i, (i + by) % count) for i in range(count)])  17.7 us
    ppermute x4, waiting for transfers between devices, shifted(): lax.ppermute(x, COLUMNS, [(i, (i + by) % count) for i in range(count)])  12 us
    pallas_call x1, Pallas kernels, shards(): call(attend, [both_wide, shape(REACH + 1, KVH, 2 * TOK, HD, dtype=F32), s...  9.6 us
    ppermute x3, starting transfers between devices, swapped(): return lax.ppermute(x, 'c', [(0, 1), (1, 0)])  6.24 us
    unnamed x10, local copies, waits for them, and re-layouts  4.4 us
    ppermute x3, waiting for transfers between devices, swapped(): return lax.ppermute(x, 'c', [(0, 1), (1, 0)])  2.63 us
  transfers between devices with their start and end apart: 11, of which 9 were waited for; matrix products, arithmetic and copies ran while one was open for 1% of the time, Pallas kernels for 3%

profile of v3, /device:TPU:6, one launch (start us, length us, event | category | flops | bytes accessed | tf_op | source)
XLA Modules:
  0.0 102.5 jit_solution(6079791615968223226)
XLA Ops:
  0.6 0.8 copy-done.2
  1.5 0.8 copy-done.3
  2.3 0.7 pack_kv.1
  3.0 10.3 %all-to-all-start.1 = ((bf16[8,64,128]{2,1,0:T(8,128)(2,1)}), bf16[8,64,128]{2,1,0:T(8,128)(2,1)S(1)}, u32[]{:S(2)}, u32[]{:S(2)}) async-start(bf16[8,64,128]{2,1,0:T(8,128)(2,1)} %pack_kv.1), calls=%async_computation.1 | async-start | bytes 262144 | tf_op jit(solution)/shard_map/all_to_all | solution.py:225
  13.4 1.0 %copy-done = bf16[32,64,128]{2,1,0:T(8,128)(2,1)S(1)} copy-done((bf16[32,64,128]{2,1,0:T(8,128)(2,1)S(1)}, bf16[32,64,128]{2,1,0:T(8,128)(2,1)}, u32[]{:S(2)}) %copy-start) | copy-done | bytes 524312
  14.4 1.0 %copy-done.1 = bf16[32,64,128]{2,1,0:T(8,128)(2,1)S(1)} copy-done((bf16[32,64,128]{2,1,0:T(8,128)(2,1)S(1)}, bf16[32,64,128]{2,1,0:T(8,128)(2,1)}, u32[]{:S(2)}) %copy-start.1) | copy-done | bytes 524312
  15.4 1.2 %pack_qg.1 = bf16[8,512,128]{2,1,0:T(8,128)(2,1)} custom-call(bf16[32,64,128]{2,1,0:T(8,128)(2,1)S(1)} %copy-done, bf16[32,64,128]{2,1,0:T(8,128)(2,1)S(1)} %copy-done.1), custom_call_target="tpu_custom_call" | custom-call | bytes 1048576 | tf_op jit(solution)/shard_map/pack_qg/pallas_call | solution.py:254
  16.6 4.6 %all-to-all-done.1.own_ref = bf16[8,64,128]{2,1,0:T(8,128)(2,1)S(1)} async-done(((bf16[8,64,128]{2,1,0:T(8,128)(2,1)}), bf16[8,64,128]{2,1,0:T(8,128)(2,1)S(1)}, u32[]{:S(2)}, u32[]{:S(2)}) %all-to-all-start.1) | async-done | bytes 131104 | tf_op jit(solution)/shard_map/all_to_all | solution.py:225
  21.2 3.6 %all-to-all-start = ((bf16[8,512,128]{2,1,0:T(8,128)(2,1)}), bf16[8,512,128]{2,1,0:T(8,128)(2,1)S(1)}, u32[]{:S(2)}, u32[]{:S(2)}) async-start(bf16[8,512,128]{2,1,0:T(8,128)(2,1)} %pack_qg.1), calls=%async_computation | async-start | bytes 2097152 | tf_op jit(solution)/shard_map/all_to_all | solution.py:225
  24.8 0.6 copy-done.4
  25.7 4.5 %collective-permute-start.2 = (bf16[8,64,128]{2,1,0:T(8,128)(2,1)S(1)}, bf16[8,64,128]{2,1,0:T(8,128)(2,1)S(1)}, u32[]{:S(2)}, u32[]{:S(2)}) collective-permute-start(bf16[8,64,128]{2,1,0:T(8,128)(2,1)S(1)} %all-to-all-done.1.own_ref), channel_id=1, source_target_pairs={{0,32},{16,48},{32,64},{48,80},{64,96},{80,112},{96,128},{112,144}... | collective-permute-start | bytes 393224 | tf_op jit(solution)/shard_map/ppermute | solution.py:230
  30.2 3.5 %collective-permute-start.1 = (bf16[8,64,128]{2,1,0:T(8,128)(2,1)S(1)}, bf16[8,64,128]{2,1,0:T(8,128)(2,1)S(1)}, u32[]{:S(2)}, u32[]{:S(2)}) collective-permute-start(bf16[8,64,128]{2,1,0:T(8,128)(2,1)S(1)} %all-to-all-done.1.own_ref), channel_id=1, source_target_pairs={{0,16},{16,32},{32,48},{48,64},{64,80},{80,96},{96,112},{112,128},... | collective-permute-start | bytes 393224 | tf_op jit(solution)/shard_map/ppermute | solution.py:230
  33.8 3.9 %collective-permute-done.2 = bf16[8,64,128]{2,1,0:T(8,128)(2,1)S(1)} collective-permute-done((bf16[8,64,128]{2,1,0:T(8,128)(2,1)S(1)}, bf16[8,64,128]{2,1,0:T(8,128)(2,1)S(1)}, u32[]{:S(2)}, u32[]{:S(2)}) %collective-permute-start.2) | collective-permute-done | bytes 131104 | tf_op jit(solution)/shard_map/ppermute | solution.py:230
  37.7 2.7 %collective-permute-done.1 = bf16[8,64,128]{2,1,0:T(8,128)(2,1)S(1)} collective-permute-done((bf16[8,64,128]{2,1,0:T(8,128)(2,1)S(1)}, bf16[8,64,128]{2,1,0:T(8,128)(2,1)S(1)}, u32[]{:S(2)}, u32[]{:S(2)}) %collective-permute-start.1) | collective-permute-done | bytes 131104 | tf_op jit(solution)/shard_map/ppermute | solution.py:230
  40.4 1.9 %collective-permute-start.3 = (bf16[2,8,64,128]{3,2,1,0:T(8,128)(2,1)S(1)}, bf16[2,8,64,128]{3,2,1,0:T(8,128)(2,1)S(1)}, u32[]{:S(2)}, u32[]{:S(2)}) collective-permute-start(bf16[2,8,64,128]{3,2,1,0:T(8,128)(2,1)S(1)} %pad_maximum_fusion.old_ref), channel_id=1, source_target_pairs={{0,1},{1,0},{2,3},{3,2},{4,5},{5,4},{6,7},{7,6},{8,9},{9,8},{10,11... | collective-permute-start | bytes 786440 | tf_op jit(solution)/shard_map/ppermute | solution.py:234
  42.3 0.1 select_reduce_fusion
  42.5 2.4 %collective-permute-start = (bf16[8,64,128]{2,1,0:T(8,128)(2,1)S(1)}, bf16[8,64,128]{2,1,0:T(8,128)(2,1)S(1)}, u32[]{:S(2)}, u32[]{:S(2)}) collective-permute-start(bf16[8,64,128]{2,1,0:T(8,128)(2,1)S(1)} %all-to-all-done.1.own_ref), channel_id=1, source_target_pairs={{0,1},{1,0},{2,3},{3,2},{4,5},{5,4},{6,7},{7,6},{8,9},{9,8},{10,11... | collective-permute-start | bytes 393224 | tf_op jit(solution)/shard_map/ppermute | solution.py:234
  44.9 0.9 collective-permute-done.other_ref
  45.9 4.1 %all-to-all-done.qg_ref = bf16[8,512,128]{2,1,0:T(8,128)(2,1)S(1)} async-done(((bf16[8,512,128]{2,1,0:T(8,128)(2,1)}), bf16[8,512,128]{2,1,0:T(8,128)(2,1)S(1)}, u32[]{:S(2)}, u32[]{:S(2)}) %all-to-all-start) | async-done | bytes 1048608 | tf_op jit(solution)/shard_map/all_to_all | solution.py:225
  49.9 9.6 %attend.1 = (bf16[8,512,128]{2,1,0:T(8,128)(2,1)}, f32[3,8,64,128]{3,2,1,0:T(8,128)S(1)}, bf16[3,8,64,128]{3,2,1,0:T(8,128)(2,1)S(1)}) custom-call(s32[1]{0:T(128)} %bitcast.core_ref, bf16[8,512,128]{2,1,0:T(8,128)(2,1)S(1)} %all-to-all-done.qg_ref, s32[4,1,512]{2,1,0:T(1,128)S(1)} %max.18.start_ref, bf16[8,64,128]{2,1,0:T(8,128)(2,1)S(1)} %all-to-all-done.1.own_ref, ...), custom_call_target="tpu_custom_call" | custom-call | flops 3623878656 | bytes 1048576 | tf_op jit(solution)/shard_map/attend/pallas_call | solution.py:261
  59.5 4.5 %all-to-all-start.2 = ((bf16[8,512,128]{2,1,0:T(8,128)(2,1)}), bf16[8,512,128]{2,1,0:T(8,128)(2,1)S(1)}, u32[]{:S(2)}, u32[]{:S(2)}) async-start(bf16[8,512,128]{2,1,0:T(8,128)(2,1)} %get-tuple-element.15), calls=%async_computation.2 | async-start | bytes 2097152 | tf_op jit(solution)/shard_map/all_to_all | solution.py:225
  64.0 1.9 %collective-permute-start.4 = (bf16[3,8,64,128]{3,2,1,0:T(8,128)(2,1)S(1)}, bf16[3,8,64,128]{3,2,1,0:T(8,128)(2,1)S(1)}, u32[]{:S(2)}, u32[]{:S(2)}) collective-permute-start(bf16[3,8,64,128]{3,2,1,0:T(8,128)(2,1)S(1)} %get-tuple-element.17), channel_id=1, source_target_pairs={{0,1},{1,0},{2,3},{3,2},{4,5},{5,4},{6,7},{7,6},{8,9},{9,8},{10,11... | collective-permute-start | bytes 1179656 | tf_op jit(solution)/shard_map/ppermute | solution.py:234
  66.0 1.7 %collective-permute-done.4.got_ref = bf16[3,8,64,128]{3,2,1,0:T(8,128)(2,1)S(1)} collective-permute-done((bf16[3,8,64,128]{3,2,1,0:T(8,128)(2,1)S(1)}, bf16[3,8,64,128]{3,2,1,0:T(8,128)(2,1)S(1)}, u32[]{:S(2)}, u32[]{:S(2)}) %collective-permute-start.4) | collective-permute-done | bytes 393248 | tf_op jit(solution)/shard_map/ppermute | solution.py:234
  67.7 5.6 %collective-permute-start.5 = (bf16[8,64,128]{2,1,0:T(8,128)(2,1)S(1)}, bf16[8,64,128]{2,1,0:T(8,128)(2,1)S(1)}, u32[]{:S(2)}, u32[]{:S(2)}) collective-permute-start(bf16[8,64,128]{2,1,0:T(8,128)(2,1)S(1)} %get-tuple-element.18), channel_id=1, source_target_pairs={{0,496},{16,0},{32,16},{48,32},{64,48},{80,64},{96,80},{112,96},{1... | collective-permute-start | bytes 393224 | tf_op jit(solution)/shard_map/ppermute | solution.py:230
  73.3 4.0 %collective-permute-start.6 = (bf16[8,64,128]{2,1,0:T(8,128)(2,1)S(1)}, bf16[8,64,128]{2,1,0:T(8,128)(2,1)S(1)}, u32[]{:S(2)}, u32[]{:S(2)}) collective-permute-start(bf16[8,64,128]{2,1,0:T(8,128)(2,1)S(1)} %get-tuple-element.19), channel_id=1, source_target_pairs={{0,480},{16,496},{32,0},{48,16},{64,32},{80,48},{96,64},{112,80},{... | collective-permute-start | bytes 393224 | tf_op jit(solution)/shard_map/ppermute | solution.py:230
  77.4 5.4 %collective-permute-done.6.two_ref = bf16[8,64,128]{2,1,0:T(8,128)(2,1)S(1)} collective-permute-done((bf16[8,64,128]{2,1,0:T(8,128)(2,1)S(1)}, bf16[8,64,128]{2,1,0:T(8,128)(2,1)S(1)}, u32[]{:S(2)}, u32[]{:S(2)}) %collective-permute-start.6) | collective-permute-done | bytes 131104 | tf_op jit(solution)/shard_map/ppermute | solution.py:230
  82.8 0.7 add_terms.1
  83.5 5.8 %all-to-all-done.2.x_ref = bf16[8,512,128]{2,1,0:T(8,128)(2,1)S(1)} async-done(((bf16[8,512,128]{2,1,0:T(8,128)(2,1)}), bf16[8,512,128]{2,1,0:T(8,128)(2,1)S(1)}, u32[]{:S(2)}, u32[]{:S(2)}) %all-to-all-start.2) | async-done | bytes 1048608 | tf_op jit(solution)/shard_map/all_to_all | solution.py:225
  89.3 4.5 %all-to-all-start.3 = ((bf16[8,64,128]{2,1,0:T(8,128)(2,1)}), bf16[8,64,128]{2,1,0:T(8,128)(2,1)S(1)}, u32[]{:S(2)}, u32[]{:S(2)}) async-start(bf16[8,64,128]{2,1,0:T(8,128)(2,1)} %add_terms.1), calls=%async_computation.3 | async-start | bytes 262144 | tf_op jit(solution)/shard_map/all_to_all | solution.py:225
  93.9 1.1 %unpack_od.1 = (bf16[32,64,128]{2,1,0:T(8,128)(2,1)}, bf16[32,64,128]{2,1,0:T(8,128)(2,1)}) custom-call(bf16[8,512,128]{2,1,0:T(8,128)(2,1)S(1)} %all-to-all-done.2.x_ref), custom_call_target="tpu_custom_call" | custom-call | bytes 1048576 | tf_op jit(solution)/shard_map/unpack_od/pallas_call | solution.py:281
  95.0 6.8 %all-to-all-done.3.x_ref = bf16[8,64,128]{2,1,0:T(8,128)(2,1)S(1)} async-done(((bf16[8,64,128]{2,1,0:T(8,128)(2,1)}), bf16[8,64,128]{2,1,0:T(8,128)(2,1)S(1)}, u32[]{:S(2)}, u32[]{:S(2)}) %all-to-all-start.3) | async-done | bytes 131104 | tf_op jit(solution)/shard_map/all_to_all | solution.py:225
  101.8 0.7 unpack_kv.1
  (17 shorter events, 0.5 us)
Async XLA Ops:
  0.6 0.8 copy-start.2
  1.5 0.8 copy-start.3
  3.0 18.2 %all-to-all-start.1 = ((bf16[8,64,128]{2,1,0:T(8,128)(2,1)}), bf16[8,64,128]{2,1,0:T(8,128)(2,1)S(1)}, u32[]{:S(2)}, u32[]{:S(2)}) async-start(bf16[8,64,128]{2,1,0:T(8,128)(2,1)} %pack_kv.1), calls=%async_computation.1 | async-start | bytes 262144 | tf_op jit(solution)/shard_map/all_to_all | solution.py:225
  13.3 1.0 %copy-start = (bf16[32,64,128]{2,1,0:T(8,128)(2,1)S(1)}, bf16[32,64,128]{2,1,0:T(8,128)(2,1)}, u32[]{:S(2)}) copy-start(bf16[32,64,128]{2,1,0:T(8,128)(2,1)} %q_ref.1) | copy-start | bytes 1572868
  14.4 1.0 %copy-start.1 = (bf16[32,64,128]{2,1,0:T(8,128)(2,1)S(1)}, bf16[32,64,128]{2,1,0:T(8,128)(2,1)}, u32[]{:S(2)}) copy-start(bf16[32,64,128]{2,1,0:T(8,128)(2,1)} %g_ref.1) | copy-start | bytes 1572868
  21.2 28.7 %all-to-all-start = ((bf16[8,512,128]{2,1,0:T(8,128)(2,1)}), bf16[8,512,128]{2,1,0:T(8,128)(2,1)S(1)}, u32[]{:S(2)}, u32[]{:S(2)}) async-start(bf16[8,512,128]{2,1,0:T(8,128)(2,1)} %pack_qg.1), calls=%async_computation | async-start | bytes 2097152 | tf_op jit(solution)/shard_map/all_to_all | solution.py:225
  24.8 0.7 copy-start.4
  25.7 11.9 %collective-permute-start.2 = (bf16[8,64,128]{2,1,0:T(8,128)(2,1)S(1)}, bf16[8,64,128]{2,1,0:T(8,128)(2,1)S(1)}, u32[]{:S(2)}, u32[]{:S(2)}) collective-permute-start(bf16[8,64,128]{2,1,0:T(8,128)(2,1)S(1)} %all-to-all-done.1.own_ref), channel_id=1, source_target_pairs={{0,32},{16,48},{32,64},{48,80},{64,96},{80,112},{96,128},{112,144}... | collective-permute-start | bytes 393224 | tf_op jit(solution)/shard_map/ppermute | solution.py:230
  30.2 10.2 %collective-permute-start.1 = (bf16[8,64,128]{2,1,0:T(8,128)(2,1)S(1)}, bf16[8,64,128]{2,1,0:T(8,128)(2,1)S(1)}, u32[]{:S(2)}, u32[]{:S(2)}) collective-permute-start(bf16[8,64,128]{2,1,0:T(8,128)(2,1)S(1)} %all-to-all-done.1.own_ref), channel_id=1, source_target_pairs={{0,16},{16,32},{32,48},{48,64},{64,80},{80,96},{96,112},{112,128},... | collective-permute-start | bytes 393224 | tf_op jit(solution)/shard_map/ppermute | solution.py:230
  40.4 5.4 %collective-permute-start.3 = (bf16[2,8,64,128]{3,2,1,0:T(8,128)(2,1)S(1)}, bf16[2,8,64,128]{3,2,1,0:T(8,128)(2,1)S(1)}, u32[]{:S(2)}, u32[]{:S(2)}) collective-permute-start(bf16[2,8,64,128]{3,2,1,0:T(8,128)(2,1)S(1)} %pad_maximum_fusion.old_ref), channel_id=1, source_target_pairs={{0,1},{1,0},{2,3},{3,2},{4,5},{5,4},{6,7},{7,6},{8,9},{9,8},{10,11... | collective-permute-start | bytes 786440 | tf_op jit(solution)/shard_map/ppermute | solution.py:234
  42.5 3.4 %collective-permute-start = (bf16[8,64,128]{2,1,0:T(8,128)(2,1)S(1)}, bf16[8,64,128]{2,1,0:T(8,128)(2,1)S(1)}, u32[]{:S(2)}, u32[]{:S(2)}) collective-permute-start(bf16[8,64,128]{2,1,0:T(8,128)(2,1)S(1)} %all-to-all-done.1.own_ref), channel_id=1, source_target_pairs={{0,1},{1,0},{2,3},{3,2},{4,5},{5,4},{6,7},{7,6},{8,9},{9,8},{10,11... | collective-permute-start | bytes 393224 | tf_op jit(solution)/shard_map/ppermute | solution.py:234
  59.5 29.8 %all-to-all-start.2 = ((bf16[8,512,128]{2,1,0:T(8,128)(2,1)}), bf16[8,512,128]{2,1,0:T(8,128)(2,1)S(1)}, u32[]{:S(2)}, u32[]{:S(2)}) async-start(bf16[8,512,128]{2,1,0:T(8,128)(2,1)} %get-tuple-element.15), calls=%async_computation.2 | async-start | bytes 2097152 | tf_op jit(solution)/shard_map/all_to_all | solution.py:225
  64.0 3.6 %collective-permute-start.4 = (bf16[3,8,64,128]{3,2,1,0:T(8,128)(2,1)S(1)}, bf16[3,8,64,128]{3,2,1,0:T(8,128)(2,1)S(1)}, u32[]{:S(2)}, u32[]{:S(2)}) collective-permute-start(bf16[3,8,64,128]{3,2,1,0:T(8,128)(2,1)S(1)} %get-tuple-element.17), channel_id=1, source_target_pairs={{0,1},{1,0},{2,3},{3,2},{4,5},{5,4},{6,7},{7,6},{8,9},{9,8},{10,11... | collective-permute-start | bytes 1179656 | tf_op jit(solution)/shard_map/ppermute | solution.py:234
  67.7 9.7 %collective-permute-start.5 = (bf16[8,64,128]{2,1,0:T(8,128)(2,1)S(1)}, bf16[8,64,128]{2,1,0:T(8,128)(2,1)S(1)}, u32[]{:S(2)}, u32[]{:S(2)}) collective-permute-start(bf16[8,64,128]{2,1,0:T(8,128)(2,1)S(1)} %get-tuple-element.18), channel_id=1, source_target_pairs={{0,496},{16,0},{32,16},{48,32},{64,48},{80,64},{96,80},{112,96},{1... | collective-permute-start | bytes 393224 | tf_op jit(solution)/shard_map/ppermute | solution.py:230
  73.3 9.4 %collective-permute-start.6 = (bf16[8,64,128]{2,1,0:T(8,128)(2,1)S(1)}, bf16[8,64,128]{2,1,0:T(8,128)(2,1)S(1)}, u32[]{:S(2)}, u32[]{:S(2)}) collective-permute-start(bf16[8,64,128]{2,1,0:T(8,128)(2,1)S(1)} %get-tuple-element.19), channel_id=1, source_target_pairs={{0,480},{16,496},{32,0},{48,16},{64,32},{80,48},{96,64},{112,80},{... | collective-permute-start | bytes 393224 | tf_op jit(solution)/shard_map/ppermute | solution.py:230
  89.3 12.5 %all-to-all-start.3 = ((bf16[8,64,128]{2,1,0:T(8,128)(2,1)}), bf16[8,64,128]{2,1,0:T(8,128)(2,1)S(1)}, u32[]{:S(2)}, u32[]{:S(2)}) async-start(bf16[8,64,128]{2,1,0:T(8,128)(2,1)} %add_terms.1), calls=%async_computation.3 | async-start | bytes 262144 | tf_op jit(solution)/shard_map/all_to_all | solution.py:225

commit v4 on v3

--- a/solution.py
+++ b/solution.py
@@ -8,9 +8,9 @@
 from jax.sharding import Mesh
 from jax.sharding import PartitionSpec as P
 
-AXES = ("x", "y", "l", "h", "c")
-SIZES = (4, 8, 2, 4, 2)
-RING = ("l", "h")
+AXES = ("x", "y", "l", "h", "k", "c")
+SIZES = (4, 8, 2, 2, 2, 2)
+RING = ("l", "h", "k")
 COLUMNS = ("x", "y")
 
 HD = 128
@@ -25,7 +25,11 @@
 PAIR = 2
 ROWS = PAIR * PIECE
 BLOCKS = KVH // PAIR
+PLACES = [
+    sum((p >> ("k", "h", "l").index(axis) & 1) << (2 - n) for n, axis in enumerate(RING)) for p in range(KVH)
+]
 WIN = 9
+NEAR = WIN - BLOCKS
 SCALE = HD**-0.5
 SCALE2 = SCALE * math.log2(math.e)
 NEG = -1e30
@@ -77,13 +81,6 @@
         out_ref[:, pair * 2 * GROUP : (pair + 1) * 2 * GROUP, :] = both
 
 
-def pack_kv(k_ref, v_ref, out_ref, wide):
-    for at, ref in ((0, k_ref), (TOK, v_ref)):
-        wide[...] = ref[...].astype(F32).reshape(TOK * KVH, HD)
-        for j in range(KVH):
-            out_ref[j, at : at + TOK, :] = wide[pl.ds(j, TOK, stride=KVH), :].astype(BF16)
-
-
 def pack_qg(q_ref, g_ref, out_ref):
     put_heads(q_ref, out_ref, 0)
     put_heads(g_ref, out_ref, PIECE)
@@ -101,16 +98,16 @@
         ref[...] = wide[...].reshape(TOK, KVH, HD).astype(BF16)
 
 
-def attend(core_ref, qg_ref, start_ref, own_ref, other_ref, old_ref, other_old_ref,
+def attend(where_ref, qg_ref, start_ref, own_ref, other_ref, old_ref, other_old_ref,
            od_ref, mine_ref, theirs_ref,
            keys, values, keys_t, values_t, scores, probs, dscores, dk, dv):
-    core = core_ref[0]
+    core = where_ref[0]
     for column in range(REACH + 1):
         for piece in range(KVH):
             base = (REACH - column) * COL + piece * 2 * TOK
             for ref, old, which in ((own_ref, old_ref, core), (other_ref, other_old_ref, 1 - core)):
                 at = pl.ds(pl.multiple_of(base + which * TOK, TOK), TOK)
-                got = ref[piece] if column == 0 else old[column - 1, piece]
+                got = ref[PLACES[piece]] if column == 0 else old[column - 1, PLACES[piece]]
                 keys[at, :] = got[0:TOK]
                 values[at, :] = got[TOK : 2 * TOK]
     for t in range(KEYS // TILE):
@@ -126,13 +123,15 @@
     tiles = [slice(t * TILE, (t + 1) * TILE) for t in range(WIN)]
 
     class Block:
-        def __init__(self, at):
+        def __init__(self, at, count):
             self.slot = at % 2
-            self.base = at * TILE
-            self.window = slice(self.base, self.base + WIN * TILE)
-            self.pieces = slice(at * PAIR, (at + 1) * PAIR)
-            self.q = qg_ref[self.pieces, 0:PIECE, :].reshape(ROWS, HD)
-            self.g = qg_ref[self.pieces, PIECE : 2 * PIECE, :].reshape(ROWS, HD)
+            self.count = count
+            self.base = (at + WIN - count) * TILE
+            self.window = slice(self.base, self.base + count * TILE)
+            self.held = slice(0, count * TILE)
+            self.pieces = PLACES[at * PAIR : (at + 1) * PAIR]
+            self.q = jnp.concatenate([qg_ref[p, 0:PIECE, :] for p in self.pieces], axis=0)
+            self.g = jnp.concatenate([qg_ref[p, PIECE : 2 * PIECE, :] for p in self.pieces], axis=0)
             self.g_t = jnp.transpose(self.g.astype(F32))
             self.start = start_ref[at] - self.base
             self.top = jnp.full((8, ROWS), NEG, F32)
@@ -141,10 +140,15 @@
         def keys_of(self, t):
             return slice(self.base + t * TILE, self.base + (t + 1) * TILE)
 
+        def put(self, at, result):
+            rows = jnp.transpose(result).astype(BF16)
+            for n, p in enumerate(self.pieces):
+                od_ref[p, at : at + PIECE, :] = rows[n * PIECE : (n + 1) * PIECE]
+
         def score(self, t):
             s = dot(keys[self.keys_of(t), :], self.q, NT)
             seen = index >= self.start - t * TILE
-            if t == WIN - 1:
+            if t == self.count - 1:
                 seen = seen & (index <= inside)
             s = jnp.where(seen, s, NEG)
             scores[tiles[t], :] = s
@@ -160,54 +164,63 @@
 
         def output(self):
             self.inv = 1.0 / jnp.sum(self.sums, axis=0, keepdims=True)
-            out = dot(values_t[:, self.window], probs[self.slot], NN) * self.inv
+            out = dot(values_t[:, self.window], probs[self.slot, self.held], NN) * self.inv
             self.drift = jnp.sum(out * self.g_t, axis=0, keepdims=True)
-            od_ref[self.pieces, 0:PIECE, :] = jnp.transpose(out).astype(BF16).reshape(PAIR, PIECE, HD)
-            inv = jnp.transpose(jnp.broadcast_to(self.inv, (8, ROWS)))[:, 0:1]
-            self.g_scaled = (self.g.astype(F32) * inv).astype(BF16)
-            self.q_scaled = (self.q.astype(F32) * inv).astype(BF16)
+            self.put(0, out)
+            self.g_scaled = jnp.transpose((self.g_t * self.inv).astype(BF16))
 
         def dscore(self, t):
             dp = dot(values[self.keys_of(t), :], self.g, NT)
-            dscores[self.slot, tiles[t], :] = (dp - self.drift).astype(BF16) * probs[self.slot, tiles[t], :]
-
-        def key_terms(self, t):
-            at = self.keys_of(t)
-            dv[at, :] += dot(probs[self.slot, tiles[t], :], self.g_scaled, NN)
-            dk[at, :] += dot(dscores[self.slot, tiles[t], :], self.q_scaled, NN)
+            ds = ((dp - self.drift) * self.inv).astype(BF16)
+            dscores[self.slot, tiles[t], :] = ds * probs[self.slot, tiles[t], :]
+
+        def dvalue(self):
+            dv[self.window, :] += dot(probs[self.slot, self.held], self.g_scaled, NN)
+
+        def dkey(self):
+            dk[self.window, :] += dot(dscores[self.slot, self.held], self.q, NN)
 
         def dquery(self):
-            dq = dot(keys_t[:, self.window], dscores[self.slot], NN) * (self.inv * SCALE)
-            od_ref[self.pieces, PIECE : 2 * PIECE, :] = jnp.transpose(dq).astype(BF16).reshape(PAIR, PIECE, HD)
-
-    last = None
-    for at in range(BLOCKS + 1):
-        block = Block(at) if at < BLOCKS else None
-        for t in range(WIN):
+            self.put(PIECE, dot(keys_t[:, self.window], dscores[self.slot, self.held], NN) * SCALE)
+
+    def pipeline(counts):
+        last = None
+        for at in range(BLOCKS + 1):
+            block = Block(at, counts[at]) if at < BLOCKS else None
+            for t in range(WIN):
+                if block and t < block.count:
+                    block.score(t)
+                if last and t < last.count:
+                    last.dscore(t)
             if block:
-                block.score(t)
+                block.find_top()
             if last:
-                last.dscore(t)
-        if block:
-            block.find_top()
-        for t in range(WIN):
+                last.dvalue()
+            for t in range(WIN):
+                if block and t < block.count:
+                    block.weigh(t)
+            if last:
+                last.dkey()
+                last.dquery()
             if block:
-                block.weigh(t)
-            if last:
-                last.key_terms(t)
-        if last:
-            last.dquery()
-        if block:
-            block.output()
-        last = block
+                block.output()
+            last = block
+
+    @pl.when(where_ref[1] == 0)
+    def near():
+        pipeline([NEAR + 1 + at for at in range(BLOCKS)])
+
+    @pl.when(where_ref[1] != 0)
+    def far():
+        pipeline([WIN] * (BLOCKS - 1) + [BLOCKS])
 
     for column in range(REACH + 1):
         for piece in range(KVH):
             base = (REACH - column) * COL + piece * 2 * TOK
             for ref, which in ((mine_ref, core), (theirs_ref, 1 - core)):
                 at = pl.ds(pl.multiple_of(base + which * TOK, TOK), TOK)
-                ref[column, piece, 0:TOK] = (dk[at, :] * SCALE).astype(ref.dtype)
-                ref[column, piece, TOK : 2 * TOK] = dv[at, :].astype(ref.dtype)
+                ref[column, PLACES[piece], 0:TOK] = (dk[at, :] * SCALE).astype(ref.dtype)
+                ref[column, PLACES[piece], TOK : 2 * TOK] = dv[at, :].astype(ref.dtype)
 
 
 def old_terms(mine_ref, got_ref, one_ref, two_ref):
@@ -250,14 +263,17 @@
     heads_wide = shape(TOK, KVH * GROUP, HD)
     wide = [pltpu.VMEM((TOK * KVH, HD), F32)]
 
-    kv = exchange(call(pack_kv, [both_kv], [VMEM] * 2, wide, "pack_kv")(key_in, value_in)[0])
+    packed = jnp.transpose(jnp.stack([key_in, value_in]), (2, 0, 1, 3)).reshape(KVH, 2 * TOK, HD)
+    kv = exchange(packed)
     qg = exchange(call(pack_qg, [both_wide], [VMEM] * 2, [], "pack_qg")(query_in, grad_out)[0])
     other = swapped(kv)
     old = jnp.stack([shifted(kv, 1), shifted(kv, 2)])
+    old, other = lax.optimization_barrier((old, other))
     other_old = swapped(old)
 
     core = lax.axis_index("c").astype(jnp.int32)
     start = starts(doc_lengths, lax.axis_index(COLUMNS), core)
+    where = jnp.stack([core, (start[0, 0, 0] < REACH * COL - NEAR * TILE).astype(jnp.int32)])
     od, mine, theirs = call(
         attend,
         [both_wide, shape(REACH + 1, KVH, 2 * TOK, HD, dtype=F32), shape(REACH + 1, KVH, 2 * TOK, HD)],
@@ -269,7 +285,7 @@
         + [pltpu.VMEM((KEYS, HD), F32)] * 2,
         "attend",
         12 * BLOCKS * ROWS * WIN * TILE * HD,
-    )(core[None], qg, start, kv, other, old, other_old)
+    )(where, qg, start, kv, other, old, other_old)
 
     od_back = exchange(od)
     got = swapped(theirs)

time: 104 us -> 102 us (0.981)
  local copies, waits for them, and re-layouts: 4.5 us -> 2.98 us
  Pallas kernels: 14.1 us -> 12.6 us
    all_to_all x4, waiting for transfers between devices: 21.3 us -> 25.2 us  [exchange(): return lax.all_to_all(x, RING, split_axis=0, concat_axis=0, tiled=True)]
    ppermute x4, waiting for transfers between devices: 12 us -> 8.55 us  [shifted(): lax.ppermute(x, COLUMNS, [(i, (i + by) % count) for i in range(count)])]
    unnamed x10 -> x6, local copies, waits for them, and re-layouts: 4.4 us -> 1.7 us
where the time goes in v4:
time: 102 us; the launch traced here: 101 us
  starting transfers between devices  46.9 us (46%)
  waiting for transfers between devices  35.7 us (35%)
  Pallas kernels  12.6 us (12%)
  local copies, waits for them, and re-layouts  2.98 us (3%)
  between operations  1.45 us (1%)
  other arithmetic  1.44 us (1%)
    all_to_all x4, waiting for transfers between devices, exchange(): return lax.all_to_all(x, RING, split_axis=0, concat_axis=0, tiled=True)  25.2 us
    all_to_all x4, starting transfers between devices, exchange(): return lax.all_to_all(x, RING, split_axis=0, concat_axis=0, tiled=True)  22.9 us
    ppermute x4, starting transfers between devices, shifted(): lax.ppermute(x, COLUMNS, [(i, (i + by) % count) for i in range(count)])  18.2 us
    pallas_call x1, Pallas kernels, shards(): call(attend, [both_wide, shape(REACH + 1, KVH, 2 * TOK, HD, dtype=F32), s...  8.87 us
    ppermute x4, waiting for transfers between devices, shifted(): lax.ppermute(x, COLUMNS, [(i, (i + by) % count) for i in range(count)])  8.55 us
    ppermute x3, starting transfers between devices, swapped(): return lax.ppermute(x, 'c', [(0, 1), (1, 0)])  5.74 us
  transfers between devices with their start and end apart: 11, of which 9 were waited for; matrix products, arithmetic and copies ran while one was open for 1% of the time, Pallas kernels for 3%

profile of v4, /device:TPU:6, one launch (start us, length us, event | category | flops | bytes accessed | tf_op | source)
XLA Modules:
  0.0 101.0 jit_solution(3665729839455309867)
XLA Ops:
  0.6 0.9 maximum_bitcast_fusion
  1.6 0.7 copy.14
  2.3 10.3 %all-to-all-start.1 = ((bf16[8,64,128]{2,1,0:T(8,128)(2,1)}), bf16[8,64,128]{2,1,0:T(8,128)(2,1)S(1)}, u32[]{:S(2)}, u32[]{:S(2)}) async-start(bf16[8,64,128]{2,1,0:T(8,128)(2,1)} %bitcast.6), calls=%async_computation.1 | async-start | bytes 262144 | tf_op jit(solution)/shard_map/all_to_all | solution.py:238
  12.6 1.0 %copy-done.1 = bf16[32,64,128]{2,1,0:T(8,128)(2,1)S(1)} copy-done((bf16[32,64,128]{2,1,0:T(8,128)(2,1)S(1)}, bf16[32,64,128]{2,1,0:T(8,128)(2,1)}, u32[]{:S(2)}) %copy-start.1) | copy-done | bytes 524312
  13.6 1.2 %pack_qg.1 = bf16[8,512,128]{2,1,0:T(8,128)(2,1)} custom-call(bf16[32,64,128]{2,1,0:T(8,128)(2,1)S(1)} %copy-done, bf16[32,64,128]{2,1,0:T(8,128)(2,1)S(1)} %copy-done.1), custom_call_target="tpu_custom_call" | custom-call | bytes 1048576 | tf_op jit(solution)/shard_map/pack_qg/pallas_call | solution.py:268
  14.8 5.6 %all-to-all-done.1.own_ref = bf16[8,64,128]{2,1,0:T(8,128)(2,1)S(1)} async-done(((bf16[8,64,128]{2,1,0:T(8,128)(2,1)}), bf16[8,64,128]{2,1,0:T(8,128)(2,1)S(1)}, u32[]{:S(2)}, u32[]{:S(2)}) %all-to-all-start.1) | async-done | bytes 131104 | tf_op jit(solution)/shard_map/all_to_all | solution.py:238
  20.4 3.6 %all-to-all-start = ((bf16[8,512,128]{2,1,0:T(8,128)(2,1)}), bf16[8,512,128]{2,1,0:T(8,128)(2,1)S(1)}, u32[]{:S(2)}, u32[]{:S(2)}) async-start(bf16[8,512,128]{2,1,0:T(8,128)(2,1)} %pack_qg.1), calls=%async_computation | async-start | bytes 2097152 | tf_op jit(solution)/shard_map/all_to_all | solution.py:238
  24.0 4.5 %collective-permute-start.1 = (bf16[8,64,128]{2,1,0:T(8,128)(2,1)S(1)}, bf16[8,64,128]{2,1,0:T(8,128)(2,1)S(1)}, u32[]{:S(2)}, u32[]{:S(2)}) collective-permute-start(bf16[8,64,128]{2,1,0:T(8,128)(2,1)S(1)} %all-to-all-done.1.own_ref), channel_id=1, source_target_pairs={{0,32},{16,48},{32,64},{48,80},{64,96},{80,112},{96,128},{112,144}... | collective-permute-start | bytes 393224 | tf_op jit(solution)/shard_map/ppermute | solution.py:243
  28.5 3.5 %collective-permute-start = (bf16[8,64,128]{2,1,0:T(8,128)(2,1)S(1)}, bf16[8,64,128]{2,1,0:T(8,128)(2,1)S(1)}, u32[]{:S(2)}, u32[]{:S(2)}) collective-permute-start(bf16[8,64,128]{2,1,0:T(8,128)(2,1)S(1)} %all-to-all-done.1.own_ref), channel_id=1, source_target_pairs={{0,16},{16,32},{32,48},{48,64},{64,80},{80,96},{96,112},{112,128},... | collective-permute-start | bytes 393224 | tf_op jit(solution)/shard_map/ppermute | solution.py:243
  32.1 0.7 copy-done.2
  32.9 0.1 reduce
  33.0 1.9 %collective-permute-start.2 = (bf16[8,64,128]{2,1,0:T(8,128)(2,1)S(1)}, bf16[8,64,128]{2,1,0:T(8,128)(2,1)S(1)}, u32[]{:S(2)}, u32[]{:S(2)}) collective-permute-start(bf16[8,64,128]{2,1,0:T(8,128)(2,1)S(1)} %all-to-all-done.1.own_ref), channel_id=1, source_target_pairs={{0,1},{1,0},{2,3},{3,2},{4,5},{5,4},{6,7},{7,6},{8,9},{9,8},{10,11... | collective-permute-start | bytes 393224 | tf_op jit(solution)/shard_map/ppermute | solution.py:247
  34.9 0.1 select_reduce_fusion
  35.1 0.9 collective-permute-done.1
  36.0 2.7 %collective-permute-done = bf16[8,64,128]{2,1,0:T(8,128)(2,1)S(1)} collective-permute-done((bf16[8,64,128]{2,1,0:T(8,128)(2,1)S(1)}, bf16[8,64,128]{2,1,0:T(8,128)(2,1)S(1)}, u32[]{:S(2)}, u32[]{:S(2)}) %collective-permute-start) | collective-permute-done | bytes 131104 | tf_op jit(solution)/shard_map/ppermute | solution.py:243
  38.7 1.9 %collective-permute-start.3 = (bf16[2,8,64,128]{3,2,1,0:T(8,128)(2,1)S(1)}, bf16[2,8,64,128]{3,2,1,0:T(8,128)(2,1)S(1)}, u32[]{:S(2)}, u32[]{:S(2)}) collective-permute-start(bf16[2,8,64,128]{3,2,1,0:T(8,128)(2,1)S(1)} %pad_maximum_fusion.old_ref), channel_id=1, source_target_pairs={{0,1},{1,0},{2,3},{3,2},{4,5},{5,4},{6,7},{7,6},{8,9},{9,8},{10,11... | collective-permute-start | bytes 786440 | tf_op jit(solution)/shard_map/ppermute | solution.py:247
  40.7 0.5 slice.4
  41.9 0.2 collective-permute-done.3.other_old_ref
  42.2 7.0 %all-to-all-done.qg_ref = bf16[8,512,128]{2,1,0:T(8,128)(2,1)S(1)} async-done(((bf16[8,512,128]{2,1,0:T(8,128)(2,1)}), bf16[8,512,128]{2,1,0:T(8,128)(2,1)S(1)}, u32[]{:S(2)}, u32[]{:S(2)}) %all-to-all-start) | async-done | bytes 1048608 | tf_op jit(solution)/shard_map/all_to_all | solution.py:238
  49.2 8.9 %attend.1 = (bf16[8,512,128]{2,1,0:T(8,128)(2,1)}, f32[3,8,64,128]{3,2,1,0:T(8,128)S(1)}, bf16[3,8,64,128]{3,2,1,0:T(8,128)(2,1)S(1)}) custom-call(s32[2]{0:T(128)S(1)} %pad_add_fusion.where_ref, bf16[8,512,128]{2,1,0:T(8,128)(2,1)S(1)} %all-to-all-done.qg_ref, s32[4,1,512]{2,1,0:T(1,128)S(1)} %max.18.start_ref, ...), custom_call_target="tpu_custom_call" | custom-call | flops 3623878656 | bytes 1048576 | tf_op jit(solution)/shard_map/attend/pallas_call | solution.py:277
  58.0 4.5 %all-to-all-start.2 = ((bf16[8,512,128]{2,1,0:T(8,128)(2,1)}), bf16[8,512,128]{2,1,0:T(8,128)(2,1)S(1)}, u32[]{:S(2)}, u32[]{:S(2)}) async-start(bf16[8,512,128]{2,1,0:T(8,128)(2,1)} %get-tuple-element.19), calls=%async_computation.2 | async-start | bytes 2097152 | tf_op jit(solution)/shard_map/all_to_all | solution.py:238
  62.5 1.9 %collective-permute-start.4 = (bf16[3,8,64,128]{3,2,1,0:T(8,128)(2,1)S(1)}, bf16[3,8,64,128]{3,2,1,0:T(8,128)(2,1)S(1)}, u32[]{:S(2)}, u32[]{:S(2)}) collective-permute-start(bf16[3,8,64,128]{3,2,1,0:T(8,128)(2,1)S(1)} %get-tuple-element.21), channel_id=1, source_target_pairs={{0,1},{1,0},{2,3},{3,2},{4,5},{5,4},{6,7},{7,6},{8,9},{9,8},{10,11... | collective-permute-start | bytes 1179656 | tf_op jit(solution)/shard_map/ppermute | solution.py:247
  64.4 1.7 %collective-permute-done.4.got_ref = bf16[3,8,64,128]{3,2,1,0:T(8,128)(2,1)S(1)} collective-permute-done((bf16[3,8,64,128]{3,2,1,0:T(8,128)(2,1)S(1)}, bf16[3,8,64,128]{3,2,1,0:T(8,128)(2,1)S(1)}, u32[]{:S(2)}, u32[]{:S(2)}) %collective-permute-start.4) | collective-permute-done | bytes 393248 | tf_op jit(solution)/shard_map/ppermute | solution.py:247
  66.2 6.2 %collective-permute-start.5 = (bf16[8,64,128]{2,1,0:T(8,128)(2,1)S(1)}, bf16[8,64,128]{2,1,0:T(8,128)(2,1)S(1)}, u32[]{:S(2)}, u32[]{:S(2)}) collective-permute-start(bf16[8,64,128]{2,1,0:T(8,128)(2,1)S(1)} %get-tuple-element.22), channel_id=1, source_target_pairs={{0,496},{16,0},{32,16},{48,32},{64,48},{80,64},{96,80},{112,96},{1... | collective-permute-start | bytes 393224 | tf_op jit(solution)/shard_map/ppermute | solution.py:243
  72.4 4.0 %collective-permute-start.6 = (bf16[8,64,128]{2,1,0:T(8,128)(2,1)S(1)}, bf16[8,64,128]{2,1,0:T(8,128)(2,1)S(1)}, u32[]{:S(2)}, u32[]{:S(2)}) collective-permute-start(bf16[8,64,128]{2,1,0:T(8,128)(2,1)S(1)} %get-tuple-element.23), channel_id=1, source_target_pairs={{0,480},{16,496},{32,0},{48,16},{64,32},{80,48},{96,64},{112,80},{... | collective-permute-start | bytes 393224 | tf_op jit(solution)/shard_map/ppermute | solution.py:243
  76.4 4.9 %collective-permute-done.6.two_ref = bf16[8,64,128]{2,1,0:T(8,128)(2,1)S(1)} collective-permute-done((bf16[8,64,128]{2,1,0:T(8,128)(2,1)S(1)}, bf16[8,64,128]{2,1,0:T(8,128)(2,1)S(1)}, u32[]{:S(2)}, u32[]{:S(2)}) %collective-permute-start.6) | collective-permute-done | bytes 131104 | tf_op jit(solution)/shard_map/ppermute | solution.py:243
  81.4 0.7 add_terms.1
  82.1 5.8 %all-to-all-done.2.x_ref = bf16[8,512,128]{2,1,0:T(8,128)(2,1)S(1)} async-done(((bf16[8,512,128]{2,1,0:T(8,128)(2,1)}), bf16[8,512,128]{2,1,0:T(8,128)(2,1)S(1)}, u32[]{:S(2)}, u32[]{:S(2)}) %all-to-all-start.2) | async-done | bytes 1048608 | tf_op jit(solution)/shard_map/all_to_all | solution.py:238
  87.8 4.5 %all-to-all-start.3 = ((bf16[8,64,128]{2,1,0:T(8,128)(2,1)}), bf16[8,64,128]{2,1,0:T(8,128)(2,1)S(1)}, u32[]{:S(2)}, u32[]{:S(2)}) async-start(bf16[8,64,128]{2,1,0:T(8,128)(2,1)} %add_terms.1), calls=%async_computation.3 | async-start | bytes 262144 | tf_op jit(solution)/shard_map/all_to_all | solution.py:238
  92.4 1.1 %unpack_od.1 = (bf16[32,64,128]{2,1,0:T(8,128)(2,1)}, bf16[32,64,128]{2,1,0:T(8,128)(2,1)}) custom-call(bf16[8,512,128]{2,1,0:T(8,128)(2,1)S(1)} %all-to-all-done.2.x_ref), custom_call_target="tpu_custom_call" | custom-call | bytes 1048576 | tf_op jit(solution)/shard_map/unpack_od/pallas_call | solution.py:297
  93.5 6.8 %all-to-all-done.3.x_ref = bf16[8,64,128]{2,1,0:T(8,128)(2,1)S(1)} async-done(((bf16[8,64,128]{2,1,0:T(8,128)(2,1)}), bf16[8,64,128]{2,1,0:T(8,128)(2,1)S(1)}, u32[]{:S(2)}, u32[]{:S(2)}) %all-to-all-start.3) | async-done | bytes 131104 | tf_op jit(solution)/shard_map/all_to_all | solution.py:238
  100.3 0.7 unpack_kv.1
  (16 shorter events, 0.4 us)
Async XLA Ops:
  0.6 12.0 %copy-start = (bf16[32,64,128]{2,1,0:T(8,128)(2,1)S(1)}, bf16[32,64,128]{2,1,0:T(8,128)(2,1)}, u32[]{:S(2)}) copy-start(bf16[32,64,128]{2,1,0:T(8,128)(2,1)} %q_ref.1) | copy-start | bytes 1572868
  2.3 18.2 %all-to-all-start.1 = ((bf16[8,64,128]{2,1,0:T(8,128)(2,1)}), bf16[8,64,128]{2,1,0:T(8,128)(2,1)S(1)}, u32[]{:S(2)}, u32[]{:S(2)}) async-start(bf16[8,64,128]{2,1,0:T(8,128)(2,1)} %bitcast.6), calls=%async_computation.1 | async-start | bytes 262144 | tf_op jit(solution)/shard_map/all_to_all | solution.py:238
  12.6 1.0 %copy-start.1 = (bf16[32,64,128]{2,1,0:T(8,128)(2,1)S(1)}, bf16[32,64,128]{2,1,0:T(8,128)(2,1)}, u32[]{:S(2)}) copy-start(bf16[32,64,128]{2,1,0:T(8,128)(2,1)} %g_ref.1) | copy-start | bytes 1572868
  20.4 28.7 %all-to-all-start = ((bf16[8,512,128]{2,1,0:T(8,128)(2,1)}), bf16[8,512,128]{2,1,0:T(8,128)(2,1)S(1)}, u32[]{:S(2)}, u32[]{:S(2)}) async-start(bf16[8,512,128]{2,1,0:T(8,128)(2,1)} %pack_qg.1), calls=%async_computation | async-start | bytes 2097152 | tf_op jit(solution)/shard_map/all_to_all | solution.py:238
  24.0 11.9 %collective-permute-start.1 = (bf16[8,64,128]{2,1,0:T(8,128)(2,1)S(1)}, bf16[8,64,128]{2,1,0:T(8,128)(2,1)S(1)}, u32[]{:S(2)}, u32[]{:S(2)}) collective-permute-start(bf16[8,64,128]{2,1,0:T(8,128)(2,1)S(1)} %all-to-all-done.1.own_ref), channel_id=1, source_target_pairs={{0,32},{16,48},{32,64},{48,80},{64,96},{80,112},{96,128},{112,144}... | collective-permute-start | bytes 393224 | tf_op jit(solution)/shard_map/ppermute | solution.py:243
  28.5 10.2 %collective-permute-start = (bf16[8,64,128]{2,1,0:T(8,128)(2,1)S(1)}, bf16[8,64,128]{2,1,0:T(8,128)(2,1)S(1)}, u32[]{:S(2)}, u32[]{:S(2)}) collective-permute-start(bf16[8,64,128]{2,1,0:T(8,128)(2,1)S(1)} %all-to-all-done.1.own_ref), channel_id=1, source_target_pairs={{0,16},{16,32},{32,48},{48,64},{64,80},{80,96},{96,112},{112,128},... | collective-permute-start | bytes 393224 | tf_op jit(solution)/shard_map/ppermute | solution.py:243
  32.1 0.7 copy-start.2
  33.0 5.7 %collective-permute-start.2 = (bf16[8,64,128]{2,1,0:T(8,128)(2,1)S(1)}, bf16[8,64,128]{2,1,0:T(8,128)(2,1)S(1)}, u32[]{:S(2)}, u32[]{:S(2)}) collective-permute-start(bf16[8,64,128]{2,1,0:T(8,128)(2,1)S(1)} %all-to-all-done.1.own_ref), channel_id=1, source_target_pairs={{0,1},{1,0},{2,3},{3,2},{4,5},{5,4},{6,7},{7,6},{8,9},{9,8},{10,11... | collective-permute-start | bytes 393224 | tf_op jit(solution)/shard_map/ppermute | solution.py:247
  38.7 3.4 %collective-permute-start.3 = (bf16[2,8,64,128]{3,2,1,0:T(8,128)(2,1)S(1)}, bf16[2,8,64,128]{3,2,1,0:T(8,128)(2,1)S(1)}, u32[]{:S(2)}, u32[]{:S(2)}) collective-permute-start(bf16[2,8,64,128]{3,2,1,0:T(8,128)(2,1)S(1)} %pad_maximum_fusion.old_ref), channel_id=1, source_target_pairs={{0,1},{1,0},{2,3},{3,2},{4,5},{5,4},{6,7},{7,6},{8,9},{9,8},{10,11... | collective-permute-start | bytes 786440 | tf_op jit(solution)/shard_map/ppermute | solution.py:247
  58.0 29.8 %all-to-all-start.2 = ((bf16[8,512,128]{2,1,0:T(8,128)(2,1)}), bf16[8,512,128]{2,1,0:T(8,128)(2,1)S(1)}, u32[]{:S(2)}, u32[]{:S(2)}) async-start(bf16[8,512,128]{2,1,0:T(8,128)(2,1)} %get-tuple-element.19), calls=%async_computation.2 | async-start | bytes 2097152 | tf_op jit(solution)/shard_map/all_to_all | solution.py:238
  62.5 3.6 %collective-permute-start.4 = (bf16[3,8,64,128]{3,2,1,0:T(8,128)(2,1)S(1)}, bf16[3,8,64,128]{3,2,1,0:T(8,128)(2,1)S(1)}, u32[]{:S(2)}, u32[]{:S(2)}) collective-permute-start(bf16[3,8,64,128]{3,2,1,0:T(8,128)(2,1)S(1)} %get-tuple-element.21), channel_id=1, source_target_pairs={{0,1},{1,0},{2,3},{3,2},{4,5},{5,4},{6,7},{7,6},{8,9},{9,8},{10,11... | collective-permute-start | bytes 1179656 | tf_op jit(solution)/shard_map/ppermute | solution.py:247
  66.2 10.2 %collective-permute-start.5 = (bf16[8,64,128]{2,1,0:T(8,128)(2,1)S(1)}, bf16[8,64,128]{2,1,0:T(8,128)(2,1)S(1)}, u32[]{:S(2)}, u32[]{:S(2)}) collective-permute-start(bf16[8,64,128]{2,1,0:T(8,128)(2,1)S(1)} %get-tuple-element.22), channel_id=1, source_target_pairs={{0,496},{16,0},{32,16},{48,32},{64,48},{80,64},{96,80},{112,96},{1... | collective-permute-start | bytes 393224 | tf_op jit(solution)/shard_map/ppermute | solution.py:243
  72.4 9.0 %collective-permute-start.6 = (bf16[8,64,128]{2,1,0:T(8,128)(2,1)S(1)}, bf16[8,64,128]{2,1,0:T(8,128)(2,1)S(1)}, u32[]{:S(2)}, u32[]{:S(2)}) collective-permute-start(bf16[8,64,128]{2,1,0:T(8,128)(2,1)S(1)} %get-tuple-element.23), channel_id=1, source_target_pairs={{0,480},{16,496},{32,0},{48,16},{64,32},{80,48},{96,64},{112,80},{... | collective-permute-start | bytes 393224 | tf_op jit(solution)/shard_map/ppermute | solution.py:243
  87.8 12.5 %all-to-all-start.3 = ((bf16[8,64,128]{2,1,0:T(8,128)(2,1)}), bf16[8,64,128]{2,1,0:T(8,128)(2,1)S(1)}, u32[]{:S(2)}, u32[]{:S(2)}) async-start(bf16[8,64,128]{2,1,0:T(8,128)(2,1)} %add_terms.1), calls=%async_computation.3 | async-start | bytes 262144 | tf_op jit(solution)/shard_map/all_to_all | solution.py:238

commit v5 on v4

--- a/solution.py
+++ b/solution.py
@@ -38,6 +38,7 @@
 BF16 = jnp.bfloat16
 VMEM = pl.BlockSpec(memory_space=pltpu.VMEM)
 SMEM = pl.BlockSpec(memory_space=pltpu.SMEM)
+HBM = pl.BlockSpec(memory_space=pl.ANY)
 NT = (((1,), (1,)), ((), ()))
 NN = (((1,), (0,)), ((), ()))
 
@@ -46,12 +47,12 @@
     return lax.dot_general(a, b, dims, preferred_element_type=F32)
 
 
-def call(kernel, outs, ins, scratch, name, flops=0, nbytes=1 << 20):
+def call(kernel, outs, ins, scratch, name, flops=0, nbytes=1 << 20, first=VMEM):
     return pl.pallas_call(
         kernel,
         out_shape=outs,
         in_specs=ins,
-        out_specs=[VMEM] * len(outs),
+        out_specs=[first] + [VMEM] * (len(outs) - 1),
         scratch_shapes=scratch,
         compiler_params=pltpu.CompilerParams(vmem_limit_bytes=48 << 20),
         cost_estimate=pl.CostEstimate(flops=flops, bytes_accessed=nbytes, transcendentals=0),
@@ -100,7 +101,7 @@
 
 def attend(where_ref, qg_ref, start_ref, own_ref, other_ref, old_ref, other_old_ref,
            od_ref, mine_ref, theirs_ref,
-           keys, values, keys_t, values_t, scores, probs, dscores, dk, dv):
+           keys, values, keys_t, values_t, scores, probs, dscores, dk, dv, od, sems):
     core = where_ref[0]
     for column in range(REACH + 1):
         for piece in range(KVH):
@@ -123,7 +124,8 @@
     tiles = [slice(t * TILE, (t + 1) * TILE) for t in range(WIN)]
 
     class Block:
-        def __init__(self, at, count):
+        def __init__(self, at, count, sent):
+            self.sent = sent
             self.slot = at % 2
             self.count = count
             self.base = (at + WIN - count) * TILE
@@ -143,7 +145,11 @@
         def put(self, at, result):
             rows = jnp.transpose(result).astype(BF16)
             for n, p in enumerate(self.pieces):
-                od_ref[p, at : at + PIECE, :] = rows[n * PIECE : (n + 1) * PIECE]
+                piece = (p, pl.ds(at, PIECE))
+                od[piece] = rows[n * PIECE : (n + 1) * PIECE]
+                copy = pltpu.make_async_copy(od.at[piece], od_ref.at[piece], sems.at[len(self.sent)])
+                copy.start()
+                self.sent.append(copy)
 
         def score(self, t):
             s = dot(keys[self.keys_of(t), :], self.q, NT)
@@ -185,8 +191,9 @@
 
     def pipeline(counts):
         last = None
+        sent = []
         for at in range(BLOCKS + 1):
-            block = Block(at, counts[at]) if at < BLOCKS else None
+            block = Block(at, counts[at], sent) if at < BLOCKS else None
             for t in range(WIN):
                 if block and t < block.count:
                     block.score(t)
@@ -205,6 +212,8 @@
             if block:
                 block.output()
             last = block
+        for copy in sent:
+            copy.wait()
 
     @pl.when(where_ref[1] == 0)
     def near():
@@ -282,9 +291,11 @@
         + [pltpu.VMEM((HD, KEYS), BF16)] * 2
         + [pltpu.VMEM((WIN * TILE, ROWS), F32)]
         + [pltpu.VMEM((2, WIN * TILE, ROWS), BF16)] * 2
-        + [pltpu.VMEM((KEYS, HD), F32)] * 2,
+        + [pltpu.VMEM((KEYS, HD), F32)] * 2
+        + [pltpu.VMEM((KVH, 2 * PIECE, HD), BF16), pltpu.SemaphoreType.DMA((4 * BLOCKS,))],
         "attend",
         12 * BLOCKS * ROWS * WIN * TILE * HD,
+        first=HBM,
     )(where, qg, start, kv, other, old, other_old)
 
     od_back = exchange(od)

time: 102 us -> 102 us (level)
  no operation moved by 1% of the time
where the time goes in v5:
time: 102 us; the launch traced here: 101 us
  starting transfers between devices  47.1 us (46%)
  waiting for transfers between devices  35.4 us (35%)
  Pallas kernels  12.3 us (12%)
  local copies, waits for them, and re-layouts  2.98 us (3%)
  between operations  1.46 us (1%)
  other arithmetic  1.44 us (1%)
    all_to_all x4, waiting for transfers between devices, exchange(): return lax.all_to_all(x, RING, split_axis=0, concat_axis=0, tiled=True)  25.3 us
    all_to_all x4, starting transfers between devices, exchange(): return lax.all_to_all(x, RING, split_axis=0, concat_axis=0, tiled=True)  22.9 us
    ppermute x4, starting transfers between devices, shifted(): lax.ppermute(x, COLUMNS, [(i, (i + by) % count) for i in range(count)])  18.4 us
    pallas_call x1, Pallas kernels, shards(): call(attend, [both_wide, shape(REACH + 1, KVH, 2 * TOK, HD, dtype=F32), s...  8.51 us
    ppermute x4, waiting for transfers between devices, shifted(): lax.ppermute(x, COLUMNS, [(i, (i + by) % count) for i in range(count)])  8.21 us
    ppermute x3, starting transfers between devices, swapped(): return lax.ppermute(x, 'c', [(0, 1), (1, 0)])  5.74 us
  transfers between devices with their start and end apart: 11, of which 9 were waited for; matrix products, arithmetic and copies ran while one was open for 1% of the time, Pallas kernels for 3%

profile of v5, /device:TPU:6, one launch (start us, length us, event | category | flops | bytes accessed | tf_op | source)
XLA Modules:
  0.0 100.7 jit_solution(17984726331001647231)
XLA Ops:
  0.6 0.9 maximum_bitcast_fusion
  1.6 0.7 copy.14
  2.3 10.3 %all-to-all-start.1 = ((bf16[8,64,128]{2,1,0:T(8,128)(2,1)}), bf16[8,64,128]{2,1,0:T(8,128)(2,1)S(1)}, u32[]{:S(2)}, u32[]{:S(2)}) async-start(bf16[8,64,128]{2,1,0:T(8,128)(2,1)} %bitcast.6), calls=%async_computation.1 | async-start | bytes 262144 | tf_op jit(solution)/shard_map/all_to_all | solution.py:247
  12.6 1.0 %copy-done.1 = bf16[32,64,128]{2,1,0:T(8,128)(2,1)S(1)} copy-done((bf16[32,64,128]{2,1,0:T(8,128)(2,1)S(1)}, bf16[32,64,128]{2,1,0:T(8,128)(2,1)}, u32[]{:S(2)}) %copy-start.1) | copy-done | bytes 524312
  13.6 1.2 %pack_qg.1 = bf16[8,512,128]{2,1,0:T(8,128)(2,1)} custom-call(bf16[32,64,128]{2,1,0:T(8,128)(2,1)S(1)} %copy-done, bf16[32,64,128]{2,1,0:T(8,128)(2,1)S(1)} %copy-done.1), custom_call_target="tpu_custom_call" | custom-call | bytes 1048576 | tf_op jit(solution)/shard_map/pack_qg/pallas_call | solution.py:277
  14.8 5.6 %all-to-all-done.1.own_ref = bf16[8,64,128]{2,1,0:T(8,128)(2,1)S(1)} async-done(((bf16[8,64,128]{2,1,0:T(8,128)(2,1)}), bf16[8,64,128]{2,1,0:T(8,128)(2,1)S(1)}, u32[]{:S(2)}, u32[]{:S(2)}) %all-to-all-start.1) | async-done | bytes 131104 | tf_op jit(solution)/shard_map/all_to_all | solution.py:247
  20.4 3.6 %all-to-all-start = ((bf16[8,512,128]{2,1,0:T(8,128)(2,1)}), bf16[8,512,128]{2,1,0:T(8,128)(2,1)S(1)}, u32[]{:S(2)}, u32[]{:S(2)}) async-start(bf16[8,512,128]{2,1,0:T(8,128)(2,1)} %pack_qg.1), calls=%async_computation | async-start | bytes 2097152 | tf_op jit(solution)/shard_map/all_to_all | solution.py:247
  24.0 4.5 %collective-permute-start.1 = (bf16[8,64,128]{2,1,0:T(8,128)(2,1)S(1)}, bf16[8,64,128]{2,1,0:T(8,128)(2,1)S(1)}, u32[]{:S(2)}, u32[]{:S(2)}) collective-permute-start(bf16[8,64,128]{2,1,0:T(8,128)(2,1)S(1)} %all-to-all-done.1.own_ref), channel_id=1, source_target_pairs={{0,32},{16,48},{32,64},{48,80},{64,96},{80,112},{96,128},{112,144}... | collective-permute-start | bytes 393224 | tf_op jit(solution)/shard_map/ppermute | solution.py:252
  28.5 3.5 %collective-permute-start = (bf16[8,64,128]{2,1,0:T(8,128)(2,1)S(1)}, bf16[8,64,128]{2,1,0:T(8,128)(2,1)S(1)}, u32[]{:S(2)}, u32[]{:S(2)}) collective-permute-start(bf16[8,64,128]{2,1,0:T(8,128)(2,1)S(1)} %all-to-all-done.1.own_ref), channel_id=1, source_target_pairs={{0,16},{16,32},{32,48},{48,64},{64,80},{80,96},{96,112},{112,128},... | collective-permute-start | bytes 393224 | tf_op jit(solution)/shard_map/ppermute | solution.py:252
  32.1 0.7 copy-done.2
  32.9 0.1 reduce
  33.0 1.9 %collective-permute-start.2 = (bf16[8,64,128]{2,1,0:T(8,128)(2,1)S(1)}, bf16[8,64,128]{2,1,0:T(8,128)(2,1)S(1)}, u32[]{:S(2)}, u32[]{:S(2)}) collective-permute-start(bf16[8,64,128]{2,1,0:T(8,128)(2,1)S(1)} %all-to-all-done.1.own_ref), channel_id=1, source_target_pairs={{0,1},{1,0},{2,3},{3,2},{4,5},{5,4},{6,7},{7,6},{8,9},{9,8},{10,11... | collective-permute-start | bytes 393224 | tf_op jit(solution)/shard_map/ppermute | solution.py:256
  34.9 0.1 select_reduce_fusion
  35.1 0.9 collective-permute-done.1
  36.0 2.7 %collective-permute-done = bf16[8,64,128]{2,1,0:T(8,128)(2,1)S(1)} collective-permute-done((bf16[8,64,128]{2,1,0:T(8,128)(2,1)S(1)}, bf16[8,64,128]{2,1,0:T(8,128)(2,1)S(1)}, u32[]{:S(2)}, u32[]{:S(2)}) %collective-permute-start) | collective-permute-done | bytes 131104 | tf_op jit(solution)/shard_map/ppermute | solution.py:252
  38.7 1.9 %collective-permute-start.3 = (bf16[2,8,64,128]{3,2,1,0:T(8,128)(2,1)S(1)}, bf16[2,8,64,128]{3,2,1,0:T(8,128)(2,1)S(1)}, u32[]{:S(2)}, u32[]{:S(2)}) collective-permute-start(bf16[2,8,64,128]{3,2,1,0:T(8,128)(2,1)S(1)} %pad_maximum_fusion.old_ref), channel_id=1, source_target_pairs={{0,1},{1,0},{2,3},{3,2},{4,5},{5,4},{6,7},{7,6},{8,9},{9,8},{10,11... | collective-permute-start | bytes 786440 | tf_op jit(solution)/shard_map/ppermute | solution.py:256
  40.7 0.5 slice.4
  41.9 0.2 collective-permute-done.3.other_old_ref
  42.2 7.0 %all-to-all-done.qg_ref = bf16[8,512,128]{2,1,0:T(8,128)(2,1)S(1)} async-done(((bf16[8,512,128]{2,1,0:T(8,128)(2,1)}), bf16[8,512,128]{2,1,0:T(8,128)(2,1)S(1)}, u32[]{:S(2)}, u32[]{:S(2)}) %all-to-all-start) | async-done | bytes 1048608 | tf_op jit(solution)/shard_map/all_to_all | solution.py:247
  49.2 8.5 %attend.1 = (bf16[8,512,128]{2,1,0:T(8,128)(2,1)}, f32[3,8,64,128]{3,2,1,0:T(8,128)S(1)}, bf16[3,8,64,128]{3,2,1,0:T(8,128)(2,1)S(1)}) custom-call(s32[2]{0:T(128)S(1)} %pad_add_fusion.where_ref, bf16[8,512,128]{2,1,0:T(8,128)(2,1)S(1)} %all-to-all-done.qg_ref, s32[4,1,512]{2,1,0:T(1,128)S(1)} %max.18.start_ref, ...), custom_call_target="tpu_custom_call" | custom-call | flops 3623878656 | bytes 1048576 | tf_op jit(solution)/shard_map/attend/pallas_call | solution.py:286
  57.7 4.5 %all-to-all-start.2 = ((bf16[8,512,128]{2,1,0:T(8,128)(2,1)}), bf16[8,512,128]{2,1,0:T(8,128)(2,1)S(1)}, u32[]{:S(2)}, u32[]{:S(2)}) async-start(bf16[8,512,128]{2,1,0:T(8,128)(2,1)} %get-tuple-element.19), calls=%async_computation.2 | async-start | bytes 2097152 | tf_op jit(solution)/shard_map/all_to_all | solution.py:247
  62.2 1.9 %collective-permute-start.4 = (bf16[3,8,64,128]{3,2,1,0:T(8,128)(2,1)S(1)}, bf16[3,8,64,128]{3,2,1,0:T(8,128)(2,1)S(1)}, u32[]{:S(2)}, u32[]{:S(2)}) collective-permute-start(bf16[3,8,64,128]{3,2,1,0:T(8,128)(2,1)S(1)} %get-tuple-element.21), channel_id=1, source_target_pairs={{0,1},{1,0},{2,3},{3,2},{4,5},{5,4},{6,7},{7,6},{8,9},{9,8},{10,11... | collective-permute-start | bytes 1179656 | tf_op jit(solution)/shard_map/ppermute | solution.py:256
  64.1 1.7 %collective-permute-done.4.got_ref = bf16[3,8,64,128]{3,2,1,0:T(8,128)(2,1)S(1)} collective-permute-done((bf16[3,8,64,128]{3,2,1,0:T(8,128)(2,1)S(1)}, bf16[3,8,64,128]{3,2,1,0:T(8,128)(2,1)S(1)}, u32[]{:S(2)}, u32[]{:S(2)}) %collective-permute-start.4) | collective-permute-done | bytes 393248 | tf_op jit(solution)/shard_map/ppermute | solution.py:256
  65.8 5.6 %collective-permute-start.5 = (bf16[8,64,128]{2,1,0:T(8,128)(2,1)S(1)}, bf16[8,64,128]{2,1,0:T(8,128)(2,1)S(1)}, u32[]{:S(2)}, u32[]{:S(2)}) collective-permute-start(bf16[8,64,128]{2,1,0:T(8,128)(2,1)S(1)} %get-tuple-element.22), channel_id=1, source_target_pairs={{0,496},{16,0},{32,16},{48,32},{64,48},{80,64},{96,80},{112,96},{1... | collective-permute-start | bytes 393224 | tf_op jit(solution)/shard_map/ppermute | solution.py:252
  71.5 4.8 %collective-permute-start.6 = (bf16[8,64,128]{2,1,0:T(8,128)(2,1)S(1)}, bf16[8,64,128]{2,1,0:T(8,128)(2,1)S(1)}, u32[]{:S(2)}, u32[]{:S(2)}) collective-permute-start(bf16[8,64,128]{2,1,0:T(8,128)(2,1)S(1)} %get-tuple-element.23), channel_id=1, source_target_pairs={{0,480},{16,496},{32,0},{48,16},{64,32},{80,48},{96,64},{112,80},{... | collective-permute-start | bytes 393224 | tf_op jit(solution)/shard_map/ppermute | solution.py:252
  76.3 4.6 %collective-permute-done.6.two_ref = bf16[8,64,128]{2,1,0:T(8,128)(2,1)S(1)} collective-permute-done((bf16[8,64,128]{2,1,0:T(8,128)(2,1)S(1)}, bf16[8,64,128]{2,1,0:T(8,128)(2,1)S(1)}, u32[]{:S(2)}, u32[]{:S(2)}) %collective-permute-start.6) | collective-permute-done | bytes 131104 | tf_op jit(solution)/shard_map/ppermute | solution.py:252
  80.9 0.7 add_terms.1
  81.6 5.9 %all-to-all-done.2.x_ref = bf16[8,512,128]{2,1,0:T(8,128)(2,1)S(1)} async-done(((bf16[8,512,128]{2,1,0:T(8,128)(2,1)}), bf16[8,512,128]{2,1,0:T(8,128)(2,1)S(1)}, u32[]{:S(2)}, u32[]{:S(2)}) %all-to-all-start.2) | async-done | bytes 1048608 | tf_op jit(solution)/shard_map/all_to_all | solution.py:247
  87.5 4.5 %all-to-all-start.3 = ((bf16[8,64,128]{2,1,0:T(8,128)(2,1)}), bf16[8,64,128]{2,1,0:T(8,128)(2,1)S(1)}, u32[]{:S(2)}, u32[]{:S(2)}) async-start(bf16[8,64,128]{2,1,0:T(8,128)(2,1)} %add_terms.1), calls=%async_computation.3 | async-start | bytes 262144 | tf_op jit(solution)/shard_map/all_to_all | solution.py:247
  92.0 1.1 %unpack_od.1 = (bf16[32,64,128]{2,1,0:T(8,128)(2,1)}, bf16[32,64,128]{2,1,0:T(8,128)(2,1)}) custom-call(bf16[8,512,128]{2,1,0:T(8,128)(2,1)S(1)} %all-to-all-done.2.x_ref), custom_call_target="tpu_custom_call" | custom-call | bytes 1048576 | tf_op jit(solution)/shard_map/unpack_od/pallas_call | solution.py:308
  93.2 6.8 %all-to-all-done.3.x_ref = bf16[8,64,128]{2,1,0:T(8,128)(2,1)S(1)} async-done(((bf16[8,64,128]{2,1,0:T(8,128)(2,1)}), bf16[8,64,128]{2,1,0:T(8,128)(2,1)S(1)}, u32[]{:S(2)}, u32[]{:S(2)}) %all-to-all-start.3) | async-done | bytes 131104 | tf_op jit(solution)/shard_map/all_to_all | solution.py:247
  100.0 0.7 unpack_kv.1
  (16 shorter events, 0.4 us)
Async XLA Ops:
  0.6 12.0 %copy-start = (bf16[32,64,128]{2,1,0:T(8,128)(2,1)S(1)}, bf16[32,64,128]{2,1,0:T(8,128)(2,1)}, u32[]{:S(2)}) copy-start(bf16[32,64,128]{2,1,0:T(8,128)(2,1)} %q_ref.1) | copy-start | bytes 1572868
  2.3 18.2 %all-to-all-start.1 = ((bf16[8,64,128]{2,1,0:T(8,128)(2,1)}), bf16[8,64,128]{2,1,0:T(8,128)(2,1)S(1)}, u32[]{:S(2)}, u32[]{:S(2)}) async-start(bf16[8,64,128]{2,1,0:T(8,128)(2,1)} %bitcast.6), calls=%async_computation.1 | async-start | bytes 262144 | tf_op jit(solution)/shard_map/all_to_all | solution.py:247
  12.6 1.0 %copy-start.1 = (bf16[32,64,128]{2,1,0:T(8,128)(2,1)S(1)}, bf16[32,64,128]{2,1,0:T(8,128)(2,1)}, u32[]{:S(2)}) copy-start(bf16[32,64,128]{2,1,0:T(8,128)(2,1)} %g_ref.1) | copy-start | bytes 1572868
  20.4 28.7 %all-to-all-start = ((bf16[8,512,128]{2,1,0:T(8,128)(2,1)}), bf16[8,512,128]{2,1,0:T(8,128)(2,1)S(1)}, u32[]{:S(2)}, u32[]{:S(2)}) async-start(bf16[8,512,128]{2,1,0:T(8,128)(2,1)} %pack_qg.1), calls=%async_computation | async-start | bytes 2097152 | tf_op jit(solution)/shard_map/all_to_all | solution.py:247
  24.0 11.9 %collective-permute-start.1 = (bf16[8,64,128]{2,1,0:T(8,128)(2,1)S(1)}, bf16[8,64,128]{2,1,0:T(8,128)(2,1)S(1)}, u32[]{:S(2)}, u32[]{:S(2)}) collective-permute-start(bf16[8,64,128]{2,1,0:T(8,128)(2,1)S(1)} %all-to-all-done.1.own_ref), channel_id=1, source_target_pairs={{0,32},{16,48},{32,64},{48,80},{64,96},{80,112},{96,128},{112,144}... | collective-permute-start | bytes 393224 | tf_op jit(solution)/shard_map/ppermute | solution.py:252
  28.5 10.2 %collective-permute-start = (bf16[8,64,128]{2,1,0:T(8,128)(2,1)S(1)}, bf16[8,64,128]{2,1,0:T(8,128)(2,1)S(1)}, u32[]{:S(2)}, u32[]{:S(2)}) collective-permute-start(bf16[8,64,128]{2,1,0:T(8,128)(2,1)S(1)} %all-to-all-done.1.own_ref), channel_id=1, source_target_pairs={{0,16},{16,32},{32,48},{48,64},{64,80},{80,96},{96,112},{112,128},... | collective-permute-start | bytes 393224 | tf_op jit(solution)/shard_map/ppermute | solution.py:252
  32.1 0.7 copy-start.2
  33.0 5.7 %collective-permute-start.2 = (bf16[8,64,128]{2,1,0:T(8,128)(2,1)S(1)}, bf16[8,64,128]{2,1,0:T(8,128)(2,1)S(1)}, u32[]{:S(2)}, u32[]{:S(2)}) collective-permute-start(bf16[8,64,128]{2,1,0:T(8,128)(2,1)S(1)} %all-to-all-done.1.own_ref), channel_id=1, source_target_pairs={{0,1},{1,0},{2,3},{3,2},{4,5},{5,4},{6,7},{7,6},{8,9},{9,8},{10,11... | collective-permute-start | bytes 393224 | tf_op jit(solution)/shard_map/ppermute | solution.py:256
  38.7 3.4 %collective-permute-start.3 = (bf16[2,8,64,128]{3,2,1,0:T(8,128)(2,1)S(1)}, bf16[2,8,64,128]{3,2,1,0:T(8,128)(2,1)S(1)}, u32[]{:S(2)}, u32[]{:S(2)}) collective-permute-start(bf16[2,8,64,128]{3,2,1,0:T(8,128)(2,1)S(1)} %pad_maximum_fusion.old_ref), channel_id=1, source_target_pairs={{0,1},{1,0},{2,3},{3,2},{4,5},{5,4},{6,7},{7,6},{8,9},{9,8},{10,11... | collective-permute-start | bytes 786440 | tf_op jit(solution)/shard_map/ppermute | solution.py:256
  57.7 29.8 %all-to-all-start.2 = ((bf16[8,512,128]{2,1,0:T(8,128)(2,1)}), bf16[8,512,128]{2,1,0:T(8,128)(2,1)S(1)}, u32[]{:S(2)}, u32[]{:S(2)}) async-start(bf16[8,512,128]{2,1,0:T(8,128)(2,1)} %get-tuple-element.19), calls=%async_computation.2 | async-start | bytes 2097152 | tf_op jit(solution)/shard_map/all_to_all | solution.py:247
  62.2 3.6 %collective-permute-start.4 = (bf16[3,8,64,128]{3,2,1,0:T(8,128)(2,1)S(1)}, bf16[3,8,64,128]{3,2,1,0:T(8,128)(2,1)S(1)}, u32[]{:S(2)}, u32[]{:S(2)}) collective-permute-start(bf16[3,8,64,128]{3,2,1,0:T(8,128)(2,1)S(1)} %get-tuple-element.21), channel_id=1, source_target_pairs={{0,1},{1,0},{2,3},{3,2},{4,5},{5,4},{6,7},{7,6},{8,9},{9,8},{10,11... | collective-permute-start | bytes 1179656 | tf_op jit(solution)/shard_map/ppermute | solution.py:256
  65.8 10.5 %collective-permute-start.5 = (bf16[8,64,128]{2,1,0:T(8,128)(2,1)S(1)}, bf16[8,64,128]{2,1,0:T(8,128)(2,1)S(1)}, u32[]{:S(2)}, u32[]{:S(2)}) collective-permute-start(bf16[8,64,128]{2,1,0:T(8,128)(2,1)S(1)} %get-tuple-element.22), channel_id=1, source_target_pairs={{0,496},{16,0},{32,16},{48,32},{64,48},{80,64},{96,80},{112,96},{1... | collective-permute-start | bytes 393224 | tf_op jit(solution)/shard_map/ppermute | solution.py:252
  71.5 9.4 %collective-permute-start.6 = (bf16[8,64,128]{2,1,0:T(8,128)(2,1)S(1)}, bf16[8,64,128]{2,1,0:T(8,128)(2,1)S(1)}, u32[]{:S(2)}, u32[]{:S(2)}) collective-permute-start(bf16[8,64,128]{2,1,0:T(8,128)(2,1)S(1)} %get-tuple-element.23), channel_id=1, source_target_pairs={{0,480},{16,496},{32,0},{48,16},{64,32},{80,48},{96,64},{112,80},{... | collective-permute-start | bytes 393224 | tf_op jit(solution)/shard_map/ppermute | solution.py:252
  87.5 12.5 %all-to-all-start.3 = ((bf16[8,64,128]{2,1,0:T(8,128)(2,1)}), bf16[8,64,128]{2,1,0:T(8,128)(2,1)S(1)}, u32[]{:S(2)}, u32[]{:S(2)}) async-start(bf16[8,64,128]{2,1,0:T(8,128)(2,1)} %add_terms.1), calls=%async_computation.3 | async-start | bytes 262144 | tf_op jit(solution)/shard_map/all_to_all | solution.py:247

commit v6 on v5

--- a/solution.py
+++ b/solution.py
@@ -215,13 +215,13 @@
         for copy in sent:
             copy.wait()
 
+    @pl.when(where_ref[1] != 0)
+    def far():
+        pipeline([WIN] * (BLOCKS - 1) + [BLOCKS])
+
     @pl.when(where_ref[1] == 0)
     def near():
         pipeline([NEAR + 1 + at for at in range(BLOCKS)])
-
-    @pl.when(where_ref[1] != 0)
-    def far():
-        pipeline([WIN] * (BLOCKS - 1) + [BLOCKS])
 
     for column in range(REACH + 1):
         for piece in range(KVH):
@@ -272,7 +272,7 @@
     heads_wide = shape(TOK, KVH * GROUP, HD)
     wide = [pltpu.VMEM((TOK * KVH, HD), F32)]
 
-    packed = jnp.transpose(jnp.stack([key_in, value_in]), (2, 0, 1, 3)).reshape(KVH, 2 * TOK, HD)
+    packed = jnp.transpose(jnp.concatenate([key_in, value_in], axis=0), (1, 0, 2))
     kv = exchange(packed)
     qg = exchange(call(pack_qg, [both_wide], [VMEM] * 2, [], "pack_qg")(query_in, grad_out)[0])
     other = swapped(kv)

time: 102 us -> 102 us (level)
    unnamed x6 -> x10, local copies, waits for them, and re-layouts: 1.7 us -> 2.62 us
where the time goes in v6:
time: 102 us; the launch traced here: 101 us
  starting transfers between devices  46.3 us (45%)
  waiting for transfers between devices  36.3 us (36%)
  Pallas kernels  12.4 us (12%)
  local copies, waits for them, and re-layouts  3.23 us (3%)
  between operations  1.48 us (1%)
  other arithmetic  1.17 us (1%)
    all_to_all x4, waiting for transfers between devices, exchange(): return lax.all_to_all(x, RING, split_axis=0, concat_axis=0, tiled=True)  25.4 us
    all_to_all x4, starting transfers between devices, exchange(): return lax.all_to_all(x, RING, split_axis=0, concat_axis=0, tiled=True)  22.9 us
    ppermute x4, starting transfers between devices, shifted(): lax.ppermute(x, COLUMNS, [(i, (i + by) % count) for i in range(count)])  17.7 us
    ppermute x4, waiting for transfers between devices, shifted(): lax.ppermute(x, COLUMNS, [(i, (i + by) % count) for i in range(count)])  8.98 us
    pallas_call x1, Pallas kernels, shards(): call(attend, [both_wide, shape(REACH + 1, KVH, 2 * TOK, HD, dtype=F32), s...  8.68 us
    ppermute x3, starting transfers between devices, swapped(): return lax.ppermute(x, 'c', [(0, 1), (1, 0)])  5.74 us
    unnamed x10, local copies, waits for them, and re-layouts  2.62 us
  transfers between devices with their start and end apart: 11, of which 9 were waited for; matrix products, arithmetic and copies ran while one was open for 1% of the time, Pallas kernels for 3%

profile of v6, /device:TPU:6, one launch (start us, length us, event | category | flops | bytes accessed | tf_op | source)
XLA Modules:
  0.0 100.9 jit_solution(11708542985641030050)
XLA Ops:
  0.7 0.9 copy.16
  1.6 0.7 maximum_bitcast_fusion
  2.3 10.3 %all-to-all-start.1 = ((bf16[8,64,128]{2,1,0:T(8,128)(2,1)}), bf16[8,64,128]{2,1,0:T(8,128)(2,1)S(1)}, u32[]{:S(2)}, u32[]{:S(2)}) async-start(bf16[8,64,128]{2,1,0:T(8,128)(2,1)} %maximum_bitcast_fusion), calls=%async_computation.1 | async-start | bytes 262144 | tf_op jit(solution)/shard_map/all_to_all | solution.py:247
  12.6 1.0 %copy-done.1 = bf16[32,64,128]{2,1,0:T(8,128)(2,1)S(1)} copy-done((bf16[32,64,128]{2,1,0:T(8,128)(2,1)S(1)}, bf16[32,64,128]{2,1,0:T(8,128)(2,1)}, u32[]{:S(2)}) %copy-start.1) | copy-done | bytes 524312
  13.6 1.2 %pack_qg.1 = bf16[8,512,128]{2,1,0:T(8,128)(2,1)} custom-call(bf16[32,64,128]{2,1,0:T(8,128)(2,1)S(1)} %copy-done, bf16[32,64,128]{2,1,0:T(8,128)(2,1)S(1)} %copy-done.1), custom_call_target="tpu_custom_call" | custom-call | bytes 1048576 | tf_op jit(solution)/shard_map/pack_qg/pallas_call | solution.py:277
  14.8 5.6 %all-to-all-done.1.own_ref = bf16[8,64,128]{2,1,0:T(8,128)(2,1)S(1)} async-done(((bf16[8,64,128]{2,1,0:T(8,128)(2,1)}), bf16[8,64,128]{2,1,0:T(8,128)(2,1)S(1)}, u32[]{:S(2)}, u32[]{:S(2)}) %all-to-all-start.1) | async-done | bytes 131104 | tf_op jit(solution)/shard_map/all_to_all | solution.py:247
  20.4 3.6 %all-to-all-start = ((bf16[8,512,128]{2,1,0:T(8,128)(2,1)}), bf16[8,512,128]{2,1,0:T(8,128)(2,1)S(1)}, u32[]{:S(2)}, u32[]{:S(2)}) async-start(bf16[8,512,128]{2,1,0:T(8,128)(2,1)} %pack_qg.1), calls=%async_computation | async-start | bytes 2097152 | tf_op jit(solution)/shard_map/all_to_all | solution.py:247
  24.0 4.5 %collective-permute-start.1 = (bf16[8,64,128]{2,1,0:T(8,128)(2,1)S(1)}, bf16[8,64,128]{2,1,0:T(8,128)(2,1)S(1)}, u32[]{:S(2)}, u32[]{:S(2)}) collective-permute-start(bf16[8,64,128]{2,1,0:T(8,128)(2,1)S(1)} %all-to-all-done.1.own_ref), channel_id=1, source_target_pairs={{0,32},{16,48},{32,64},{48,80},{64,96},{80,112},{96,128},{112,144}... | collective-permute-start | bytes 393224 | tf_op jit(solution)/shard_map/ppermute | solution.py:252
  28.5 3.5 %collective-permute-start = (bf16[8,64,128]{2,1,0:T(8,128)(2,1)S(1)}, bf16[8,64,128]{2,1,0:T(8,128)(2,1)S(1)}, u32[]{:S(2)}, u32[]{:S(2)}) collective-permute-start(bf16[8,64,128]{2,1,0:T(8,128)(2,1)S(1)} %all-to-all-done.1.own_ref), channel_id=1, source_target_pairs={{0,16},{16,32},{32,48},{48,64},{64,80},{80,96},{96,112},{112,128},... | collective-permute-start | bytes 393224 | tf_op jit(solution)/shard_map/ppermute | solution.py:252
  32.1 0.7 copy-done.3
  32.9 0.1 reduce
  33.0 1.9 %collective-permute-start.2 = (bf16[8,64,128]{2,1,0:T(8,128)(2,1)S(1)}, bf16[8,64,128]{2,1,0:T(8,128)(2,1)S(1)}, u32[]{:S(2)}, u32[]{:S(2)}) collective-permute-start(bf16[8,64,128]{2,1,0:T(8,128)(2,1)S(1)} %all-to-all-done.1.own_ref), channel_id=1, source_target_pairs={{0,1},{1,0},{2,3},{3,2},{4,5},{5,4},{6,7},{7,6},{8,9},{9,8},{10,11... | collective-permute-start | bytes 393224 | tf_op jit(solution)/shard_map/ppermute | solution.py:256
  34.9 0.1 select_reduce_fusion
  35.1 0.9 collective-permute-done.1
  36.0 2.7 %collective-permute-done = bf16[8,64,128]{2,1,0:T(8,128)(2,1)S(1)} collective-permute-done((bf16[8,64,128]{2,1,0:T(8,128)(2,1)S(1)}, bf16[8,64,128]{2,1,0:T(8,128)(2,1)S(1)}, u32[]{:S(2)}, u32[]{:S(2)}) %collective-permute-start) | collective-permute-done | bytes 131104 | tf_op jit(solution)/shard_map/ppermute | solution.py:252
  38.7 1.9 %collective-permute-start.3 = (bf16[2,8,64,128]{3,2,1,0:T(8,128)(2,1)S(1)}, bf16[2,8,64,128]{3,2,1,0:T(8,128)(2,1)S(1)}, u32[]{:S(2)}, u32[]{:S(2)}) collective-permute-start(bf16[2,8,64,128]{3,2,1,0:T(8,128)(2,1)S(1)} %pad_maximum_fusion.old_ref), channel_id=1, source_target_pairs={{0,1},{1,0},{2,3},{3,2},{4,5},{5,4},{6,7},{7,6},{8,9},{9,8},{10,11... | collective-permute-start | bytes 786440 | tf_op jit(solution)/shard_map/ppermute | solution.py:256
  40.7 0.5 slice.4
  41.9 0.2 collective-permute-done.3.other_old_ref
  42.2 7.0 %all-to-all-done.qg_ref = bf16[8,512,128]{2,1,0:T(8,128)(2,1)S(1)} async-done(((bf16[8,512,128]{2,1,0:T(8,128)(2,1)}), bf16[8,512,128]{2,1,0:T(8,128)(2,1)S(1)}, u32[]{:S(2)}, u32[]{:S(2)}) %all-to-all-start) | async-done | bytes 1048608 | tf_op jit(solution)/shard_map/all_to_all | solution.py:247
  49.1 8.7 %attend.1 = (bf16[8,512,128]{2,1,0:T(8,128)(2,1)}, f32[3,8,64,128]{3,2,1,0:T(8,128)S(1)}, bf16[3,8,64,128]{3,2,1,0:T(8,128)(2,1)S(1)}) custom-call(s32[2]{0:T(128)S(1)} %pad_add_fusion.where_ref, bf16[8,512,128]{2,1,0:T(8,128)(2,1)S(1)} %all-to-all-done.qg_ref, s32[4,1,512]{2,1,0:T(1,128)S(1)} %max.18.start_ref, ...), custom_call_target="tpu_custom_call" | custom-call | flops 3623878656 | bytes 1048576 | tf_op jit(solution)/shard_map/attend/pallas_call | solution.py:286
  57.8 4.5 %all-to-all-start.2 = ((bf16[8,512,128]{2,1,0:T(8,128)(2,1)}), bf16[8,512,128]{2,1,0:T(8,128)(2,1)S(1)}, u32[]{:S(2)}, u32[]{:S(2)}) async-start(bf16[8,512,128]{2,1,0:T(8,128)(2,1)} %get-tuple-element.19), calls=%async_computation.2 | async-start | bytes 2097152 | tf_op jit(solution)/shard_map/all_to_all | solution.py:247
  62.4 1.9 %collective-permute-start.4 = (bf16[3,8,64,128]{3,2,1,0:T(8,128)(2,1)S(1)}, bf16[3,8,64,128]{3,2,1,0:T(8,128)(2,1)S(1)}, u32[]{:S(2)}, u32[]{:S(2)}) collective-permute-start(bf16[3,8,64,128]{3,2,1,0:T(8,128)(2,1)S(1)} %get-tuple-element.21), channel_id=1, source_target_pairs={{0,1},{1,0},{2,3},{3,2},{4,5},{5,4},{6,7},{7,6},{8,9},{9,8},{10,11... | collective-permute-start | bytes 1179656 | tf_op jit(solution)/shard_map/ppermute | solution.py:256
  64.3 1.7 %collective-permute-done.4.got_ref = bf16[3,8,64,128]{3,2,1,0:T(8,128)(2,1)S(1)} collective-permute-done((bf16[3,8,64,128]{3,2,1,0:T(8,128)(2,1)S(1)}, bf16[3,8,64,128]{3,2,1,0:T(8,128)(2,1)S(1)}, u32[]{:S(2)}, u32[]{:S(2)}) %collective-permute-start.4) | collective-permute-done | bytes 393248 | tf_op jit(solution)/shard_map/ppermute | solution.py:256
  66.0 5.6 %collective-permute-start.5 = (bf16[8,64,128]{2,1,0:T(8,128)(2,1)S(1)}, bf16[8,64,128]{2,1,0:T(8,128)(2,1)S(1)}, u32[]{:S(2)}, u32[]{:S(2)}) collective-permute-start(bf16[8,64,128]{2,1,0:T(8,128)(2,1)S(1)} %get-tuple-element.22), channel_id=1, source_target_pairs={{0,496},{16,0},{32,16},{48,32},{64,48},{80,64},{96,80},{112,96},{1... | collective-permute-start | bytes 393224 | tf_op jit(solution)/shard_map/ppermute | solution.py:252
  71.7 4.0 %collective-permute-start.6 = (bf16[8,64,128]{2,1,0:T(8,128)(2,1)S(1)}, bf16[8,64,128]{2,1,0:T(8,128)(2,1)S(1)}, u32[]{:S(2)}, u32[]{:S(2)}) collective-permute-start(bf16[8,64,128]{2,1,0:T(8,128)(2,1)S(1)} %get-tuple-element.23), channel_id=1, source_target_pairs={{0,480},{16,496},{32,0},{48,16},{64,32},{80,48},{96,64},{112,80},{... | collective-permute-start | bytes 393224 | tf_op jit(solution)/shard_map/ppermute | solution.py:252
  75.7 5.4 %collective-permute-done.6.two_ref = bf16[8,64,128]{2,1,0:T(8,128)(2,1)S(1)} collective-permute-done((bf16[8,64,128]{2,1,0:T(8,128)(2,1)S(1)}, bf16[8,64,128]{2,1,0:T(8,128)(2,1)S(1)}, u32[]{:S(2)}, u32[]{:S(2)}) %collective-permute-start.6) | collective-permute-done | bytes 131104 | tf_op jit(solution)/shard_map/ppermute | solution.py:252
  81.1 0.7 add_terms.1
  81.8 5.9 %all-to-all-done.2.x_ref = bf16[8,512,128]{2,1,0:T(8,128)(2,1)S(1)} async-done(((bf16[8,512,128]{2,1,0:T(8,128)(2,1)}), bf16[8,512,128]{2,1,0:T(8,128)(2,1)S(1)}, u32[]{:S(2)}, u32[]{:S(2)}) %all-to-all-start.2) | async-done | bytes 1048608 | tf_op jit(solution)/shard_map/all_to_all | solution.py:247
  87.7 4.5 %all-to-all-start.3 = ((bf16[8,64,128]{2,1,0:T(8,128)(2,1)}), bf16[8,64,128]{2,1,0:T(8,128)(2,1)S(1)}, u32[]{:S(2)}, u32[]{:S(2)}) async-start(bf16[8,64,128]{2,1,0:T(8,128)(2,1)} %add_terms.1), calls=%async_computation.3 | async-start | bytes 262144 | tf_op jit(solution)/shard_map/all_to_all | solution.py:247
  92.2 1.1 %unpack_od.1 = (bf16[32,64,128]{2,1,0:T(8,128)(2,1)}, bf16[32,64,128]{2,1,0:T(8,128)(2,1)}) custom-call(bf16[8,512,128]{2,1,0:T(8,128)(2,1)S(1)} %all-to-all-done.2.x_ref), custom_call_target="tpu_custom_call" | custom-call | bytes 1048576 | tf_op jit(solution)/shard_map/unpack_od/pallas_call | solution.py:308
  93.3 6.9 %all-to-all-done.3.x_ref = bf16[8,64,128]{2,1,0:T(8,128)(2,1)S(1)} async-done(((bf16[8,64,128]{2,1,0:T(8,128)(2,1)}), bf16[8,64,128]{2,1,0:T(8,128)(2,1)S(1)}, u32[]{:S(2)}, u32[]{:S(2)}) %all-to-all-start.3) | async-done | bytes 131104 | tf_op jit(solution)/shard_map/all_to_all | solution.py:247
  100.2 0.7 unpack_kv.1
  (19 shorter events, 0.4 us)
Async XLA Ops:
  0.6 0.9 copy-start.2
  0.6 11.9 %copy-start = (bf16[32,64,128]{2,1,0:T(8,128)(2,1)S(1)}, bf16[32,64,128]{2,1,0:T(8,128)(2,1)}, u32[]{:S(2)}) copy-start(bf16[32,64,128]{2,1,0:T(8,128)(2,1)} %q_ref.1) | copy-start | bytes 1572868
  2.3 18.2 %all-to-all-start.1 = ((bf16[8,64,128]{2,1,0:T(8,128)(2,1)}), bf16[8,64,128]{2,1,0:T(8,128)(2,1)S(1)}, u32[]{:S(2)}, u32[]{:S(2)}) async-start(bf16[8,64,128]{2,1,0:T(8,128)(2,1)} %maximum_bitcast_fusion), calls=%async_computation.1 | async-start | bytes 262144 | tf_op jit(solution)/shard_map/all_to_all | solution.py:247
  12.6 1.0 %copy-start.1 = (bf16[32,64,128]{2,1,0:T(8,128)(2,1)S(1)}, bf16[32,64,128]{2,1,0:T(8,128)(2,1)}, u32[]{:S(2)}) copy-start(bf16[32,64,128]{2,1,0:T(8,128)(2,1)} %g_ref.1) | copy-start | bytes 1572868
  20.4 28.7 %all-to-all-start = ((bf16[8,512,128]{2,1,0:T(8,128)(2,1)}), bf16[8,512,128]{2,1,0:T(8,128)(2,1)S(1)}, u32[]{:S(2)}, u32[]{:S(2)}) async-start(bf16[8,512,128]{2,1,0:T(8,128)(2,1)} %pack_qg.1), calls=%async_computation | async-start | bytes 2097152 | tf_op jit(solution)/shard_map/all_to_all | solution.py:247
  24.0 11.9 %collective-permute-start.1 = (bf16[8,64,128]{2,1,0:T(8,128)(2,1)S(1)}, bf16[8,64,128]{2,1,0:T(8,128)(2,1)S(1)}, u32[]{:S(2)}, u32[]{:S(2)}) collective-permute-start(bf16[8,64,128]{2,1,0:T(8,128)(2,1)S(1)} %all-to-all-done.1.own_ref), channel_id=1, source_target_pairs={{0,32},{16,48},{32,64},{48,80},{64,96},{80,112},{96,128},{112,144}... | collective-permute-start | bytes 393224 | tf_op jit(solution)/shard_map/ppermute | solution.py:252
  28.5 10.2 %collective-permute-start = (bf16[8,64,128]{2,1,0:T(8,128)(2,1)S(1)}, bf16[8,64,128]{2,1,0:T(8,128)(2,1)S(1)}, u32[]{:S(2)}, u32[]{:S(2)}) collective-permute-start(bf16[8,64,128]{2,1,0:T(8,128)(2,1)S(1)} %all-to-all-done.1.own_ref), channel_id=1, source_target_pairs={{0,16},{16,32},{32,48},{48,64},{64,80},{80,96},{96,112},{112,128},... | collective-permute-start | bytes 393224 | tf_op jit(solution)/shard_map/ppermute | solution.py:252
  32.1 0.7 copy-start.3
  33.0 5.7 %collective-permute-start.2 = (bf16[8,64,128]{2,1,0:T(8,128)(2,1)S(1)}, bf16[8,64,128]{2,1,0:T(8,128)(2,1)S(1)}, u32[]{:S(2)}, u32[]{:S(2)}) collective-permute-start(bf16[8,64,128]{2,1,0:T(8,128)(2,1)S(1)} %all-to-all-done.1.own_ref), channel_id=1, source_target_pairs={{0,1},{1,0},{2,3},{3,2},{4,5},{5,4},{6,7},{7,6},{8,9},{9,8},{10,11... | collective-permute-start | bytes 393224 | tf_op jit(solution)/shard_map/ppermute | solution.py:256
  38.7 3.4 %collective-permute-start.3 = (bf16[2,8,64,128]{3,2,1,0:T(8,128)(2,1)S(1)}, bf16[2,8,64,128]{3,2,1,0:T(8,128)(2,1)S(1)}, u32[]{:S(2)}, u32[]{:S(2)}) collective-permute-start(bf16[2,8,64,128]{3,2,1,0:T(8,128)(2,1)S(1)} %pad_maximum_fusion.old_ref), channel_id=1, source_target_pairs={{0,1},{1,0},{2,3},{3,2},{4,5},{5,4},{6,7},{7,6},{8,9},{9,8},{10,11... | collective-permute-start | bytes 786440 | tf_op jit(solution)/shard_map/ppermute | solution.py:256
  57.8 29.8 %all-to-all-start.2 = ((bf16[8,512,128]{2,1,0:T(8,128)(2,1)}), bf16[8,512,128]{2,1,0:T(8,128)(2,1)S(1)}, u32[]{:S(2)}, u32[]{:S(2)}) async-start(bf16[8,512,128]{2,1,0:T(8,128)(2,1)} %get-tuple-element.19), calls=%async_computation.2 | async-start | bytes 2097152 | tf_op jit(solution)/shard_map/all_to_all | solution.py:247
  62.4 3.6 %collective-permute-start.4 = (bf16[3,8,64,128]{3,2,1,0:T(8,128)(2,1)S(1)}, bf16[3,8,64,128]{3,2,1,0:T(8,128)(2,1)S(1)}, u32[]{:S(2)}, u32[]{:S(2)}) collective-permute-start(bf16[3,8,64,128]{3,2,1,0:T(8,128)(2,1)S(1)} %get-tuple-element.21), channel_id=1, source_target_pairs={{0,1},{1,0},{2,3},{3,2},{4,5},{5,4},{6,7},{7,6},{8,9},{9,8},{10,11... | collective-permute-start | bytes 1179656 | tf_op jit(solution)/shard_map/ppermute | solution.py:256
  66.0 9.7 %collective-permute-start.5 = (bf16[8,64,128]{2,1,0:T(8,128)(2,1)S(1)}, bf16[8,64,128]{2,1,0:T(8,128)(2,1)S(1)}, u32[]{:S(2)}, u32[]{:S(2)}) collective-permute-start(bf16[8,64,128]{2,1,0:T(8,128)(2,1)S(1)} %get-tuple-element.22), channel_id=1, source_target_pairs={{0,496},{16,0},{32,16},{48,32},{64,48},{80,64},{96,80},{112,96},{1... | collective-permute-start | bytes 393224 | tf_op jit(solution)/shard_map/ppermute | solution.py:252
  71.7 9.4 %collective-permute-start.6 = (bf16[8,64,128]{2,1,0:T(8,128)(2,1)S(1)}, bf16[8,64,128]{2,1,0:T(8,128)(2,1)S(1)}, u32[]{:S(2)}, u32[]{:S(2)}) collective-permute-start(bf16[8,64,128]{2,1,0:T(8,128)(2,1)S(1)} %get-tuple-element.23), channel_id=1, source_target_pairs={{0,480},{16,496},{32,0},{48,16},{64,32},{80,48},{96,64},{112,80},{... | collective-permute-start | bytes 393224 | tf_op jit(solution)/shard_map/ppermute | solution.py:252
  87.7 12.6 %all-to-all-start.3 = ((bf16[8,64,128]{2,1,0:T(8,128)(2,1)}), bf16[8,64,128]{2,1,0:T(8,128)(2,1)S(1)}, u32[]{:S(2)}, u32[]{:S(2)}) async-start(bf16[8,64,128]{2,1,0:T(8,128)(2,1)} %add_terms.1), calls=%async_computation.3 | async-start | bytes 262144 | tf_op jit(solution)/shard_map/all_to_all | solution.py:247
